TPU v7x, 512 devices: a whole 4x8x8 slice. The times are simulated.
512 devices in a mesh: gz: 32 (over x, y), xy: 16 (over z, core).
Axes of the slice: x: 4, y: 8, z: 8, core: 2. Of those that a mesh axis runs over, the one named last changes fastest.
Arguments:
- load_field: float32 [256, 256, 512], P('gz', 'xy'), may hold values from -8 to 8
- density: float32 [256, 256, 512], P('gz', 'xy'), may hold values from 0.2 to 1
- void_mask: int32 [32, 32, 64], P('gz', 'xy'), may hold values 0 or 1
Outputs:
- adjoint: float32 [256, 256, 512], P('gz', 'xy')
- residual: float32 [256, 256, 512], P('gz', 'xy')
Inputs may be any that keep to these rules, and one draw needn't show every extreme that they name: `void_mask`: 1 marks a void brick.
All inputs are finite; a program needn't handle non-finite values. No bound on the sum of `void_mask` on one device may be relied on, other than what follows from the above.
Results may differ from a plain program's by a relative error of at most 0.0003.
Values sent between devices are 32-bit elements; how exact they have to be, the bound alone decides.
No kernel may reach another device: no remote copies, remote signals or barrier semaphores. Data moves between devices by JAX's collectives and lax.ppermute only.
A program may use at most 128 MiB of HBM per device.

v0:
```python
import jax
import jax.numpy as jnp
from jax import lax
from jax.sharding import PartitionSpec as P

DEGREE = 4


THETA = 1.15
DELTA = 0.85


def with_halo(cells, sides, width):
    for axis, dim in sides:
        count = lax.axis_size(axis)
        ends = count - 1
        head = lax.slice_in_dim(cells, 0, width, axis=dim)
        tail = lax.slice_in_dim(cells, cells.shape[dim] - width, cells.shape[dim], axis=dim)
        cells = jnp.concatenate(
            [
                lax.ppermute(tail, axis, [(i, (i + 1) % count) for i in range(ends)]),
                cells,
                lax.ppermute(head, axis, [((i + 1) % count, i) for i in range(ends)]),
            ],
            axis=dim,
        )
    return cells


def neighbours(padded):
    total = padded[2:, 1:-1, 1:-1] + padded[:-2, 1:-1, 1:-1]
    total = total + padded[1:-1, 2:, 1:-1] + padded[1:-1, :-2, 1:-1]
    return total + padded[1:-1, 1:-1, 2:] + padded[1:-1, 1:-1, :-2]


def operate(field, root, padder):
    weighted = root * field
    return root * (6.0 * weighted - neighbours(padder(weighted)))


def chebyshev(solution, remain, root, padder):
    inverse = 1.0 / (6.0 * root * root)
    sigma = THETA / DELTA
    rho = 1.0 / sigma
    step = inverse * remain / THETA
    for turn in range(DEGREE):
        solution = solution + step
        remain = remain - operate(step, root, padder)
        if turn + 1 < DEGREE:
            rho_next = 1.0 / (2.0 * sigma - rho)
            step = rho_next * rho * step + 2.0 * rho_next / DELTA * inverse * remain
            rho = rho_next
    return (solution, remain)


def blocks(field):
    a, b, c = field.shape
    return field.reshape(a // 2, 2, b // 2, 2, c // 2, 2).sum(axis=(1, 3, 5))


def prolong(field):
    return jnp.repeat(jnp.repeat(jnp.repeat(field, 2, 0), 2, 1), 2, 2)


def pad_last(field):
    return jnp.pad(field, ((0, 0), (0, 0), (1, 1)))


def fine_pad(field):
    return pad_last(with_halo(field, (("gz", 0), ("xy", 1)), 1))


def middle_pad(field):
    return pad_last(with_halo(field, (("gz", 0), ("xy", 1)), 1))


def coarse_pad(field):
    return pad_last(with_halo(field, (("gz", 0), ("xy", 1)), 1))


def coarsest(right, root):
    solution, unused = chebyshev(jnp.zeros_like(right), right, root, coarse_pad)
    return solution


def level(right, root, padder, inner):
    solution, remain = chebyshev(jnp.zeros_like(right), right, root, padder)
    coarse = inner(0.5 * blocks(remain), 0.125 * blocks(root))
    fine = prolong(coarse)
    solution = solution + fine
    remain = remain - operate(fine, root, padder)
    return chebyshev(solution, remain, root, padder)


def middle(right, root):
    solution, unused = level(right, root, middle_pad, coarsest)
    return solution


def on_device(load_field, density, void_mask):
    voids = jnp.repeat(jnp.repeat(jnp.repeat(void_mask, 8, 0), 8, 1), 8, 2)
    stiff = jnp.where(voids == 1, 0.01, 0.01 + 0.99 * density * density * density)
    return level(load_field, jnp.sqrt(stiff), fine_pad, middle)


def solution(mesh):
    in_specs = (P("gz", "xy", None), P("gz", "xy", None), P("gz", "xy", None))
    out_specs = (P("gz", "xy", None), P("gz", "xy", None))
    return jax.shard_map(
        on_device, mesh=mesh, in_specs=in_specs, out_specs=out_specs, check_vma=False
    )
```

profile of v0, /device:TPU:251, one launch (start us, length us, event | category | flops | bytes accessed | tf_op | source)
XLA Modules:
  0.0 435.3 jit_solution(7834578047454549462)
XLA Ops:
  8.2 3.8 collective-permute-done
  12.0 7.2 %collective-permute-start.3 = (f32[10,1,512]{2,1,0:T(1,128)S(1)}, f32[10,1,512]{2,1,0:T(1,128)S(1)}, u32[]{:S(2)}, u32[]{:S(2)}) collective-permute-start(f32[10,1,512]{2,1,0:T(1,128)S(1)} %get-tuple-element.56), channel_id=1, source_target_pairs={{0,1},{1,2},{2,3},{3,4},{4,5},{5,6},{6,7},{7,8},{8,9},{9,10},{10,1... | collective-permute-start | bytes 61448 | tf_op jit(solution)/shard_map/ppermute | solution.py:21
  21.1 4.4 %collective-permute-done.2 = f32[10,1,512]{2,1,0:T(1,128)S(1)} collective-permute-done((f32[10,1,512]{2,1,0:T(1,128)S(1)}, f32[10,1,512]{2,1,0:T(1,128)S(1)}, u32[]{:S(2)}, u32[]{:S(2)}) %collective-permute-start.2) | collective-permute-done | bytes 20512 | tf_op jit(solution)/shard_map/ppermute | solution.py:23
  31.5 3.4 collective-permute-done.4
  40.0 4.4 %collective-permute-done.6 = f32[10,1,512]{2,1,0:T(1,128)S(1)} collective-permute-done((f32[10,1,512]{2,1,0:T(1,128)S(1)}, f32[10,1,512]{2,1,0:T(1,128)S(1)}, u32[]{:S(2)}, u32[]{:S(2)}) %collective-permute-start.6) | collective-permute-done | bytes 20512 | tf_op jit(solution)/shard_map/ppermute | solution.py:23
  50.3 3.4 collective-permute-done.8
  58.8 4.4 %collective-permute-done.10 = f32[10,1,512]{2,1,0:T(1,128)S(1)} collective-permute-done((f32[10,1,512]{2,1,0:T(1,128)S(1)}, f32[10,1,512]{2,1,0:T(1,128)S(1)}, u32[]{:S(2)}, u32[]{:S(2)}) %collective-permute-start.10) | collective-permute-done | bytes 20512 | tf_op jit(solution)/shard_map/ppermute | solution.py:23
  69.2 3.5 collective-permute-done.12
  78.0 18.1 %reshape.47 = f32[4,2,8,2,256,2]{5,4,3,2,1,0:T(8,128)} reshape(f32[8,16,512]{2,1,0:T(8,128)S(1)} %get-tuple-element.39) | data formatting | bytes 524288 | tf_op jit(solution)/shard_map/reshape | solution.py:58
  96.1 7.0 %reduce_sum.36 = f32[4,8,256]{2,1,0:T(8,128)S(1)} reduce(f32[4,2,8,2,256,2]{5,4,3,2,1,0:T(8,128)} %reshape.47, f32[]{:T(128)} %constant.24.clone.1), dimensions={1,3,5}, to_apply=%region_0.1 | reduce | flops 57344 | bytes 294916 | tf_op jit(solution)/shard_map/reduce_sum | solution.py:58
  103.7 18.1 %reshape.48 = f32[4,2,8,2,256,2]{5,4,3,2,1,0:T(8,128)} reshape(f32[8,16,512]{2,1,0:T(8,128)S(1)} %fusion.37) | data formatting | bytes 524288 | tf_op jit(solution)/shard_map/reshape | solution.py:58
  121.8 7.0 %reduce_sum.37 = f32[4,8,256]{2,1,0:T(8,128)S(1)} reduce(f32[4,2,8,2,256,2]{5,4,3,2,1,0:T(8,128)} %reshape.48, f32[]{:T(128)} %constant.24.clone.1), dimensions={1,3,5}, to_apply=%region_1.2 | reduce | flops 57344 | bytes 294916 | tf_op jit(solution)/shard_map/reduce_sum | solution.py:58
  137.2 6.0 %collective-permute-start.19 = (f32[6,1,256]{2,1,0:T(1,128)S(1)}, f32[6,1,256]{2,1,0:T(1,128)S(1)}, u32[]{:S(2)}, u32[]{:S(2)}) collective-permute-start(f32[6,1,256]{2,1,0:T(1,128)S(1)} %get-tuple-element.90), channel_id=1, source_target_pairs={{0,1},{1,2},{2,3},{3,4},{4,5},{5,6},{6,7},{7,8},{8,9},{9,10},{10,1... | collective-permute-start | bytes 18440 | tf_op jit(solution)/shard_map/ppermute | solution.py:21
  145.2 4.2 collective-permute-done.18
  163.1 4.2 collective-permute-done.22
  181.1 4.2 collective-permute-done.26
  199.3 4.0 collective-permute-done.30
  223.0 4.2 collective-permute-done.34
  240.7 4.2 collective-permute-done.38
  258.5 4.2 collective-permute-done.42
  276.9 4.2 collective-permute-done.46
  294.8 4.2 collective-permute-done.50
  312.8 4.2 collective-permute-done.54
  330.8 4.2 collective-permute-done.58
  345.8 3.4 collective-permute-done.60
  354.3 4.4 %collective-permute-done.62 = f32[10,1,512]{2,1,0:T(1,128)S(1)} collective-permute-done((f32[10,1,512]{2,1,0:T(1,128)S(1)}, f32[10,1,512]{2,1,0:T(1,128)S(1)}, u32[]{:S(2)}, u32[]{:S(2)}) %collective-permute-start.62) | collective-permute-done | bytes 20512 | tf_op jit(solution)/shard_map/ppermute | solution.py:23
  364.6 3.4 collective-permute-done.64
  373.1 4.4 %collective-permute-done.66 = f32[10,1,512]{2,1,0:T(1,128)S(1)} collective-permute-done((f32[10,1,512]{2,1,0:T(1,128)S(1)}, f32[10,1,512]{2,1,0:T(1,128)S(1)}, u32[]{:S(2)}, u32[]{:S(2)}) %collective-permute-start.66) | collective-permute-done | bytes 20512 | tf_op jit(solution)/shard_map/ppermute | solution.py:23
  383.4 3.4 collective-permute-done.68
  391.8 4.4 %collective-permute-done.70 = f32[10,1,512]{2,1,0:T(1,128)S(1)} collective-permute-done((f32[10,1,512]{2,1,0:T(1,128)S(1)}, f32[10,1,512]{2,1,0:T(1,128)S(1)}, u32[]{:S(2)}, u32[]{:S(2)}) %collective-permute-start.70) | collective-permute-done | bytes 20512 | tf_op jit(solution)/shard_map/ppermute | solution.py:23
  398.9 3.5 collective-permute-start.72
  410.8 4.4 %collective-permute-done.74 = f32[10,1,512]{2,1,0:T(1,128)S(1)} collective-permute-done((f32[10,1,512]{2,1,0:T(1,128)S(1)}, f32[10,1,512]{2,1,0:T(1,128)S(1)}, u32[]{:S(2)}, u32[]{:S(2)}) %collective-permute-start.74) | collective-permute-done | bytes 20512 | tf_op jit(solution)/shard_map/ppermute | solution.py:23
  (255 shorter events, 265.4 us)
Async XLA Ops:
  5.2 6.8 %collective-permute-start = (f32[1,16,512]{2,1,0:T(8,128)S(1)}, f32[1,16,512]{2,1,0:T(8,128)S(1)}, u32[]{:S(2)}, u32[]{:S(2)}) collective-permute-start(f32[1,16,512]{2,1,0:T(8,128)S(1)} %get-tuple-element.75), channel_id=1, source_target_pairs={{16,0},{32,16},{48,32},{64,48},{80,64},{96,80},{112,96},{128,112},... | collective-permute-start | bytes 98312 | tf_op jit(solution)/shard_map/ppermute | solution.py:23
  12.0 9.1 %collective-permute-start.3 = (f32[10,1,512]{2,1,0:T(1,128)S(1)}, f32[10,1,512]{2,1,0:T(1,128)S(1)}, u32[]{:S(2)}, u32[]{:S(2)}) collective-permute-start(f32[10,1,512]{2,1,0:T(1,128)S(1)} %get-tuple-element.56), channel_id=1, source_target_pairs={{0,1},{1,2},{2,3},{3,4},{4,5},{5,6},{6,7},{7,8},{8,9},{9,10},{10,1... | collective-permute-start | bytes 61448 | tf_op jit(solution)/shard_map/ppermute | solution.py:21
  19.2 6.3 %collective-permute-start.2 = (f32[10,1,512]{2,1,0:T(1,128)S(1)}, f32[10,1,512]{2,1,0:T(1,128)S(1)}, u32[]{:S(2)}, u32[]{:S(2)}) collective-permute-start(f32[10,1,512]{2,1,0:T(1,128)S(1)} %get-tuple-element.57), channel_id=1, source_target_pairs={{1,0},{2,1},{3,2},{4,3},{5,4},{6,5},{7,6},{8,7},{9,8},{10,9},{11,1... | collective-permute-start | bytes 61448 | tf_op jit(solution)/shard_map/ppermute | solution.py:23
  28.1 6.8 %collective-permute-start.4 = (f32[1,16,512]{2,1,0:T(8,128)S(1)}, f32[1,16,512]{2,1,0:T(8,128)S(1)}, u32[]{:S(2)}, u32[]{:S(2)}) collective-permute-start(f32[1,16,512]{2,1,0:T(8,128)S(1)} %get-tuple-element.73), channel_id=1, source_target_pairs={{16,0},{32,16},{48,32},{64,48},{80,64},{96,80},{112,96},{128,112},... | collective-permute-start | bytes 98312 | tf_op jit(solution)/shard_map/ppermute | solution.py:23
  38.0 6.3 %collective-permute-start.6 = (f32[10,1,512]{2,1,0:T(1,128)S(1)}, f32[10,1,512]{2,1,0:T(1,128)S(1)}, u32[]{:S(2)}, u32[]{:S(2)}) collective-permute-start(f32[10,1,512]{2,1,0:T(1,128)S(1)} %get-tuple-element.55), channel_id=1, source_target_pairs={{1,0},{2,1},{3,2},{4,3},{5,4},{6,5},{7,6},{8,7},{9,8},{10,9},{11,1... | collective-permute-start | bytes 61448 | tf_op jit(solution)/shard_map/ppermute | solution.py:23
  46.9 6.8 %collective-permute-start.8 = (f32[1,16,512]{2,1,0:T(8,128)S(1)}, f32[1,16,512]{2,1,0:T(8,128)S(1)}, u32[]{:S(2)}, u32[]{:S(2)}) collective-permute-start(f32[1,16,512]{2,1,0:T(8,128)S(1)} %get-tuple-element.71), channel_id=1, source_target_pairs={{16,0},{32,16},{48,32},{64,48},{80,64},{96,80},{112,96},{128,112},... | collective-permute-start | bytes 98312 | tf_op jit(solution)/shard_map/ppermute | solution.py:23
  56.8 6.3 %collective-permute-start.10 = (f32[10,1,512]{2,1,0:T(1,128)S(1)}, f32[10,1,512]{2,1,0:T(1,128)S(1)}, u32[]{:S(2)}, u32[]{:S(2)}) collective-permute-start(f32[10,1,512]{2,1,0:T(1,128)S(1)} %get-tuple-element.53), channel_id=1, source_target_pairs={{1,0},{2,1},{3,2},{4,3},{5,4},{6,5},{7,6},{8,7},{9,8},{10,9},{11,1... | collective-permute-start | bytes 61448 | tf_op jit(solution)/shard_map/ppermute | solution.py:23
  65.9 6.8 %collective-permute-start.12 = (f32[1,16,512]{2,1,0:T(8,128)S(1)}, f32[1,16,512]{2,1,0:T(8,128)S(1)}, u32[]{:S(2)}, u32[]{:S(2)}) collective-permute-start(f32[1,16,512]{2,1,0:T(8,128)S(1)} %get-tuple-element.69), channel_id=1, source_target_pairs={{16,0},{32,16},{48,32},{64,48},{80,64},{96,80},{112,96},{128,112},... | collective-permute-start | bytes 98312 | tf_op jit(solution)/shard_map/ppermute | solution.py:23
  72.7 30.4 %collective-permute-start.15 = (f32[10,1,512]{2,1,0:T(1,128)S(1)}, f32[10,1,512]{2,1,0:T(1,128)S(1)}, u32[]{:S(2)}, u32[]{:S(2)}) collective-permute-start(f32[10,1,512]{2,1,0:T(1,128)S(1)} %get-tuple-element.50), channel_id=1, source_target_pairs={{0,1},{1,2},{2,3},{3,4},{4,5},{5,6},{6,7},{7,8},{8,9},{9,10},{10,1... | collective-permute-start | bytes 61448 | tf_op jit(solution)/shard_map/ppermute | solution.py:21
  76.1 27.0 %collective-permute-start.14 = (f32[10,1,512]{2,1,0:T(1,128)S(1)}, f32[10,1,512]{2,1,0:T(1,128)S(1)}, u32[]{:S(2)}, u32[]{:S(2)}) collective-permute-start(f32[10,1,512]{2,1,0:T(1,128)S(1)} %get-tuple-element.51), channel_id=1, source_target_pairs={{1,0},{2,1},{3,2},{4,3},{5,4},{6,5},{7,6},{8,7},{9,8},{10,9},{11,1... | collective-permute-start | bytes 61448 | tf_op jit(solution)/shard_map/ppermute | solution.py:23
  130.7 6.5 %collective-permute-start.16 = (f32[1,8,256]{2,1,0:T(8,128)S(1)}, f32[1,8,256]{2,1,0:T(8,128)S(1)}, u32[]{:S(2)}, u32[]{:S(2)}) collective-permute-start(f32[1,8,256]{2,1,0:T(8,128)S(1)} %get-tuple-element.109), channel_id=1, source_target_pairs={{16,0},{32,16},{48,32},{64,48},{80,64},{96,80},{112,96},{128,112},... | collective-permute-start | bytes 24584 | tf_op jit(solution)/shard_map/ppermute | solution.py:23
  137.2 7.9 %collective-permute-start.19 = (f32[6,1,256]{2,1,0:T(1,128)S(1)}, f32[6,1,256]{2,1,0:T(1,128)S(1)}, u32[]{:S(2)}, u32[]{:S(2)}) collective-permute-start(f32[6,1,256]{2,1,0:T(1,128)S(1)} %get-tuple-element.90), channel_id=1, source_target_pairs={{0,1},{1,2},{2,3},{3,4},{4,5},{5,6},{6,7},{7,8},{8,9},{9,10},{10,1... | collective-permute-start | bytes 18440 | tf_op jit(solution)/shard_map/ppermute | solution.py:21
  151.6 6.5 %collective-permute-start.20 = (f32[1,8,256]{2,1,0:T(8,128)S(1)}, f32[1,8,256]{2,1,0:T(8,128)S(1)}, u32[]{:S(2)}, u32[]{:S(2)}) collective-permute-start(f32[1,8,256]{2,1,0:T(8,128)S(1)} %get-tuple-element.107), channel_id=1, source_target_pairs={{16,0},{32,16},{48,32},{64,48},{80,64},{96,80},{112,96},{128,112},... | collective-permute-start | bytes 24584 | tf_op jit(solution)/shard_map/ppermute | solution.py:23
  169.5 6.5 %collective-permute-start.24 = (f32[1,8,256]{2,1,0:T(8,128)S(1)}, f32[1,8,256]{2,1,0:T(8,128)S(1)}, u32[]{:S(2)}, u32[]{:S(2)}) collective-permute-start(f32[1,8,256]{2,1,0:T(8,128)S(1)} %get-tuple-element.105), channel_id=1, source_target_pairs={{16,0},{32,16},{48,32},{64,48},{80,64},{96,80},{112,96},{128,112},... | collective-permute-start | bytes 24584 | tf_op jit(solution)/shard_map/ppermute | solution.py:23
  187.5 6.5 %collective-permute-start.28 = (f32[1,8,256]{2,1,0:T(8,128)S(1)}, f32[1,8,256]{2,1,0:T(8,128)S(1)}, u32[]{:S(2)}, u32[]{:S(2)}) collective-permute-start(f32[1,8,256]{2,1,0:T(8,128)S(1)} %get-tuple-element.103), channel_id=1, source_target_pairs={{16,0},{32,16},{48,32},{64,48},{80,64},{96,80},{112,96},{128,112},... | collective-permute-start | bytes 24584 | tf_op jit(solution)/shard_map/ppermute | solution.py:23
  211.5 6.4 %collective-permute-start.32 = (f32[1,4,128]{2,1,0:T(4,128)S(1)}, f32[1,4,128]{2,1,0:T(4,128)S(1)}, u32[]{:S(2)}, u32[]{:S(2)}) collective-permute-start(f32[1,4,128]{2,1,0:T(4,128)S(1)} %get-tuple-element.121), channel_id=1, source_target_pairs={{16,0},{32,16},{48,32},{64,48},{80,64},{96,80},{112,96},{128,112},... | collective-permute-start | bytes 6152 | tf_op jit(solution)/shard_map/ppermute | solution.py:23
  229.2 6.4 %collective-permute-start.36 = (f32[1,4,128]{2,1,0:T(4,128)S(1)}, f32[1,4,128]{2,1,0:T(4,128)S(1)}, u32[]{:S(2)}, u32[]{:S(2)}) collective-permute-start(f32[1,4,128]{2,1,0:T(4,128)S(1)} %get-tuple-element.119), channel_id=1, source_target_pairs={{16,0},{32,16},{48,32},{64,48},{80,64},{96,80},{112,96},{128,112},... | collective-permute-start | bytes 6152 | tf_op jit(solution)/shard_map/ppermute | solution.py:23
  247.0 6.4 %collective-permute-start.40 = (f32[1,4,128]{2,1,0:T(4,128)S(1)}, f32[1,4,128]{2,1,0:T(4,128)S(1)}, u32[]{:S(2)}, u32[]{:S(2)}) collective-permute-start(f32[1,4,128]{2,1,0:T(4,128)S(1)} %get-tuple-element.117), channel_id=1, source_target_pairs={{16,0},{32,16},{48,32},{64,48},{80,64},{96,80},{112,96},{128,112},... | collective-permute-start | bytes 6152 | tf_op jit(solution)/shard_map/ppermute | solution.py:23
  265.3 6.5 %collective-permute-start.44 = (f32[1,8,256]{2,1,0:T(8,128)S(1)}, f32[1,8,256]{2,1,0:T(8,128)S(1)}, u32[]{:S(2)}, u32[]{:S(2)}) collective-permute-start(f32[1,8,256]{2,1,0:T(8,128)S(1)} %get-tuple-element.99), channel_id=1, source_target_pairs={{16,0},{32,16},{48,32},{64,48},{80,64},{96,80},{112,96},{128,112},... | collective-permute-start | bytes 24584 | tf_op jit(solution)/shard_map/ppermute | solution.py:23
  283.3 6.5 %collective-permute-start.48 = (f32[1,8,256]{2,1,0:T(8,128)S(1)}, f32[1,8,256]{2,1,0:T(8,128)S(1)}, u32[]{:S(2)}, u32[]{:S(2)}) collective-permute-start(f32[1,8,256]{2,1,0:T(8,128)S(1)} %get-tuple-element.97), channel_id=1, source_target_pairs={{16,0},{32,16},{48,32},{64,48},{80,64},{96,80},{112,96},{128,112},... | collective-permute-start | bytes 24584 | tf_op jit(solution)/shard_map/ppermute | solution.py:23
  301.2 6.5 %collective-permute-start.52 = (f32[1,8,256]{2,1,0:T(8,128)S(1)}, f32[1,8,256]{2,1,0:T(8,128)S(1)}, u32[]{:S(2)}, u32[]{:S(2)}) collective-permute-start(f32[1,8,256]{2,1,0:T(8,128)S(1)} %get-tuple-element.95), channel_id=1, source_target_pairs={{16,0},{32,16},{48,32},{64,48},{80,64},{96,80},{112,96},{128,112},... | collective-permute-start | bytes 24584 | tf_op jit(solution)/shard_map/ppermute | solution.py:23
  319.2 6.5 %collective-permute-start.56 = (f32[1,8,256]{2,1,0:T(8,128)S(1)}, f32[1,8,256]{2,1,0:T(8,128)S(1)}, u32[]{:S(2)}, u32[]{:S(2)}) collective-permute-start(f32[1,8,256]{2,1,0:T(8,128)S(1)} %get-tuple-element.93), channel_id=1, source_target_pairs={{16,0},{32,16},{48,32},{64,48},{80,64},{96,80},{112,96},{128,112},... | collective-permute-start | bytes 24584 | tf_op jit(solution)/shard_map/ppermute | solution.py:23
  342.4 6.8 %collective-permute-start.60 = (f32[1,16,512]{2,1,0:T(8,128)S(1)}, f32[1,16,512]{2,1,0:T(8,128)S(1)}, u32[]{:S(2)}, u32[]{:S(2)}) collective-permute-start(f32[1,16,512]{2,1,0:T(8,128)S(1)} %get-tuple-element.67), channel_id=1, source_target_pairs={{16,0},{32,16},{48,32},{64,48},{80,64},{96,80},{112,96},{128,112},... | collective-permute-start | bytes 98312 | tf_op jit(solution)/shard_map/ppermute | solution.py:23
  352.3 6.3 %collective-permute-start.62 = (f32[10,1,512]{2,1,0:T(1,128)S(1)}, f32[10,1,512]{2,1,0:T(1,128)S(1)}, u32[]{:S(2)}, u32[]{:S(2)}) collective-permute-start(f32[10,1,512]{2,1,0:T(1,128)S(1)} %get-tuple-element.49), channel_id=1, source_target_pairs={{1,0},{2,1},{3,2},{4,3},{5,4},{6,5},{7,6},{8,7},{9,8},{10,9},{11,1... | collective-permute-start | bytes 61448 | tf_op jit(solution)/shard_map/ppermute | solution.py:23
  361.2 6.8 %collective-permute-start.64 = (f32[1,16,512]{2,1,0:T(8,128)S(1)}, f32[1,16,512]{2,1,0:T(8,128)S(1)}, u32[]{:S(2)}, u32[]{:S(2)}) collective-permute-start(f32[1,16,512]{2,1,0:T(8,128)S(1)} %get-tuple-element.65), channel_id=1, source_target_pairs={{16,0},{32,16},{48,32},{64,48},{80,64},{96,80},{112,96},{128,112},... | collective-permute-start | bytes 98312 | tf_op jit(solution)/shard_map/ppermute | solution.py:23
  371.1 6.3 %collective-permute-start.66 = (f32[10,1,512]{2,1,0:T(1,128)S(1)}, f32[10,1,512]{2,1,0:T(1,128)S(1)}, u32[]{:S(2)}, u32[]{:S(2)}) collective-permute-start(f32[10,1,512]{2,1,0:T(1,128)S(1)} %get-tuple-element.47), channel_id=1, source_target_pairs={{1,0},{2,1},{3,2},{4,3},{5,4},{6,5},{7,6},{8,7},{9,8},{10,9},{11,1... | collective-permute-start | bytes 61448 | tf_op jit(solution)/shard_map/ppermute | solution.py:23
  380.0 6.8 %collective-permute-start.68 = (f32[1,16,512]{2,1,0:T(8,128)S(1)}, f32[1,16,512]{2,1,0:T(8,128)S(1)}, u32[]{:S(2)}, u32[]{:S(2)}) collective-permute-start(f32[1,16,512]{2,1,0:T(8,128)S(1)} %get-tuple-element.63), channel_id=1, source_target_pairs={{16,0},{32,16},{48,32},{64,48},{80,64},{96,80},{112,96},{128,112},... | collective-permute-start | bytes 98312 | tf_op jit(solution)/shard_map/ppermute | solution.py:23
  389.9 6.3 %collective-permute-start.70 = (f32[10,1,512]{2,1,0:T(1,128)S(1)}, f32[10,1,512]{2,1,0:T(1,128)S(1)}, u32[]{:S(2)}, u32[]{:S(2)}) collective-permute-start(f32[10,1,512]{2,1,0:T(1,128)S(1)} %get-tuple-element.45), channel_id=1, source_target_pairs={{1,0},{2,1},{3,2},{4,3},{5,4},{6,5},{7,6},{8,7},{9,8},{10,9},{11,1... | collective-permute-start | bytes 61448 | tf_op jit(solution)/shard_map/ppermute | solution.py:23
  398.9 6.9 %collective-permute-start.72 = (f32[1,16,512]{2,1,0:T(8,128)S(1)}, f32[1,16,512]{2,1,0:T(8,128)S(1)}, u32[]{:S(2)}, u32[]{:S(2)}) collective-permute-start(f32[1,16,512]{2,1,0:T(8,128)S(1)} %get-tuple-element.61), channel_id=1, source_target_pairs={{16,0},{32,16},{48,32},{64,48},{80,64},{96,80},{112,96},{128,112},... | collective-permute-start | bytes 98312 | tf_op jit(solution)/shard_map/ppermute | solution.py:23
  408.9 6.3 %collective-permute-start.74 = (f32[10,1,512]{2,1,0:T(1,128)S(1)}, f32[10,1,512]{2,1,0:T(1,128)S(1)}, u32[]{:S(2)}, u32[]{:S(2)}) collective-permute-start(f32[10,1,512]{2,1,0:T(1,128)S(1)} %get-tuple-element.43), channel_id=1, source_target_pairs={{1,0},{2,1},{3,2},{4,3},{5,4},{6,5},{7,6},{8,7},{9,8},{10,9},{11,1... | collective-permute-start | bytes 61448 | tf_op jit(solution)/shard_map/ppermute | solution.py:23
  417.8 6.8 %collective-permute-start.76 = (f32[1,16,512]{2,1,0:T(8,128)S(1)}, f32[1,16,512]{2,1,0:T(8,128)S(1)}, u32[]{:S(2)}, u32[]{:S(2)}) collective-permute-start(f32[1,16,512]{2,1,0:T(8,128)S(1)} %get-tuple-element.59), channel_id=1, source_target_pairs={{16,0},{32,16},{48,32},{64,48},{80,64},{96,80},{112,96},{128,112},... | collective-permute-start | bytes 98312 | tf_op jit(solution)/shard_map/ppermute | solution.py:23
  427.7 6.3 %collective-permute-start.78 = (f32[10,1,512]{2,1,0:T(1,128)S(1)}, f32[10,1,512]{2,1,0:T(1,128)S(1)}, u32[]{:S(2)}, u32[]{:S(2)}) collective-permute-start(f32[10,1,512]{2,1,0:T(1,128)S(1)} %get-tuple-element.41), channel_id=1, source_target_pairs={{1,0},{2,1},{3,2},{4,3},{5,4},{6,5},{7,6},{8,7},{9,8},{10,9},{11,1... | collective-permute-start | bytes 61448 | tf_op jit(solution)/shard_map/ppermute | solution.py:23
  (56 other events, 693.3 us)
where the time goes:
time: 438 us; the launch traced here: 435 us
  starting transfers between devices  213 us (49%)
  waiting for transfers between devices  145 us (33%)
  local copies, waits for them, and re-layouts  46.2 us (11%)
  other arithmetic  28.2 us (6%)
    ppermute x40, waiting for transfers between devices, with_halo(): lax.ppermute(head, axis, [((i + 1) % count, i) for i in range(ends)])  145 us
    ppermute x40, starting transfers between devices, with_halo(): lax.ppermute(tail, axis, [(i, (i + 1) % count) for i in range(ends)])  108 us
    ppermute x40, starting transfers between devices, with_halo(): lax.ppermute(head, axis, [((i + 1) % count, i) for i in range(ends)])  105 us
    reshape x3, local copies, waits for them, and re-layouts, blocks(): return field.reshape(a // 2, 2, b // 2, 2, c // 2, 2).sum(axis=(1, 3, 5))  38.3 us
    reduce_sum x4, other arithmetic, blocks(): return field.reshape(a // 2, 2, b // 2, 2, c // 2, 2).sum(axis=(1, 3, 5))  14.4 us
  transfers between devices with their start and end apart: 80, of which 39 were waited for; matrix products, arithmetic and copies ran while one was open for 6% of the time, Pallas kernels for 0%

commit v1 on v0

v1 whole, which is shorter than its diff:
```python
import jax
import jax.numpy as jnp
from jax import lax
from jax.experimental import pallas as pl
from jax.experimental.pallas import tpu as pltpu
from jax.sharding import PartitionSpec as P


DEGREE = 4
THETA = 1.15
DELTA = 0.85
FIRST = 1.0 / (6.0 * THETA)
LEAST = 0.05
F32 = jnp.float32
LANES = 128


def coefficients():
    sigma = THETA / DELTA
    rho = 1.0 / sigma
    pairs = []
    for turn in range(DEGREE - 1):
        rho_next = 1.0 / (2.0 * sigma - rho)
        pairs.append((rho_next * rho, 2.0 * rho_next / (6.0 * DELTA)))
        rho = rho_next
    return pairs


COEFFICIENTS = coefficients()


def iota(shape, dim):
    return lax.broadcasted_iota(jnp.int32, shape, dim)


def row_mask(rows, base, count):
    place = iota((rows, LANES), 0) + base
    return jnp.where((place >= 0) & (place < count), 1.0, 0.0).astype(F32)


def loop(low, high, body):
    def step(z, carry):
        body(z)
        return carry

    lax.fori_loop(low, high, step, 0)


def columns(ref, z):
    return [ref[z, :, pl.ds(k, LANES)] for k in range(0, ref.shape[2], LANES)]


def put(ref, z, cols):
    for k, col in enumerate(cols):
        ref[z, :, pl.ds(k * LANES, LANES)] = col


def neighbours(ref, z):
    here = columns(ref, z)
    rows = here[0].shape[0]
    lane = iota((rows, LANES), 1)
    above = [pltpu.roll(c, 1, 1) for c in here]
    below = [pltpu.roll(c, LANES - 1, 1) for c in here]
    out = []
    for k, c in enumerate(here):
        left = above[k - 1] if k > 0 else 0.0
        right = below[k + 1] if k + 1 < len(here) else 0.0
        total = jnp.where(lane == 0, left, above[k]) + jnp.where(lane == LANES - 1, right, below[k])
        total = total + (pltpu.roll(c, 1, 0) + pltpu.roll(c, rows - 1, 0))
        at = pl.ds(k * LANES, LANES)
        out.append(total + (ref[z - 1, :, at] + ref[z + 1, :, at]))
    return here, out


def smooth(bufs, q, y, low, high, y_low, y_high, y_off, y_new, mask, z_scale, passes, finish=None):
    first, second = bufs

    def begin(z, keep):
        scale = z_scale(z, FIRST)
        w = [(scale * mask) * c for c in columns(q, z)]
        put(first, z, w)
        if keep:
            old = [0.0] * len(w) if y_new else columns(y, z - y_off)
            put(y, z - y_off, [a + b for a, b in zip(old, w)])

    def ranged(lo, hi, make):
        if lo < min(y_low, hi):
            loop(lo, min(y_low, hi), lambda z: make(z, False))
        if max(lo, y_low) < min(hi, y_high):
            loop(max(lo, y_low), min(hi, y_high), lambda z: make(z, True))
        if max(lo, y_high) < hi:
            loop(max(lo, y_high), hi, lambda z: make(z, False))

    ranged(low, high, begin)
    for turn in range(passes):
        source, target = (first, second) if turn % 2 == 0 else (second, first)

        def advance(z, keep, source=source, target=target, turn=turn):
            here, around = neighbours(source, z)
            rest = [a - 6.0 * b + c for a, b, c in zip(columns(q, z), here, around)]
            if turn == DEGREE - 1 and finish is not None:
                finish(z, rest)
                return
            put(q, z, rest)
            if turn < DEGREE - 1:
                c1, c2 = COEFFICIENTS[turn]
                scale = z_scale(z, c2) * mask
                w = [c1 * a + scale * b for a, b in zip(here, rest)]
                put(target, z, w)
                if keep:
                    put(y, z - y_off, [a + b for a, b in zip(columns(y, z - y_off), w)])

        ranged(low + 1 + turn, high - 1 - turn, advance)


def z_mask(base, count):
    def scaled(z, value):
        place = z + base
        return jnp.where((place >= 0) & (place < count), F32(value), F32(0.0))

    return scaled


def odd_even(ref, at, start):
    return ref[at, pl.ds(start, 16, 2), :] + ref[at, pl.ds(start + 1, 16, 2), :]


def exact_product(left, right):
    high = left.astype(jnp.bfloat16)
    rest = left - high.astype(F32)
    middle = rest.astype(jnp.bfloat16)
    low = (rest - middle.astype(F32)).astype(jnp.bfloat16)
    parts = [jnp.dot(part, right, preferred_element_type=F32) for part in (high, middle, low)]
    return (parts[2] + parts[1]) + parts[0]


def pair_sum(length):
    at = iota((length, length // 2), 0)
    return jnp.where((at >> 1) == iota((length, length // 2), 1), 1.0, 0.0).astype(jnp.bfloat16)


def pair_copy(length):
    at = iota((length // 2, length), 1)
    return jnp.where((at >> 1) == iota((length // 2, length), 0), 1.0, 0.0).astype(jnp.bfloat16)


def scale_kernel(load, density, void, up, down, root):
    bricks = jnp.where(void[0] == 1, 1.0, 0.0).astype(F32)
    bricks = jnp.concatenate([jnp.broadcast_to(bricks[k : k + 1], (8, 64)) for k in range(2)], axis=0)
    spread = jnp.where((iota((64, 512), 1) >> 3) == iota((64, 512), 0), 1.0, 0.0).astype(jnp.bfloat16)
    voids = jnp.dot(bricks.astype(jnp.bfloat16), spread, preferred_element_type=F32)
    for z in range(8):
        d = density[z]
        r = jnp.sqrt(jnp.where(voids > 0.5, 0.01, 0.01 + 0.99 * d * d * d))
        q = load[z] / r
        up[z] = q
        down[z] = q
        root[z] = r
        if z >= 3:
            up[5 + z] = r
        if z < 5:
            down[8 + z] = r


def fine_pack_kernel(low, up, root, high, left, right):
    at = 0
    for ref, count in ((low, 13), (up, 8), (root, 8), (high, 13)):
        for k in range(count):
            left[at + k] = ref[k, 0:8]
            right[at + k] = ref[k, 8:16]
        at += count


def fine_pre_kernel(counts, low, up, root, high, left, right, q, y, r, mid_low, mid_high, w0, w1, s0, s1, m0):
    gz, xy = lax.axis_index("gz"), lax.axis_index("xy")
    mask = row_mask(32, 16 * xy - 8, 16 * counts[1])
    z_scale = z_mask(8 * gz - 8, 8 * counts[0])

    def row(target, z, ref, k, at):
        target[z, 0:8] = left[at + k]
        target[z, 8:24] = ref[k]
        target[z, 24:32] = right[at + k]

    for k in range(8):
        row(q, k, low, k, 0)
        row(q, 8 + k, up, k, 13)
        row(q, 16 + k, high, k, 29)
        row(r, 5 + k, root, k, 21)
    for k in range(5):
        row(r, k, low, 8 + k, 0)
        row(r, 13 + k, high, 8 + k, 29)
    smooth((w0, w1), q, y, 0, 24, 8, 16, 8, True, mask, z_scale, DEGREE)

    s0[:, 32:40] = jnp.zeros((32, 8, LANES), F32)
    s1[:, 32:40] = jnp.zeros((32, 8, LANES), F32)

    def fold(m):
        ra, rb = columns(r, 2 * m + 1), columns(r, 2 * m + 2)
        qa, qb = columns(q, 2 * m + 4), columns(q, 2 * m + 5)
        for k in range(4):
            s0[4 * m + k, 0:32] = ra[k] * qa[k] + rb[k] * qb[k]
            s1[4 * m + k, 0:32] = ra[k] + rb[k]

    loop(0, 8, fold)
    for m in range(8):
        for k in range(4):
            at = pl.ds(k * LANES, LANES)
            m0[m * 16 : m * 16 + 16, at] = odd_even(s0, 4 * m + k, 4)
            m0[128 + m * 16 : 144 + m * 16, at] = odd_even(s1, 4 * m + k, 4)
    sums = exact_product(m0[...], pair_sum(512))
    roots = 0.125 * sums[128:256]
    rights = 0.5 * sums[0:128] / jnp.maximum(roots, LEAST)
    for m in range(4):
        mid_low[m] = rights[m * 16 : m * 16 + 16]
        mid_low[4 + m] = roots[m * 16 : m * 16 + 16]
        mid_high[m] = rights[64 + m * 16 : 80 + m * 16]
        mid_high[4 + m] = roots[64 + m * 16 : 80 + m * 16]


def mid_pack_kernel(*refs):
    parts, left, right = refs[:6], refs[6], refs[7]
    for n, ref in enumerate(parts):
        for k in range(8):
            right[8 * n + k] = ref[k, 0:8]
            left[8 * n + k] = ref[k, 4:12]


def mid_pre_kernel(counts, *refs):
    parts, (left, right), rest = refs[:6], refs[6:8], refs[8:]
    q, y, r, coarse, coarse_low, coarse_high, coarse_root, w0, w1, s0, s1, m0 = rest
    gz, xy = lax.axis_index("gz"), lax.axis_index("xy")
    mask = row_mask(32, 8 * xy - 10, 8 * counts[1])
    z_scale = z_mask(4 * gz - 10, 4 * counts[0])
    for n, ref in enumerate(parts):
        for k in range(8):
            target, z = (q, 4 * n + k) if k < 4 else (r, 4 * n + k - 4)
            target[z, 0:8] = left[8 * n + k]
            target[z, 8:24] = ref[k]
            target[z, 20:28] = right[8 * n + k]
            target[z, 28:32] = jnp.zeros((4, 256), F32)
    smooth((w0, w1), q, y, 0, 24, 7, 17, 7, True, mask, z_scale, DEGREE)

    s0[:, 32:40] = jnp.zeros((16, 8, LANES), F32)
    s1[:, 32:40] = jnp.zeros((20, 8, LANES), F32)
    for m in range(10):
        ra, rb = columns(r, 2 * m + 2), columns(r, 2 * m + 3)
        qa, qb = columns(q, 2 * m + 2), columns(q, 2 * m + 3)
        for k in range(2):
            s1[2 * m + k, 0:32] = ra[k] + rb[k]
            if 0 < m < 9:
                s0[2 * m - 2 + k, 0:32] = ra[k] * qa[k] + rb[k] * qb[k]
    for m in range(10):
        for k in range(2):
            at = pl.ds(k * LANES, LANES)
            m0[m * 16 : m * 16 + 16, at] = odd_even(s1, 2 * m + k, 2)
            if 0 < m < 9:
                j = 160 + (m - 1) * 16
                m0[j : j + 16, at] = odd_even(s1, 2 * m + k, 4)
                j = 288 + (m - 1) * 16
                m0[j : j + 16, at] = odd_even(s0, 2 * m - 2 + k, 4)
    sums = exact_product(m0[...], pair_sum(256))
    rights = 0.5 * sums[288:416] / jnp.maximum(0.125 * sums[160:288], LEAST)
    for m in range(10):
        coarse_root[m] = 0.125 * sums[m * 16 : m * 16 + 16]
    for m in range(8):
        coarse[m] = rights[m * 16 : m * 16 + 16]
    for m in range(2):
        coarse_low[m] = rights[m * 16 : m * 16 + 16]
        coarse_high[m] = rights[96 + m * 16 : 112 + m * 16]


def coarse_pack_kernel(*refs):
    parts, left, right = refs[:5], refs[5], refs[6]
    at = 0
    for ref in parts:
        for k in range(ref.shape[0]):
            right[at + k] = ref[k, 0:8]
            left[at + k] = ref[k, 6:14]
        at += ref.shape[0]


def finish_kernel(counts, *refs):
    parts, (left, right), refs = refs[:5], refs[5:7], refs[7:]
    coarse_root, mid_q, mid_y, mid_r, fine_q, fine_y, fine_r, out_x, out_r = refs[:9]
    cq, cy, cw0, cw1, mq, my, mw0, mw1, mp, fq, fy, fw0, fw1, fp, e0, u0, e1, u1 = refs[9:]
    gz, xy = lax.axis_index("gz"), lax.axis_index("xy")

    at = 0
    for ref in parts:
        for k in range(ref.shape[0]):
            cq[at + k, 0:8] = left[at + k]
            cq[at + k, 4:20] = ref[k]
            cq[at + k, 14:22] = right[at + k]
            cq[at + k, 22:24] = jnp.zeros((2, 128), F32)
        at += ref.shape[0]
    mask = row_mask(24, 4 * xy - 7, 4 * counts[1])
    z_scale = z_mask(2 * gz - 7, 2 * counts[0])
    smooth((cw0, cw1), cq, cy, 0, 16, 3, 13, 3, True, mask, z_scale, DEGREE - 1)
    for k in range(10):
        e0[k * 16 : k * 16 + 16] = cy[k, 3:19] / jnp.maximum(coarse_root[k], LEAST)
    u0[...] = exact_product(e0[...], pair_copy(256))

    mp[...] = jnp.zeros((2, 32, LANES), F32)
    for k in range(10):
        for j in range(2):
            at = pl.ds(j * LANES, LANES)
            value = u0[k * 16 : k * 16 + 12, at]
            mp[j, pl.ds(2, 12, 2), :] = value
            mp[j, pl.ds(3, 12, 2), :] = value
            mw1[2 * k + 2, :, at] = mid_r[2 * k + 2, :, at] * mp[j]
            mw1[2 * k + 3, :, at] = mid_r[2 * k + 3, :, at] * mp[j]

    def correct(w, q_in, q_out, y_in, y_out, y_low, y_high):
        def body(z, keep):
            here, around = neighbours(w, z)
            put(q_out, z, [a - 6.0 * b + c for a, b, c in zip(columns(q_in, z), here, around)])
            if keep:
                put(y_out, z - y_low, [a + b for a, b in zip(columns(y_in, z - y_low), here)])

        loop(4, y_low, lambda z: body(z, False))
        loop(y_low, y_high, lambda z: body(z, True))
        loop(y_high, 20, lambda z: body(z, False))

    correct(mw1, mid_q, mq, mid_y, my, 7, 17)
    mask = row_mask(32, 8 * xy - 10, 8 * counts[1])
    z_scale = z_mask(4 * gz - 10, 4 * counts[0])
    smooth((mw0, mw1), mq, my, 4, 20, 7, 17, 7, False, mask, z_scale, DEGREE - 1)
    for k in range(10):
        e1[k * 16 : k * 16 + 16] = my[k, 7:23] / jnp.maximum(mid_r[7 + k, 7:23], LEAST)
    u1[...] = exact_product(e1[...], pair_copy(512))

    fp[...] = jnp.zeros((4, 32, LANES), F32)
    for k in range(10):
        for j in range(4):
            at = pl.ds(j * LANES, LANES)
            value = u1[k * 16 : k * 16 + 14, at]
            fp[j, pl.ds(2, 14, 2), :] = value
            fp[j, pl.ds(3, 14, 2), :] = value
            if k > 0:
                fw1[2 * k + 2, :, at] = fine_r[2 * k - 1, :, at] * fp[j]
            if k < 9:
                fw1[2 * k + 3, :, at] = fine_r[2 * k, :, at] * fp[j]
    correct(fw1, fine_q, fq, fine_y, fy, 8, 16)
    mask = row_mask(32, 16 * xy - 8, 16 * counts[1])
    z_scale = z_mask(8 * gz - 8, 8 * counts[0])

    def finish(z, rest):
        for k, col in enumerate(rest):
            at = pl.ds(k * LANES, LANES)
            r = fine_r[z - 3, 8:24, at]
            out_r[z - 8, :, at] = r * col[8:24]
            out_x[z - 8, :, at] = fy[z - 8, 8:24, at] / r

    smooth((fw0, fw1), fq, fy, 4, 20, 8, 16, 8, False, mask, z_scale, DEGREE, finish)


def call(kernel, operands, out_shapes, scratch=()):
    whole = pl.BlockSpec(memory_space=pltpu.VMEM)
    return pl.pallas_call(
        kernel,
        out_shape=[jax.ShapeDtypeStruct(s, F32) for s in out_shapes],
        in_specs=[whole] * len(operands),
        out_specs=[whole] * len(out_shapes),
        scratch_shapes=[pltpu.VMEM(s, F32) for s in scratch],
        compiler_params=pltpu.CompilerParams(vmem_limit_bytes=24 * 1024 * 1024),
    )(*operands)


def send(block, axis, shift):
    count = lax.axis_size(axis)
    pairs = [(i, i + shift) for i in range(count) if 0 <= i + shift < count]
    return lax.ppermute(block, axis, pairs)


def with_counts(kernel):
    counts = (lax.axis_size("gz"), lax.axis_size("xy"))
    return lambda *refs: kernel(counts, *refs)


def on_device(load_field, density, void_mask):
    up, down, root = call(
        scale_kernel, (load_field, density, void_mask), [(13, 16, 512), (13, 16, 512), (8, 16, 512)]
    )
    low, high = send(up, "gz", 1), send(down, "gz", -1)
    to_left, to_right = call(fine_pack_kernel, (low, up, root, high), [(42, 8, 512)] * 2)
    left, right = send(to_right, "xy", 1), send(to_left, "xy", -1)
    fine_q, fine_y, fine_r, mid_low, mid_high = call(
        with_counts(fine_pre_kernel),
        (low, up, root, high, left, right),
        [(24, 32, 512), (8, 32, 512), (18, 32, 512), (8, 16, 256), (8, 16, 256)],
        [(24, 32, 512), (24, 32, 512), (32, 40, LANES), (32, 40, LANES), (256, 512)],
    )
    a1, b1 = send(mid_low, "gz", 1), send(mid_high, "gz", -1)
    a2, b2 = send(mid_low, "gz", 2), send(mid_high, "gz", -2)
    parts = (a2, a1, mid_low, mid_high, b1, b2)
    to_left, to_right = call(mid_pack_kernel, parts, [(48, 8, 256)] * 2)
    left, right = send(to_right, "xy", 1), send(to_left, "xy", -1)
    mid_q, mid_y, mid_r, coarse, coarse_low, coarse_high, coarse_root = call(
        with_counts(mid_pre_kernel),
        parts + (left, right),
        [(24, 32, 256), (10, 32, 256), (24, 32, 256), (8, 16, 128), (2, 16, 128), (2, 16, 128), (10, 16, 128)],
        [(24, 32, 256), (24, 32, 256), (16, 40, LANES), (20, 40, LANES), (416, 256)],
    )
    a1, b1 = send(coarse_low, "gz", 1), send(coarse_high, "gz", -1)
    a2, b2 = send(coarse_low, "gz", 2), send(coarse_high, "gz", -2)
    parts = (a2, a1, coarse, b1, b2)
    to_left, to_right = call(coarse_pack_kernel, parts, [(16, 8, 128)] * 2)
    left, right = send(to_right, "xy", 1), send(to_left, "xy", -1)
    return tuple(
        call(
            with_counts(finish_kernel),
            parts + (left, right, coarse_root, mid_q, mid_y, mid_r, fine_q, fine_y, fine_r),
            [(8, 16, 512), (8, 16, 512)],
            [(16, 24, 128), (10, 24, 128), (16, 24, 128), (16, 24, 128)]
            + [(24, 32, 256), (10, 32, 256), (24, 32, 256), (24, 32, 256), (2, 32, LANES)]
            + [(24, 32, 512), (8, 32, 512), (24, 32, 512), (24, 32, 512), (4, 32, LANES)]
            + [(160, 128), (160, 256), (160, 256), (160, 512)],
        )
    )


def solution(mesh):
    specs = (P("gz", "xy", None), P("gz", "xy", None), P("gz", "xy", None))
    return jax.shard_map(
        on_device, mesh=mesh, in_specs=specs, out_specs=specs[:2], check_vma=False
    )
```

time: 438 us -> 136 us (0.31)
  the two profiles are of different devices: /device:TPU:251 before, /device:TPU:199 now
where the time goes in v1:
time: 136 us; the launch traced here: 135 us
  starting transfers between devices  56.3 us (41%)
  waiting for transfers between devices  41.3 us (30%)
  Pallas kernels  34.2 us (25%)
  local copies, waits for them, and re-layouts  2.57 us (2%)
    ppermute x16, starting transfers between devices, send(): return lax.ppermute(block, axis, pairs)  56.3 us
    ppermute x16, waiting for transfers between devices, send(): return lax.ppermute(block, axis, pairs)  41.3 us
    pallas_call x7, Pallas kernels, call(): pl.pallas_call(kernel, out_shape=[jax.ShapeDtypeStruct(s, F32) for s in o...  34.2 us
  transfers between devices with their start and end apart: 16, of which 10 were waited for; matrix products, arithmetic and copies ran while one was open for 0% of the time, Pallas kernels for 0%

profile of v1, /device:TPU:199, one launch (start us, length us, event | category | flops | bytes accessed | tf_op | source)
XLA Modules:
  0.0 135.2 jit_solution(6618911392647709124)
XLA Ops:
  0.6 0.9 copy-done
  1.6 0.9 copy-done.1
  2.5 0.7 copy-done.2
  3.5 5.4 %collective-permute-start.1 = (f32[13,16,512]{2,1,0:T(8,128)S(1)}, f32[13,16,512]{2,1,0:T(8,128)S(1)}, u32[]{:S(2)}, u32[]{:S(2)}) collective-permute-start(f32[13,16,512]{2,1,0:T(8,128)S(1)} %get-tuple-element.25), channel_id=1, source_target_pairs={{16,0},{32,16},{48,32},{64,48},{80,64},{96,80},{112,96},{128,112},... | collective-permute-start | bytes 1277960 | tf_op jit(solution)/shard_map/ppermute | solution.py:372
  8.8 1.9 %collective-permute-start = (f32[13,16,512]{2,1,0:T(8,128)S(1)}, f32[13,16,512]{2,1,0:T(8,128)S(1)}, u32[]{:S(2)}, u32[]{:S(2)}) collective-permute-start(f32[13,16,512]{2,1,0:T(8,128)S(1)} %get-tuple-element.23.up.refs_1_), channel_id=1, source_target_pairs={{0,16},{16,32},{32,48},{48,64},{64,80},{80,96},{96,112},{112,128},... | collective-permute-start | bytes 1277960 | tf_op jit(solution)/shard_map/ppermute | solution.py:372
  10.8 6.5 %collective-permute-done.1.high.refs_3_ = f32[13,16,512]{2,1,0:T(8,128)S(1)} collective-permute-done((f32[13,16,512]{2,1,0:T(8,128)S(1)}, f32[13,16,512]{2,1,0:T(8,128)S(1)}, u32[]{:S(2)}, u32[]{:S(2)}) %collective-permute-start.1) | collective-permute-done | bytes 426016 | tf_op jit(solution)/shard_map/ppermute | solution.py:372
  17.3 5.9 %collective-permute-done.low.refs_0_ = f32[13,16,512]{2,1,0:T(8,128)S(1)} collective-permute-done((f32[13,16,512]{2,1,0:T(8,128)S(1)}, f32[13,16,512]{2,1,0:T(8,128)S(1)}, u32[]{:S(2)}, u32[]{:S(2)}) %collective-permute-start) | collective-permute-done | bytes 426016 | tf_op jit(solution)/shard_map/ppermute | solution.py:372
  23.3 7.0 %collective-permute-start.2 = (f32[42,8,512]{2,1,0:T(8,128)S(1)}, f32[42,8,512]{2,1,0:T(8,128)S(1)}, u32[]{:S(2)}, u32[]{:S(2)}) collective-permute-start(f32[42,8,512]{2,1,0:T(8,128)S(1)} %get-tuple-element.26), channel_id=1, source_target_pairs={{0,1},{1,2},{2,3},{3,4},{4,5},{5,6},{6,7},{7,8},{8,9},{9,10},{10,1... | collective-permute-start | bytes 2064392 | tf_op jit(solution)/shard_map/ppermute | solution.py:372
  30.3 1.9 %collective-permute-start.3 = (f32[42,8,512]{2,1,0:T(8,128)S(1)}, f32[42,8,512]{2,1,0:T(8,128)S(1)}, u32[]{:S(2)}, u32[]{:S(2)}) collective-permute-start(f32[42,8,512]{2,1,0:T(8,128)S(1)} %get-tuple-element.27), channel_id=1, source_target_pairs={{1,0},{2,1},{3,2},{4,3},{5,4},{6,5},{7,6},{8,7},{9,8},{10,9},{11,1... | collective-permute-start | bytes 2064392 | tf_op jit(solution)/shard_map/ppermute | solution.py:372
  32.2 5.9 %collective-permute-done.2.refs_4_ = f32[42,8,512]{2,1,0:T(8,128)S(1)} collective-permute-done((f32[42,8,512]{2,1,0:T(8,128)S(1)}, f32[42,8,512]{2,1,0:T(8,128)S(1)}, u32[]{:S(2)}, u32[]{:S(2)}) %collective-permute-start.2) | collective-permute-done | bytes 688160 | tf_op jit(solution)/shard_map/ppermute | solution.py:372
  38.1 5.6 %collective-permute-done.3.refs_5_ = f32[42,8,512]{2,1,0:T(8,128)S(1)} collective-permute-done((f32[42,8,512]{2,1,0:T(8,128)S(1)}, f32[42,8,512]{2,1,0:T(8,128)S(1)}, u32[]{:S(2)}, u32[]{:S(2)}) %collective-permute-start.3) | collective-permute-done | bytes 688160 | tf_op jit(solution)/shard_map/ppermute | solution.py:372
  43.7 9.6 %shard_map.52 = (f32[24,32,512]{2,1,0:T(8,128)S(1)}, f32[8,32,512]{2,1,0:T(8,128)S(1)}, f32[18,32,512]{2,1,0:T(8,128)S(1)}, f32[8,16,256]{2,1,0:T(8,128)S(1)}, f32[8,16,256]{2,1,0:T(8,128)S(1)}) custom-call(f32[13,16,512]{2,1,0:T(8,128)S(1)} %collective-permute-done.low.refs_0_, f32[13,16,512]{2,1,0:T(8,128)S(1)} %get-tuple-element.23.up.refs_1_, ...), custom_call_target="tpu_custom_call" | custom-call | tf_op jit(solution)/shard_map/pallas_call | solution.py:359
  53.3 1.9 %collective-permute-start.5 = (f32[8,16,256]{2,1,0:T(8,128)S(1)}, f32[8,16,256]{2,1,0:T(8,128)S(1)}, u32[]{:S(2)}, u32[]{:S(2)}) collective-permute-start(f32[8,16,256]{2,1,0:T(8,128)S(1)} %get-tuple-element.28.refs_2_), channel_id=1, source_target_pairs={{0,16},{16,32},{32,48},{48,64},{64,80},{80,96},{96,112},{112,128},... | collective-permute-start | bytes 393224 | tf_op jit(solution)/shard_map/ppermute | solution.py:372
  55.3 1.9 %collective-permute-start.4 = (f32[8,16,256]{2,1,0:T(8,128)S(1)}, f32[8,16,256]{2,1,0:T(8,128)S(1)}, u32[]{:S(2)}, u32[]{:S(2)}) collective-permute-start(f32[8,16,256]{2,1,0:T(8,128)S(1)} %get-tuple-element.28.refs_2_), channel_id=1, source_target_pairs={{0,32},{16,48},{32,64},{48,80},{64,96},{80,112},{96,128},{112,144}... | collective-permute-start | bytes 393224 | tf_op jit(solution)/shard_map/ppermute | solution.py:372
  57.2 6.4 %collective-permute-start.7 = (f32[8,16,256]{2,1,0:T(8,128)S(1)}, f32[8,16,256]{2,1,0:T(8,128)S(1)}, u32[]{:S(2)}, u32[]{:S(2)}) collective-permute-start(f32[8,16,256]{2,1,0:T(8,128)S(1)} %get-tuple-element.29.refs_3_), channel_id=1, source_target_pairs={{32,0},{48,16},{64,32},{80,48},{96,64},{112,80},{128,96},{144,112}... | collective-permute-start | bytes 393224 | tf_op jit(solution)/shard_map/ppermute | solution.py:372
  63.6 3.4 %collective-permute-start.6 = (f32[8,16,256]{2,1,0:T(8,128)S(1)}, f32[8,16,256]{2,1,0:T(8,128)S(1)}, u32[]{:S(2)}, u32[]{:S(2)}) collective-permute-start(f32[8,16,256]{2,1,0:T(8,128)S(1)} %get-tuple-element.29.refs_3_), channel_id=1, source_target_pairs={{16,0},{32,16},{48,32},{64,48},{80,64},{96,80},{112,96},{128,112},... | collective-permute-start | bytes 393224 | tf_op jit(solution)/shard_map/ppermute | solution.py:372
  66.9 1.2 collective-permute-done.7.refs_5_
  68.2 1.5 %collective-permute-done.6.refs_4_ = f32[8,16,256]{2,1,0:T(8,128)S(1)} collective-permute-done((f32[8,16,256]{2,1,0:T(8,128)S(1)}, f32[8,16,256]{2,1,0:T(8,128)S(1)}, u32[]{:S(2)}, u32[]{:S(2)}) %collective-permute-start.6) | collective-permute-done | bytes 131104 | tf_op jit(solution)/shard_map/ppermute | solution.py:372
  69.7 5.0 %collective-permute-start.8 = (f32[48,8,256]{2,1,0:T(8,128)S(1)}, f32[48,8,256]{2,1,0:T(8,128)S(1)}, u32[]{:S(2)}, u32[]{:S(2)}) collective-permute-start(f32[48,8,256]{2,1,0:T(8,128)S(1)} %get-tuple-element.30), channel_id=1, source_target_pairs={{0,1},{1,2},{2,3},{3,4},{4,5},{5,6},{6,7},{7,8},{8,9},{9,10},{10,1... | collective-permute-start | bytes 1179656 | tf_op jit(solution)/shard_map/ppermute | solution.py:372
  74.7 1.9 %collective-permute-start.9 = (f32[48,8,256]{2,1,0:T(8,128)S(1)}, f32[48,8,256]{2,1,0:T(8,128)S(1)}, u32[]{:S(2)}, u32[]{:S(2)}) collective-permute-start(f32[48,8,256]{2,1,0:T(8,128)S(1)} %get-tuple-element.31), channel_id=1, source_target_pairs={{1,0},{2,1},{3,2},{4,3},{5,4},{6,5},{7,6},{8,7},{9,8},{10,9},{11,1... | collective-permute-start | bytes 1179656 | tf_op jit(solution)/shard_map/ppermute | solution.py:372
  76.7 2.8 %collective-permute-done.8.refs_6_ = f32[48,8,256]{2,1,0:T(8,128)S(1)} collective-permute-done((f32[48,8,256]{2,1,0:T(8,128)S(1)}, f32[48,8,256]{2,1,0:T(8,128)S(1)}, u32[]{:S(2)}, u32[]{:S(2)}) %collective-permute-start.8) | collective-permute-done | bytes 393248 | tf_op jit(solution)/shard_map/ppermute | solution.py:372
  79.4 5.6 %collective-permute-done.9.refs_7_ = f32[48,8,256]{2,1,0:T(8,128)S(1)} collective-permute-done((f32[48,8,256]{2,1,0:T(8,128)S(1)}, f32[48,8,256]{2,1,0:T(8,128)S(1)}, u32[]{:S(2)}, u32[]{:S(2)}) %collective-permute-start.9) | collective-permute-done | bytes 393248 | tf_op jit(solution)/shard_map/ppermute | solution.py:372
  85.0 7.7 %shard_map.54 = (f32[24,32,256]{2,1,0:T(8,128)S(1)}, f32[10,32,256]{2,1,0:T(8,128)S(1)}, f32[24,32,256]{2,1,0:T(8,128)S(1)}, f32[8,16,128]{2,1,0:T(8,128)S(1)}, ...) custom-call(f32[8,16,256]{2,1,0:T(8,128)S(1)} %collective-permute-done.4.refs_0_, ...), custom_call_target="tpu_custom_call" | custom-call | tf_op jit(solution)/shard_map/pallas_call | solution.py:359
  92.8 1.9 %collective-permute-start.11 = (f32[2,16,128]{2,1,0:T(8,128)S(1)}, f32[2,16,128]{2,1,0:T(8,128)S(1)}, u32[]{:S(2)}, u32[]{:S(2)}) collective-permute-start(f32[2,16,128]{2,1,0:T(8,128)S(1)} %get-tuple-element.32), channel_id=1, source_target_pairs={{0,16},{16,32},{32,48},{48,64},{64,80},{80,96},{96,112},{112,128},... | collective-permute-start | bytes 49160 | tf_op jit(solution)/shard_map/ppermute | solution.py:372
  94.7 3.8 %collective-permute-start.10 = (f32[2,16,128]{2,1,0:T(8,128)S(1)}, f32[2,16,128]{2,1,0:T(8,128)S(1)}, u32[]{:S(2)}, u32[]{:S(2)}) collective-permute-start(f32[2,16,128]{2,1,0:T(8,128)S(1)} %get-tuple-element.32), channel_id=1, source_target_pairs={{0,32},{16,48},{32,64},{48,80},{64,96},{80,112},{96,128},{112,144}... | collective-permute-start | bytes 49160 | tf_op jit(solution)/shard_map/ppermute | solution.py:372
  98.5 5.5 %collective-permute-start.13 = (f32[2,16,128]{2,1,0:T(8,128)S(1)}, f32[2,16,128]{2,1,0:T(8,128)S(1)}, u32[]{:S(2)}, u32[]{:S(2)}) collective-permute-start(f32[2,16,128]{2,1,0:T(8,128)S(1)} %get-tuple-element.34), channel_id=1, source_target_pairs={{32,0},{48,16},{64,32},{80,48},{96,64},{112,80},{128,96},{144,112}... | collective-permute-start | bytes 49160 | tf_op jit(solution)/shard_map/ppermute | solution.py:372
  104.0 3.1 %collective-permute-start.12 = (f32[2,16,128]{2,1,0:T(8,128)S(1)}, f32[2,16,128]{2,1,0:T(8,128)S(1)}, u32[]{:S(2)}, u32[]{:S(2)}) collective-permute-start(f32[2,16,128]{2,1,0:T(8,128)S(1)} %get-tuple-element.34), channel_id=1, source_target_pairs={{16,0},{32,16},{48,32},{64,48},{80,64},{96,80},{112,96},{128,112},... | collective-permute-start | bytes 49160 | tf_op jit(solution)/shard_map/ppermute | solution.py:372
  107.1 1.4 %collective-permute-done.12.refs_3_ = f32[2,16,128]{2,1,0:T(8,128)S(1)} collective-permute-done((f32[2,16,128]{2,1,0:T(8,128)S(1)}, f32[2,16,128]{2,1,0:T(8,128)S(1)}, u32[]{:S(2)}, u32[]{:S(2)}) %collective-permute-start.12) | collective-permute-done | bytes 16416 | tf_op jit(solution)/shard_map/ppermute | solution.py:372
  108.5 3.5 %collective-permute-start.14 = (f32[16,8,128]{2,1,0:T(8,128)S(1)}, f32[16,8,128]{2,1,0:T(8,128)S(1)}, u32[]{:S(2)}, u32[]{:S(2)}) collective-permute-start(f32[16,8,128]{2,1,0:T(8,128)S(1)} %get-tuple-element.35), channel_id=1, source_target_pairs={{0,1},{1,2},{2,3},{3,4},{4,5},{5,6},{6,7},{7,8},{8,9},{9,10},{10,1... | collective-permute-start | bytes 196616 | tf_op jit(solution)/shard_map/ppermute | solution.py:372
  112.0 1.9 %collective-permute-start.15 = (f32[16,8,128]{2,1,0:T(8,128)S(1)}, f32[16,8,128]{2,1,0:T(8,128)S(1)}, u32[]{:S(2)}, u32[]{:S(2)}) collective-permute-start(f32[16,8,128]{2,1,0:T(8,128)S(1)} %get-tuple-element.36), channel_id=1, source_target_pairs={{1,0},{2,1},{3,2},{4,3},{5,4},{6,5},{7,6},{8,7},{9,8},{10,9},{11,1... | collective-permute-start | bytes 196616 | tf_op jit(solution)/shard_map/ppermute | solution.py:372
  113.9 4.9 %collective-permute-done.15.refs_6_ = f32[16,8,128]{2,1,0:T(8,128)S(1)} collective-permute-done((f32[16,8,128]{2,1,0:T(8,128)S(1)}, f32[16,8,128]{2,1,0:T(8,128)S(1)}, u32[]{:S(2)}, u32[]{:S(2)}) %collective-permute-start.15) | collective-permute-done | bytes 65568 | tf_op jit(solution)/shard_map/ppermute | solution.py:372
  118.8 16.5 %shard_map.56 = (f32[8,16,512]{2,1,0:T(8,128)}, f32[8,16,512]{2,1,0:T(8,128)}) custom-call(f32[2,16,128]{2,1,0:T(8,128)S(1)} %collective-permute-done.10.refs_0_, f32[2,16,128]{2,1,0:T(8,128)S(1)} %collective-permute-done.11.refs_1_, f32[8,16,128]{2,1,0:T(8,128)S(1)} %get-tuple-element.33.refs_2_, f32[2,16,128]{2,1,0:T(8,128)S(1)} %collective-permute-done.12.refs_3_, ...), custom_call_target="tpu_custom_call" | custom-call | tf_op jit(solution)/shard_map/pallas_call | solution.py:359
  (13 shorter events, 0.5 us)
Async XLA Ops:
  0.6 1.0 copy-start
  1.6 0.9 copy-start.1
  2.5 0.7 copy-start.2
  3.5 13.8 %collective-permute-start.1 = (f32[13,16,512]{2,1,0:T(8,128)S(1)}, f32[13,16,512]{2,1,0:T(8,128)S(1)}, u32[]{:S(2)}, u32[]{:S(2)}) collective-permute-start(f32[13,16,512]{2,1,0:T(8,128)S(1)} %get-tuple-element.25), channel_id=1, source_target_pairs={{16,0},{32,16},{48,32},{64,48},{80,64},{96,80},{112,96},{128,112},... | collective-permute-start | bytes 1277960 | tf_op jit(solution)/shard_map/ppermute | solution.py:372
  8.8 14.4 %collective-permute-start = (f32[13,16,512]{2,1,0:T(8,128)S(1)}, f32[13,16,512]{2,1,0:T(8,128)S(1)}, u32[]{:S(2)}, u32[]{:S(2)}) collective-permute-start(f32[13,16,512]{2,1,0:T(8,128)S(1)} %get-tuple-element.23.up.refs_1_), channel_id=1, source_target_pairs={{0,16},{16,32},{32,48},{48,64},{64,80},{80,96},{96,112},{112,128},... | collective-permute-start | bytes 1277960 | tf_op jit(solution)/shard_map/ppermute | solution.py:372
  23.3 14.8 %collective-permute-start.2 = (f32[42,8,512]{2,1,0:T(8,128)S(1)}, f32[42,8,512]{2,1,0:T(8,128)S(1)}, u32[]{:S(2)}, u32[]{:S(2)}) collective-permute-start(f32[42,8,512]{2,1,0:T(8,128)S(1)} %get-tuple-element.26), channel_id=1, source_target_pairs={{0,1},{1,2},{2,3},{3,4},{4,5},{5,6},{6,7},{7,8},{8,9},{9,10},{10,1... | collective-permute-start | bytes 2064392 | tf_op jit(solution)/shard_map/ppermute | solution.py:372
  30.3 13.5 %collective-permute-start.3 = (f32[42,8,512]{2,1,0:T(8,128)S(1)}, f32[42,8,512]{2,1,0:T(8,128)S(1)}, u32[]{:S(2)}, u32[]{:S(2)}) collective-permute-start(f32[42,8,512]{2,1,0:T(8,128)S(1)} %get-tuple-element.27), channel_id=1, source_target_pairs={{1,0},{2,1},{3,2},{4,3},{5,4},{6,5},{7,6},{8,7},{9,8},{10,9},{11,1... | collective-permute-start | bytes 2064392 | tf_op jit(solution)/shard_map/ppermute | solution.py:372
  53.3 13.6 %collective-permute-start.5 = (f32[8,16,256]{2,1,0:T(8,128)S(1)}, f32[8,16,256]{2,1,0:T(8,128)S(1)}, u32[]{:S(2)}, u32[]{:S(2)}) collective-permute-start(f32[8,16,256]{2,1,0:T(8,128)S(1)} %get-tuple-element.28.refs_2_), channel_id=1, source_target_pairs={{0,16},{16,32},{32,48},{48,64},{64,80},{80,96},{96,112},{112,128},... | collective-permute-start | bytes 393224 | tf_op jit(solution)/shard_map/ppermute | solution.py:372
  55.3 11.7 %collective-permute-start.4 = (f32[8,16,256]{2,1,0:T(8,128)S(1)}, f32[8,16,256]{2,1,0:T(8,128)S(1)}, u32[]{:S(2)}, u32[]{:S(2)}) collective-permute-start(f32[8,16,256]{2,1,0:T(8,128)S(1)} %get-tuple-element.28.refs_2_), channel_id=1, source_target_pairs={{0,32},{16,48},{32,64},{48,80},{64,96},{80,112},{96,128},{112,144}... | collective-permute-start | bytes 393224 | tf_op jit(solution)/shard_map/ppermute | solution.py:372
  57.2 11.0 %collective-permute-start.7 = (f32[8,16,256]{2,1,0:T(8,128)S(1)}, f32[8,16,256]{2,1,0:T(8,128)S(1)}, u32[]{:S(2)}, u32[]{:S(2)}) collective-permute-start(f32[8,16,256]{2,1,0:T(8,128)S(1)} %get-tuple-element.29.refs_3_), channel_id=1, source_target_pairs={{32,0},{48,16},{64,32},{80,48},{96,64},{112,80},{128,96},{144,112}... | collective-permute-start | bytes 393224 | tf_op jit(solution)/shard_map/ppermute | solution.py:372
  63.6 6.1 %collective-permute-start.6 = (f32[8,16,256]{2,1,0:T(8,128)S(1)}, f32[8,16,256]{2,1,0:T(8,128)S(1)}, u32[]{:S(2)}, u32[]{:S(2)}) collective-permute-start(f32[8,16,256]{2,1,0:T(8,128)S(1)} %get-tuple-element.29.refs_3_), channel_id=1, source_target_pairs={{16,0},{32,16},{48,32},{64,48},{80,64},{96,80},{112,96},{128,112},... | collective-permute-start | bytes 393224 | tf_op jit(solution)/shard_map/ppermute | solution.py:372
  69.7 9.7 %collective-permute-start.8 = (f32[48,8,256]{2,1,0:T(8,128)S(1)}, f32[48,8,256]{2,1,0:T(8,128)S(1)}, u32[]{:S(2)}, u32[]{:S(2)}) collective-permute-start(f32[48,8,256]{2,1,0:T(8,128)S(1)} %get-tuple-element.30), channel_id=1, source_target_pairs={{0,1},{1,2},{2,3},{3,4},{4,5},{5,6},{6,7},{7,8},{8,9},{9,10},{10,1... | collective-permute-start | bytes 1179656 | tf_op jit(solution)/shard_map/ppermute | solution.py:372
  74.7 10.3 %collective-permute-start.9 = (f32[48,8,256]{2,1,0:T(8,128)S(1)}, f32[48,8,256]{2,1,0:T(8,128)S(1)}, u32[]{:S(2)}, u32[]{:S(2)}) collective-permute-start(f32[48,8,256]{2,1,0:T(8,128)S(1)} %get-tuple-element.31), channel_id=1, source_target_pairs={{1,0},{2,1},{3,2},{4,3},{5,4},{6,5},{7,6},{8,7},{9,8},{10,9},{11,1... | collective-permute-start | bytes 1179656 | tf_op jit(solution)/shard_map/ppermute | solution.py:372
  92.8 14.4 %collective-permute-start.11 = (f32[2,16,128]{2,1,0:T(8,128)S(1)}, f32[2,16,128]{2,1,0:T(8,128)S(1)}, u32[]{:S(2)}, u32[]{:S(2)}) collective-permute-start(f32[2,16,128]{2,1,0:T(8,128)S(1)} %get-tuple-element.32), channel_id=1, source_target_pairs={{0,16},{16,32},{32,48},{48,64},{64,80},{80,96},{96,112},{112,128},... | collective-permute-start | bytes 49160 | tf_op jit(solution)/shard_map/ppermute | solution.py:372
  94.7 12.4 %collective-permute-start.10 = (f32[2,16,128]{2,1,0:T(8,128)S(1)}, f32[2,16,128]{2,1,0:T(8,128)S(1)}, u32[]{:S(2)}, u32[]{:S(2)}) collective-permute-start(f32[2,16,128]{2,1,0:T(8,128)S(1)} %get-tuple-element.32), channel_id=1, source_target_pairs={{0,32},{16,48},{32,64},{48,80},{64,96},{80,112},{96,128},{112,144}... | collective-permute-start | bytes 49160 | tf_op jit(solution)/shard_map/ppermute | solution.py:372
  98.5 8.7 %collective-permute-start.13 = (f32[2,16,128]{2,1,0:T(8,128)S(1)}, f32[2,16,128]{2,1,0:T(8,128)S(1)}, u32[]{:S(2)}, u32[]{:S(2)}) collective-permute-start(f32[2,16,128]{2,1,0:T(8,128)S(1)} %get-tuple-element.34), channel_id=1, source_target_pairs={{32,0},{48,16},{64,32},{80,48},{96,64},{112,80},{128,96},{144,112}... | collective-permute-start | bytes 49160 | tf_op jit(solution)/shard_map/ppermute | solution.py:372
  104.0 4.5 %collective-permute-start.12 = (f32[2,16,128]{2,1,0:T(8,128)S(1)}, f32[2,16,128]{2,1,0:T(8,128)S(1)}, u32[]{:S(2)}, u32[]{:S(2)}) collective-permute-start(f32[2,16,128]{2,1,0:T(8,128)S(1)} %get-tuple-element.34), channel_id=1, source_target_pairs={{16,0},{32,16},{48,32},{64,48},{80,64},{96,80},{112,96},{128,112},... | collective-permute-start | bytes 49160 | tf_op jit(solution)/shard_map/ppermute | solution.py:372
  108.5 5.4 %collective-permute-start.14 = (f32[16,8,128]{2,1,0:T(8,128)S(1)}, f32[16,8,128]{2,1,0:T(8,128)S(1)}, u32[]{:S(2)}, u32[]{:S(2)}) collective-permute-start(f32[16,8,128]{2,1,0:T(8,128)S(1)} %get-tuple-element.35), channel_id=1, source_target_pairs={{0,1},{1,2},{2,3},{3,4},{4,5},{5,6},{6,7},{7,8},{8,9},{9,10},{10,1... | collective-permute-start | bytes 196616 | tf_op jit(solution)/shard_map/ppermute | solution.py:372
  112.0 6.8 %collective-permute-start.15 = (f32[16,8,128]{2,1,0:T(8,128)S(1)}, f32[16,8,128]{2,1,0:T(8,128)S(1)}, u32[]{:S(2)}, u32[]{:S(2)}) collective-permute-start(f32[16,8,128]{2,1,0:T(8,128)S(1)} %get-tuple-element.36), channel_id=1, source_target_pairs={{1,0},{2,1},{3,2},{4,3},{5,4},{6,5},{7,6},{8,7},{9,8},{10,9},{11,1... | collective-permute-start | bytes 196616 | tf_op jit(solution)/shard_map/ppermute | solution.py:372

commit v2 on v0

v2 whole, which is shorter than its diff:
```python
import jax
import jax.numpy as jnp
from jax import lax
from jax.experimental import pallas as pl
from jax.experimental.pallas import tpu as pltpu
from jax.sharding import PartitionSpec as P


DEGREE = 4
THETA = 1.15
DELTA = 0.85
FIRST = 1.0 / (6.0 * THETA)
LEAST = 0.05
F32 = jnp.float32
LANES = 128


def coefficients():
    sigma = THETA / DELTA
    rho = 1.0 / sigma
    pairs = []
    for turn in range(DEGREE - 1):
        rho_next = 1.0 / (2.0 * sigma - rho)
        pairs.append((rho_next * rho, 2.0 * rho_next / (6.0 * DELTA)))
        rho = rho_next
    return pairs


COEFFICIENTS = coefficients()


def iota(shape, dim):
    return lax.broadcasted_iota(jnp.int32, shape, dim)


def row_masks(n, base, count):
    masks = []
    for x in range(n):
        place = n * iota((8, LANES), 0) + (x + base)
        masks.append(jnp.where((place >= 0) & (place < count), 1.0, 0.0).astype(F32))
    return masks


def z_mask(base, count):
    def scaled(z, value):
        place = z + base
        return jnp.where((place >= 0) & (place < count), F32(value), F32(0.0))

    return scaled


def loop(low, high, body, width=2):
    turns = (high - low) // width

    def step(t, carry):
        for j in range(width):
            body(low + width * t + j)
        return carry

    if turns > 0:
        lax.fori_loop(0, turns, step, 0)
    for z in range(low + turns * width, high):
        body(z)


def around(ref, z, n):
    count = ref.shape[1]
    blocks = count // n
    here = [ref[z, i] for i in range(count)]
    lane = iota((8, LANES), 1)
    before = [jnp.where(lane == 0, 0.0, pltpu.roll(here[(blocks - 1) * n + x], 1, 1)) for x in range(n)]
    after = [jnp.where(lane == LANES - 1, 0.0, pltpu.roll(here[x], LANES - 1, 1)) for x in range(n)]
    total = []
    for k in range(blocks):
        row = here[k * n : k * n + n]
        up = pltpu.roll(row[n - 1], 1, 0)
        down = pltpu.roll(row[0], 7, 0)
        for x in range(n):
            i = k * n + x
            left = here[i - n] if k > 0 else before[x]
            right = here[i + n] if k + 1 < blocks else after[x]
            north = row[x - 1] if x > 0 else up
            south = row[x + 1] if x + 1 < n else down
            total.append(((left + right) + (north + south)) + (ref[z - 1, i] + ref[z + 1, i]))
    return here, total


def applied(ref, z, n, q):
    here, total = around(ref, z, n)
    return here, [q[z, i] - (6.0 * here[i] - total[i]) for i in range(len(here))]


def smooth(w, q, low, high, n, masks, z_scale, passes, finish=None):
    for turn in range(passes):

        def advance(z, turn=turn):
            here, rest = applied(w[turn], z, n, q)
            if finish is not None and turn == DEGREE - 1:
                finish(z, rest)
                return
            if turn < passes - 1 or passes == DEGREE:
                for i, value in enumerate(rest):
                    q[z, i] = value
            if turn < DEGREE - 1:
                c1, c2 = COEFFICIENTS[turn]
                scales = [z_scale(z, c2) * mask for mask in masks]
                for i, value in enumerate(rest):
                    w[turn + 1][z, i] = c1 * here[i] + scales[i % n] * value

        loop(low + 1 + turn, high - 1 - turn, advance)


def weave(source, z, k, blocks, n, x):
    return source[z * blocks + k, pl.ds(x, 8, n), :]


def exact_product(left, right):
    high = left.astype(jnp.bfloat16)
    rest = left - high.astype(F32)
    middle = rest.astype(jnp.bfloat16)
    low = (rest - middle.astype(F32)).astype(jnp.bfloat16)
    parts = [jnp.dot(part, right, preferred_element_type=F32) for part in (high, middle, low)]
    return (parts[2] + parts[1]) + parts[0]


def weave_matrix(dim):
    plain, woven = iota((512, 512), dim), iota((512, 512), 1 - dim)
    same = plain == 4 * (woven & (LANES - 1)) + (woven >> 7)
    return jnp.where(same, 1.0, 0.0).astype(jnp.bfloat16)


def scale_kernel(load_hbm, density_hbm, void_hbm, up, down, root, both, void, sems):
    copies = [
        pltpu.make_async_copy(load_hbm, both.at[pl.ds(0, 8)], sems.at[0]),
        pltpu.make_async_copy(density_hbm, both.at[pl.ds(8, 8)], sems.at[1]),
        pltpu.make_async_copy(void_hbm, void, sems.at[2]),
    ]
    for copy in copies:
        copy.start()
    matrix = weave_matrix(0)
    copies[2].wait()
    bricks = jnp.where(void[0] == 1, 1.0, 0.0).astype(F32)
    bricks = jnp.concatenate([jnp.broadcast_to(bricks[k : k + 1], (8, 64)) for k in range(2)], axis=0)
    spread = jnp.where((iota((64, LANES), 1) >> 1) == iota((64, LANES), 0), 1.0, 0.0).astype(jnp.bfloat16)
    voids = jnp.dot(bricks.astype(jnp.bfloat16), spread, preferred_element_type=F32)
    copies[0].wait()
    copies[1].wait()
    fields = exact_product(both[...].reshape(256, 512), matrix)
    for z in range(8):
        for k in range(4):
            b = fields[16 * z : 16 * z + 16, LANES * k : LANES * k + LANES]
            d = fields[128 + 16 * z : 144 + 16 * z, LANES * k : LANES * k + LANES]
            r = jnp.sqrt(jnp.where(voids > 0.5, 0.01, 0.01 + 0.99 * d * d * d))
            q = b / r
            up[4 * z + k] = q
            down[4 * z + k] = q
            root[4 * z + k] = r
            if z >= 3:
                up[4 * (5 + z) + k] = r
            if z < 5:
                down[4 * (8 + z) + k] = r


def fine_pack_kernel(low, up, root, high, left, right):
    at = 0
    for ref in (low, up, high):
        for i in range(32):
            left[at : at + 8] = ref[i, 0:8]
            right[at : at + 8] = ref[i, 8:16]
            at += 8
    for ref, first, count in ((low, 36, 16), (root, 0, 32), (high, 32, 16)):
        for i in range(first, first + count):
            left[at : at + 5] = ref[i, 0:5]
            right[at : at + 5] = ref[i, 11:16]
            at += 5


def fine_pre_kernel(counts, low, up, root, high, left, right, q, y, r, mid_q, mid_r, low1, high1, low2, high2, *scratch):
    natural, w = scratch[0], scratch[1:5]
    gz, xy = lax.axis_index("gz"), lax.axis_index("xy")
    masks = row_masks(4, 16 * xy - 8, 16 * counts[1])
    z_scale = z_mask(8 * gz - 8, 8 * counts[0])

    for n, ref in enumerate((low, up, high)):
        for i in range(32):
            j = 32 * n + i
            natural[j, 0:8] = left[8 * j : 8 * j + 8]
            natural[j, 8:24] = ref[i]
            natural[j, 24:32] = right[8 * j : 8 * j + 8]

    def begin(z):
        for k in range(4):
            for x in range(4):
                value = weave(natural, z, k, 4, 4, x)
                q[z, 4 * k + x] = value
                w[0][z, 4 * k + x] = FIRST * value

    loop(0, 24, begin)

    place = 0
    for ref, first, count in ((low, 32, 20), (root, 0, 32), (high, 32, 20)):
        for i in range(first, first + count):
            natural[place, 0:8] = jnp.zeros((8, LANES), F32)
            natural[place, 8:24] = ref[i]
            natural[place, 24:32] = jnp.zeros((8, LANES), F32)
            if 4 <= place < 68:
                j = 768 + 5 * (place - 4)
                natural[place, 3:8] = left[j : j + 5]
                natural[place, 24:29] = right[j : j + 5]
            place += 1

    def roots(z):
        for k in range(4):
            for x in range(4):
                r[z, 4 * k + x] = weave(natural, z, k, 4, 4, x)

    loop(0, 18, roots)
    smooth(w, q, 0, 24, 4, masks, z_scale, DEGREE)

    def total(z):
        for i in range(16):
            y[z, i] = (w[0][z + 8, i] + w[1][z + 8, i]) + (w[2][z + 8, i] + w[3][z + 8, i])

    loop(0, 8, total)

    def fold(m):
        for k in range(2):
            for x in range(2):
                sums, roots = None, None
                for z in range(2):
                    for i in (8 * k + 2 * x, 8 * k + 2 * x + 1, 8 * k + 2 * x + 4, 8 * k + 2 * x + 5):
                        a = r[2 * m + 1 + z, i]
                        b = a * q[2 * m + 4 + z, i]
                        sums = b if sums is None else sums + b
                        roots = a if roots is None else roots + a
                roots = 0.125 * roots
                mid_r[2 * m + k, pl.ds(x, 8, 2), :] = roots
                mid_q[2 * m + k, pl.ds(x, 8, 2), :] = 0.5 * sums / jnp.maximum(roots, LEAST)

    loop(0, 8, fold)
    for i in range(8):
        for near, far, first in ((low1, low2, 0), (high1, high2, 8)):
            values = mid_q[first + i, 2:14]
            near[12 * i : 12 * i + 12] = values
            far[12 * i : 12 * i + 12] = values
            values = mid_r[first + i, 2:14]
            near[96 + 12 * i : 108 + 12 * i] = values
            j = i - 4 if first == 0 else i
            if 0 <= j < 4:
                far[96 + 12 * j : 108 + 12 * j] = values


def mid_parts(refs):
    low2, low1, mid_q, mid_r, high1, high2 = refs

    def rows(field, z, k):
        if 8 <= z < 16:
            return (mid_q, mid_r)[field][2 * (z - 8) + k, 2:14]
        ref, z = [(low2, z), (low1, z - 4), None, None, (high1, z - 16), (high2, z - 20)][z // 4]
        if field == 1 and ref is low2:
            z = z - 2
        at = 96 * field + 12 * (2 * z + k)
        return ref[at : at + 12]

    return rows


def mid_pack_kernel(*refs):
    rows, left, right = mid_parts(refs[:6]), refs[6], refs[7]
    at = 0
    for z in range(24):
        for k in range(2):
            value = rows(0, z, k)
            right[at : at + 8] = value[0:8]
            left[at : at + 8] = value[4:12]
            at += 8
    for z in range(2, 22):
        for k in range(2):
            value = rows(1, z, k)
            right[at : at + 6] = value[2:8]
            left[at : at + 6] = value[4:10]
            at += 6


def mid_pre_kernel(counts, *refs):
    rows, (left, right), refs = mid_parts(refs[:6]), refs[6:8], refs[8:]
    q, y, r, coarse, coarse_low, coarse_high, coarse_root, natural = refs[:8]
    w = refs[8:]
    gz, xy = lax.axis_index("gz"), lax.axis_index("xy")
    masks = row_masks(4, 8 * xy - 10, 8 * counts[1])
    z_scale = z_mask(4 * gz - 10, 4 * counts[0])
    for z in range(24):
        for k in range(2):
            i = 2 * z + k
            natural[i, 0:8] = left[8 * i : 8 * i + 8]
            natural[i, 8:20] = rows(0, z, k)
            natural[i, 20:28] = right[8 * i : 8 * i + 8]
            natural[i, 28:32] = jnp.zeros((4, LANES), F32)

    def begin(z):
        for k in range(2):
            for x in range(4):
                value = weave(natural, z, k, 2, 4, x)
                q[z, 4 * k + x] = value
                w[0][z, 4 * k + x] = FIRST * value

    loop(0, 24, begin)
    for z in range(20):
        for k in range(2):
            i = 2 * z + k
            natural[i, 0:8] = jnp.zeros((8, LANES), F32)
            natural[i, 24:32] = jnp.zeros((8, LANES), F32)
            natural[i, 2:8] = left[384 + 6 * i : 390 + 6 * i]
            natural[i, 8:20] = rows(1, z + 2, k)
            natural[i, 20:26] = right[384 + 6 * i : 390 + 6 * i]

    def roots(z):
        for k in range(2):
            for x in range(4):
                r[z, 4 * k + x] = weave(natural, z, k, 2, 4, x)

    loop(0, 20, roots)
    smooth(w, q, 0, 24, 4, masks, z_scale, DEGREE)

    def total(z):
        for i in range(8):
            y[z, i] = (w[0][z + 7, i] + w[1][z + 7, i]) + (w[2][z + 7, i] + w[3][z + 7, i])

    loop(0, 10, total)

    for m in range(10):
        for x in range(2):
            sums, mean = None, None
            for z in range(2):
                for i in (2 * x, 2 * x + 1, 2 * x + 4, 2 * x + 5):
                    a = r[2 * m + z, i]
                    b = a * q[2 * m + 2 + z, i]
                    sums = b if sums is None else sums + b
                    mean = a if mean is None else mean + a
            mean = 0.125 * mean
            coarse_root[m, pl.ds(x, 8, 2), :] = mean
            if 0 < m < 9:
                coarse[m - 1, pl.ds(x, 8, 2), :] = 0.5 * sums / jnp.maximum(mean, LEAST)
    for m in range(2):
        coarse_low[m] = coarse[m]
        coarse_high[m] = coarse[6 + m]


def coarse_pack_kernel(*refs):
    parts, left, right = refs[:5], refs[5], refs[6]
    at = 0
    for ref in parts:
        for k in range(ref.shape[0]):
            right[at + k] = ref[k, 0:8]
            left[at + k] = ref[k, 8:16]
        at += ref.shape[0]


def finish_kernel(counts, *refs):
    parts, (left, right), refs = refs[:5], refs[5:7], refs[7:]
    coarse_root, mid_q, mid_y, mid_r, fine_q, fine_y, fine_r, out_x, out_r = refs[:9]
    natural, cq, error, spread, mq, mt, fq, ft, plain_x, plain_r, rows_x, rows_r = refs[9:21]
    cw, mw, fw = refs[21:25], refs[25:29], refs[29:33]
    gz, xy = lax.axis_index("gz"), lax.axis_index("xy")

    at = 0
    for ref in parts:
        for k in range(ref.shape[0]):
            natural[at, 0:4] = left[at, 2:6]
            natural[at, 4:14] = ref[k, 2:12]
            natural[at, 14:18] = right[at, 0:4]
            natural[at, 18:24] = jnp.zeros((6, LANES), F32)
            for x in range(3):
                value = weave(natural, at, 0, 1, 3, x)
                cq[at, x] = value
                cw[0][at, x] = FIRST * value
            at += 1
    masks = row_masks(3, 4 * xy - 7, 4 * counts[1])
    smooth(cw, cq, 0, 16, 3, masks, z_mask(2 * gz - 7, 2 * counts[0]), DEGREE - 1)
    for k in range(10):
        for x in range(3):
            total = (cw[0][k + 3, x] + cw[1][k + 3, x]) + (cw[2][k + 3, x] + cw[3][k + 3, x])
            natural[k, pl.ds(x, 8, 3), :] = total
        error[k] = natural[k, 2:18] / jnp.maximum(coarse_root[k], LEAST)

    for k in range(10):
        for x in range(4):
            value = error[k, pl.ds(x >> 1, 8, 2), :]
            for i in (x, 4 + x):
                mt[2 * k + 2, i] = mid_r[2 * k, i] * value
                mt[2 * k + 3, i] = mid_r[2 * k + 1, i] * value

    masks = row_masks(4, 8 * xy - 10, 8 * counts[1])
    z_scale = z_mask(4 * gz - 10, 4 * counts[0])

    def mid_correct(z):
        _, rest = applied(mt, z, 4, mid_q)
        scales = [z_scale(z, FIRST) * mask for mask in masks]
        for i, value in enumerate(rest):
            mq[z, i] = value
            mw[0][z, i] = scales[i % 4] * value

    loop(4, 20, mid_correct)
    smooth(mw, mq, 4, 20, 4, masks, z_scale, DEGREE - 1)

    def mid_error(z):
        for k in range(2):
            for x in range(4):
                i = 4 * k + x
                total = (mw[0][z, i] + mw[1][z, i]) + (mw[2][z, i] + mw[3][z, i])
                total = total + (mid_y[z - 7, i] + mt[z, i])
                spread[2 * (z - 7) + k, pl.ds(x, 8, 4), :] = total / jnp.maximum(mid_r[z - 2, i], LEAST)

    loop(7, 17, mid_error)

    def fine_prolong(k):
        for j in range(2):
            for x in range(4):
                value = spread[2 * k + j, pl.ds(6 + (x >> 1), 8, 2), :]
                for i in (8 * j + x, 8 * j + 4 + x):
                    ft[2 * k + 2, i] = fine_r[jnp.maximum(2 * k - 1, 0), i] * value
                    ft[2 * k + 3, i] = fine_r[jnp.minimum(2 * k, 17), i] * value

    loop(0, 10, fine_prolong, 1)
    masks = row_masks(4, 16 * xy - 8, 16 * counts[1])
    z_scale = z_mask(8 * gz - 8, 8 * counts[0])

    def fine_correct(z):
        _, rest = applied(ft, z, 4, fine_q)
        scales = [z_scale(z, FIRST) * mask for mask in masks]
        for i, value in enumerate(rest):
            fq[z, i] = value
            fw[0][z, i] = scales[i % 4] * value

    loop(4, 20, fine_correct)

    def finish(z, rest):
        for k in range(4):
            for x in range(4):
                i = 4 * k + x
                r = fine_r[z - 3, i]
                total = (fw[0][z, i] + fw[1][z, i]) + (fw[2][z, i] + fw[3][z, i])
                total = total + (fine_y[z - 8, i] + ft[z, i])
                plain_x[4 * (z - 8) + k, pl.ds(x, 8, 4), :] = total / r
                plain_r[4 * (z - 8) + k, pl.ds(x, 8, 4), :] = r * rest[i]

    smooth(fw, fq, 4, 20, 4, masks, z_scale, DEGREE, finish)
    matrix = weave_matrix(1)
    for plain, rows, out in ((plain_x, rows_x, out_x), (plain_r, rows_r, out_r)):
        for z in range(8):
            for k in range(4):
                rows[16 * z : 16 * z + 16, LANES * k : LANES * k + LANES] = plain[4 * z + k, 8:24]
        out[...] = exact_product(rows[...], matrix).reshape(8, 16, 512)


def call(kernel, operands, out_shapes, scratch=(), space=pltpu.VMEM):
    whole = pl.BlockSpec(memory_space=pltpu.VMEM)
    return pl.pallas_call(
        kernel,
        out_shape=[jax.ShapeDtypeStruct(s, F32) for s in out_shapes],
        in_specs=[pl.BlockSpec(memory_space=space)] * len(operands),
        out_specs=[whole] * len(out_shapes),
        scratch_shapes=[pltpu.VMEM(s, F32) if isinstance(s, tuple) else s for s in scratch],
        compiler_params=pltpu.CompilerParams(vmem_limit_bytes=30 * 1024 * 1024),
    )(*operands)


def send(block, axis, shift):
    count = lax.axis_size(axis)
    pairs = [(i, i + shift) for i in range(count) if 0 <= i + shift < count]
    return lax.ppermute(block, axis, pairs)


def with_counts(kernel):
    counts = (lax.axis_size("gz"), lax.axis_size("xy"))
    return lambda *refs: kernel(counts, *refs)


def on_device(load_field, density, void_mask):
    up, down, root = call(
        scale_kernel,
        (load_field, density, void_mask),
        [(52, 16, LANES), (52, 16, LANES), (32, 16, LANES)],
        [(16, 16, 512), pltpu.VMEM((1, 2, 64), jnp.int32), pltpu.SemaphoreType.DMA((3,))],
        pl.ANY,
    )
    low, high = send(up, "gz", 1), send(down, "gz", -1)
    to_left, to_right = call(fine_pack_kernel, (low, up, root, high), [(1088, LANES)] * 2)
    left, right = send(to_right, "xy", 1), send(to_left, "xy", -1)
    fine = (24, 16, 8, LANES)
    fine_q, fine_y, fine_r, mid_q, mid_r, low1, high1, low2, high2 = call(
        with_counts(fine_pre_kernel),
        (low, up, root, high, left, right),
        [fine, (8, 16, 8, LANES), (18, 16, 8, LANES)] + [(16, 16, LANES)] * 2 + [(192, LANES)] * 2 + [(144, LANES)] * 2,
        [(96, 32, LANES)] + [fine] * 4,
    )
    a1, b1 = send(low1, "gz", 1), send(high1, "gz", -1)
    a2, b2 = send(low2, "gz", 2), send(high2, "gz", -2)
    parts = (a2, a1, mid_q, mid_r, b1, b2)
    to_left, to_right = call(mid_pack_kernel, parts, [(624, LANES)] * 2)
    left, right = send(to_right, "xy", 1), send(to_left, "xy", -1)
    mid = (24, 8, 8, LANES)
    mid_q, mid_y, mid_r, coarse, coarse_low, coarse_high, coarse_root = call(
        with_counts(mid_pre_kernel),
        parts + (left, right),
        [mid, (10, 8, 8, LANES), (20, 8, 8, LANES), (8, 16, LANES)] + [(2, 16, LANES)] * 2 + [(10, 16, LANES)],
        [(48, 32, LANES)] + [mid] * 4,
    )
    a1, b1 = send(coarse_low, "gz", 1), send(coarse_high, "gz", -1)
    a2, b2 = send(coarse_low, "gz", 2), send(coarse_high, "gz", -2)
    parts = (a2, a1, coarse, b1, b2)
    to_left, to_right = call(coarse_pack_kernel, parts, [(16, 8, LANES)] * 2)
    left, right = send(to_right, "xy", 1), send(to_left, "xy", -1)
    coarsest = (16, 3, 8, LANES)
    return tuple(
        call(
            with_counts(finish_kernel),
            parts + (left, right, coarse_root, mid_q, mid_y, mid_r, fine_q, fine_y, fine_r),
            [(8, 16, 512), (8, 16, 512)],
            [(16, 24, LANES), coarsest, (10, 16, LANES), (20, 32, LANES), mid, mid, fine, fine]
            + [(32, 32, LANES)] * 2
            + [(128, 512)] * 2
            + [coarsest] * 4
            + [mid] * 4
            + [fine] * 4,
        )
    )


def solution(mesh):
    specs = (P("gz", "xy", None), P("gz", "xy", None), P("gz", "xy", None))
    return jax.shard_map(
        on_device, mesh=mesh, in_specs=specs, out_specs=specs[:2], check_vma=False
    )
```

time: 438 us -> 117 us (0.27)
  starting transfers between devices: 213 us -> 54.7 us
  waiting for transfers between devices: 145 us -> 40 us
  local copies, waits for them, and re-layouts: 46.2 us -> 2.57 us
  other arithmetic: 28.2 us -> 0 us
  Pallas kernels: 0 us -> 18.5 us
    ppermute x80 -> x16, starting transfers between devices: 213 us -> 54.7 us  [send(): return lax.ppermute(block, axis, pairs)]
    ppermute x80 -> x16, waiting for transfers between devices: 145 us -> 40 us  [send(): return lax.ppermute(block, axis, pairs)]
    reshape x8 -> x0, local copies, waits for them, and re-layouts: 41.4 us -> none  [the longest x3 38.3 us: blocks(): return field.reshape(a // 2, 2, b // 2, 2, c // 2, 2).sum(axis=(1, 3, 5))]
    pallas_call x0 -> x7, Pallas kernels: none -> 18.5 us  [call(): pl.pallas_call(kernel, out_shape=[jax.ShapeDtypeStruct(s, F32) for s in o...]
    reduce_sum x4 -> x0, other arithmetic: 14.4 us -> none  [blocks(): return field.reshape(a // 2, 2, b // 2, 2, c // 2, 2).sum(axis=(1, 3, 5))]
    mul x21 -> x0, other arithmetic: 5.8 us -> none  [the longest x20 5.16 us: operate(): weighted = root * field]
    concatenate x40 -> x0, other arithmetic: 4.88 us -> none  [with_halo(): jnp.concatenate([lax.ppermute(tail, axis, [(i, (i + 1) % count) for i in...]
  transfers between devices with their start and end apart: 80 -> 16, of which waited for: 39 -> 10; matrix products, arithmetic and copies ran while one was open for 6% -> 0% of each run, Pallas kernels for 0% -> 0%
where the time goes in v2:
time: 117 us
  starting transfers between devices  54.7 us (47%)
  waiting for transfers between devices  40 us (34%)
  Pallas kernels  18.5 us (16%)
  local copies, waits for them, and re-layouts  2.57 us (2%)
    ppermute x16, starting transfers between devices, send(): return lax.ppermute(block, axis, pairs)  54.7 us
    ppermute x16, waiting for transfers between devices, send(): return lax.ppermute(block, axis, pairs)  40 us
    pallas_call x7, Pallas kernels, call(): pl.pallas_call(kernel, out_shape=[jax.ShapeDtypeStruct(s, F32) for s in o...  18.5 us
    unnamed x6, local copies, waits for them, and re-layouts  2.57 us
  transfers between devices with their start and end apart: 16, of which 10 were waited for; matrix products, arithmetic and copies ran while one was open for 0% of the time, Pallas kernels for 0%

profile of v2, /device:TPU:251, one launch (start us, length us, event | category | flops | bytes accessed | tf_op | source)
XLA Modules:
  0.0 116.6 jit_solution(14753789717372916277)
XLA Ops:
  0.6 0.9 copy-done
  1.6 0.9 copy-done.1
  2.5 0.7 copy-done.2
  3.2 1.0 shard_map.50
  4.2 3.0 %collective-permute-start.1 = (f32[52,16,128]{2,1,0:T(8,128)S(1)}, f32[52,16,128]{2,1,0:T(8,128)S(1)}, u32[]{:S(2)}, u32[]{:S(2)}) collective-permute-start(f32[52,16,128]{2,1,0:T(8,128)S(1)} %get-tuple-element.29), channel_id=1, source_target_pairs={{16,0},{32,16},{48,32},{64,48},{80,64},{96,80},{112,96},{128,112},... | collective-permute-start | bytes 1277960 | tf_op jit(solution)/shard_map/ppermute | solution.py:471
  7.2 4.4 %collective-permute-start = (f32[52,16,128]{2,1,0:T(8,128)S(1)}, f32[52,16,128]{2,1,0:T(8,128)S(1)}, u32[]{:S(2)}, u32[]{:S(2)}) collective-permute-start(f32[52,16,128]{2,1,0:T(8,128)S(1)} %get-tuple-element.27.up.refs_1_), channel_id=1, source_target_pairs={{0,16},{16,32},{32,48},{48,64},{64,80},{80,96},{96,112},{112,128},... | collective-permute-start | bytes 1277960 | tf_op jit(solution)/shard_map/ppermute | solution.py:471
  11.6 7.3 %collective-permute-done.1.high.refs_3_ = f32[52,16,128]{2,1,0:T(8,128)S(1)} collective-permute-done((f32[52,16,128]{2,1,0:T(8,128)S(1)}, f32[52,16,128]{2,1,0:T(8,128)S(1)}, u32[]{:S(2)}, u32[]{:S(2)}) %collective-permute-start.1) | collective-permute-done | bytes 426016 | tf_op jit(solution)/shard_map/ppermute | solution.py:471
  18.9 0.9 collective-permute-done.low.refs_0_
  19.9 7.0 %collective-permute-start.2 = (f32[1088,128]{1,0:T(8,128)S(1)}, f32[1088,128]{1,0:T(8,128)S(1)}, u32[]{:S(2)}, u32[]{:S(2)}) collective-permute-start(f32[1088,128]{1,0:T(8,128)S(1)} %get-tuple-element.30), channel_id=1, source_target_pairs={{0,1},{1,2},{2,3},{3,4},{4,5},{5,6},{6,7},{7,8},{8,9},{9,10},{10,1... | collective-permute-start | bytes 1671176 | tf_op jit(solution)/shard_map/ppermute | solution.py:471
  26.8 1.9 %collective-permute-start.3 = (f32[1088,128]{1,0:T(8,128)S(1)}, f32[1088,128]{1,0:T(8,128)S(1)}, u32[]{:S(2)}, u32[]{:S(2)}) collective-permute-start(f32[1088,128]{1,0:T(8,128)S(1)} %get-tuple-element.31), channel_id=1, source_target_pairs={{1,0},{2,1},{3,2},{4,3},{5,4},{6,5},{7,6},{8,7},{9,8},{10,9},{11,1... | collective-permute-start | bytes 1671176 | tf_op jit(solution)/shard_map/ppermute | solution.py:471
  28.8 4.5 %collective-permute-done.2.refs_4_ = f32[1088,128]{1,0:T(8,128)S(1)} collective-permute-done((f32[1088,128]{1,0:T(8,128)S(1)}, f32[1088,128]{1,0:T(8,128)S(1)}, u32[]{:S(2)}, u32[]{:S(2)}) %collective-permute-start.2) | collective-permute-done | bytes 557088 | tf_op jit(solution)/shard_map/ppermute | solution.py:471
  33.3 5.6 %collective-permute-done.3.refs_5_ = f32[1088,128]{1,0:T(8,128)S(1)} collective-permute-done((f32[1088,128]{1,0:T(8,128)S(1)}, f32[1088,128]{1,0:T(8,128)S(1)}, u32[]{:S(2)}, u32[]{:S(2)}) %collective-permute-start.3) | collective-permute-done | bytes 557088 | tf_op jit(solution)/shard_map/ppermute | solution.py:471
  38.9 4.4 %shard_map.52 = (f32[24,16,8,128]{3,2,1,0:T(8,128)S(1)}, f32[8,16,8,128]{3,2,1,0:T(8,128)S(1)}, f32[18,16,8,128]{3,2,1,0:T(8,128)S(1)}, f32[16,16,128]{2,1,0:T(8...) custom-call(f32[52,16,128]{2,1,0:T(8,128)S(1)} %collective-permute-d, ...), custom_call_target="tpu_custom_call" | custom-call | tf_op jit(solution)/shard_map/pallas_call | solution.py:458
  43.4 6.2 %collective-permute-start.5 = (f32[192,128]{1,0:T(8,128)S(1)}, f32[192,128]{1,0:T(8,128)S(1)}, u32[]{:S(2)}, u32[]{:S(2)}) collective-permute-start(f32[192,128]{1,0:T(8,128)S(1)} %get-tuple-element.33), channel_id=1, source_target_pairs={{0,16},{16,32},{32,48},{48,64},{64,80},{80,96},{96,112},{112,128},... | collective-permute-start | bytes 294920 | tf_op jit(solution)/shard_map/ppermute | solution.py:471
  49.6 1.9 %collective-permute-start.6 = (f32[192,128]{1,0:T(8,128)S(1)}, f32[192,128]{1,0:T(8,128)S(1)}, u32[]{:S(2)}, u32[]{:S(2)}) collective-permute-start(f32[192,128]{1,0:T(8,128)S(1)} %get-tuple-element.36), channel_id=1, source_target_pairs={{16,0},{32,16},{48,32},{64,48},{80,64},{96,80},{112,96},{128,112},... | collective-permute-start | bytes 294920 | tf_op jit(solution)/shard_map/ppermute | solution.py:471
  51.5 3.1 %collective-permute-start.4 = (f32[144,128]{1,0:T(8,128)S(1)}, f32[144,128]{1,0:T(8,128)S(1)}, u32[]{:S(2)}, u32[]{:S(2)}) collective-permute-start(f32[144,128]{1,0:T(8,128)S(1)} %get-tuple-element.32), channel_id=1, source_target_pairs={{0,32},{16,48},{32,64},{48,80},{64,96},{80,112},{96,128},{112,144}... | collective-permute-start | bytes 221192 | tf_op jit(solution)/shard_map/ppermute | solution.py:471
  54.6 3.1 %collective-permute-start.7 = (f32[144,128]{1,0:T(8,128)S(1)}, f32[144,128]{1,0:T(8,128)S(1)}, u32[]{:S(2)}, u32[]{:S(2)}) collective-permute-start(f32[144,128]{1,0:T(8,128)S(1)} %get-tuple-element.37), channel_id=1, source_target_pairs={{32,0},{48,16},{64,32},{80,48},{96,64},{112,80},{128,96},{144,112}... | collective-permute-start | bytes 221192 | tf_op jit(solution)/shard_map/ppermute | solution.py:471
  57.7 5.8 %collective-permute-done.7.refs_5_ = f32[144,128]{1,0:T(8,128)S(1)} collective-permute-done((f32[144,128]{1,0:T(8,128)S(1)}, f32[144,128]{1,0:T(8,128)S(1)}, u32[]{:S(2)}, u32[]{:S(2)}) %collective-permute-start.7) | collective-permute-done | bytes 73760 | tf_op jit(solution)/shard_map/ppermute | solution.py:471
  63.6 4.1 %collective-permute-start.8 = (f32[624,128]{1,0:T(8,128)S(1)}, f32[624,128]{1,0:T(8,128)S(1)}, u32[]{:S(2)}, u32[]{:S(2)}) collective-permute-start(f32[624,128]{1,0:T(8,128)S(1)} %get-tuple-element.38), channel_id=1, source_target_pairs={{0,1},{1,2},{2,3},{3,4},{4,5},{5,6},{6,7},{7,8},{8,9},{9,10},{10,1... | collective-permute-start | bytes 958472 | tf_op jit(solution)/shard_map/ppermute | solution.py:471
  67.7 1.9 %collective-permute-start.9 = (f32[624,128]{1,0:T(8,128)S(1)}, f32[624,128]{1,0:T(8,128)S(1)}, u32[]{:S(2)}, u32[]{:S(2)}) collective-permute-start(f32[624,128]{1,0:T(8,128)S(1)} %get-tuple-element.39), channel_id=1, source_target_pairs={{1,0},{2,1},{3,2},{4,3},{5,4},{6,5},{7,6},{8,7},{9,8},{10,9},{11,1... | collective-permute-start | bytes 958472 | tf_op jit(solution)/shard_map/ppermute | solution.py:471
  69.7 2.0 %collective-permute-done.8.refs_6_ = f32[624,128]{1,0:T(8,128)S(1)} collective-permute-done((f32[624,128]{1,0:T(8,128)S(1)}, f32[624,128]{1,0:T(8,128)S(1)}, u32[]{:S(2)}, u32[]{:S(2)}) %collective-permute-start.8) | collective-permute-done | bytes 319520 | tf_op jit(solution)/shard_map/ppermute | solution.py:471
  71.7 5.6 %collective-permute-done.9.refs_7_ = f32[624,128]{1,0:T(8,128)S(1)} collective-permute-done((f32[624,128]{1,0:T(8,128)S(1)}, f32[624,128]{1,0:T(8,128)S(1)}, u32[]{:S(2)}, u32[]{:S(2)}) %collective-permute-start.9) | collective-permute-done | bytes 319520 | tf_op jit(solution)/shard_map/ppermute | solution.py:471
  77.3 4.2 %shard_map.54 = (f32[24,8,8,128]{3,2,1,0:T(8,128)S(1)}, f32[10,8,8,128]{3,2,1,0:T(8,128)S(1)}, f32[20,8,8,128]{3,2,1,0:T(8,128)S(1)}, f32[8,16,128]{2,1,0:T(8,12...) custom-call(f32[144,128]{1,0:T(8,128)S(1)} %collective-permute-done.4.refs_0_, ...), custom_call_target="tpu_custom_call" | custom-call | tf_op jit(solution)/shard_map/pallas_call | solution.py:458
  81.4 2.7 %collective-permute-start.11 = (f32[2,16,128]{2,1,0:T(8,128)S(1)}, f32[2,16,128]{2,1,0:T(8,128)S(1)}, u32[]{:S(2)}, u32[]{:S(2)}) collective-permute-start(f32[2,16,128]{2,1,0:T(8,128)S(1)} %get-tuple-element.40), channel_id=1, source_target_pairs={{0,16},{16,32},{32,48},{48,64},{64,80},{80,96},{96,112},{112,128},... | collective-permute-start | bytes 49160 | tf_op jit(solution)/shard_map/ppermute | solution.py:471
  84.1 2.7 %collective-permute-start.10 = (f32[2,16,128]{2,1,0:T(8,128)S(1)}, f32[2,16,128]{2,1,0:T(8,128)S(1)}, u32[]{:S(2)}, u32[]{:S(2)}) collective-permute-start(f32[2,16,128]{2,1,0:T(8,128)S(1)} %get-tuple-element.40), channel_id=1, source_target_pairs={{0,32},{16,48},{32,64},{48,80},{64,96},{80,112},{96,128},{112,144}... | collective-permute-start | bytes 49160 | tf_op jit(solution)/shard_map/ppermute | solution.py:471
  86.8 4.3 %collective-permute-start.13 = (f32[2,16,128]{2,1,0:T(8,128)S(1)}, f32[2,16,128]{2,1,0:T(8,128)S(1)}, u32[]{:S(2)}, u32[]{:S(2)}) collective-permute-start(f32[2,16,128]{2,1,0:T(8,128)S(1)} %get-tuple-element.42), channel_id=1, source_target_pairs={{32,0},{48,16},{64,32},{80,48},{96,64},{112,80},{128,96},{144,112}... | collective-permute-start | bytes 49160 | tf_op jit(solution)/shard_map/ppermute | solution.py:471
  91.1 3.1 %collective-permute-start.12 = (f32[2,16,128]{2,1,0:T(8,128)S(1)}, f32[2,16,128]{2,1,0:T(8,128)S(1)}, u32[]{:S(2)}, u32[]{:S(2)}) collective-permute-start(f32[2,16,128]{2,1,0:T(8,128)S(1)} %get-tuple-element.42), channel_id=1, source_target_pairs={{16,0},{32,16},{48,32},{64,48},{80,64},{96,80},{112,96},{128,112},... | collective-permute-start | bytes 49160 | tf_op jit(solution)/shard_map/ppermute | solution.py:471
  94.3 3.4 %collective-permute-done.12.refs_3_ = f32[2,16,128]{2,1,0:T(8,128)S(1)} collective-permute-done((f32[2,16,128]{2,1,0:T(8,128)S(1)}, f32[2,16,128]{2,1,0:T(8,128)S(1)}, u32[]{:S(2)}, u32[]{:S(2)}) %collective-permute-start.12) | collective-permute-done | bytes 16416 | tf_op jit(solution)/shard_map/ppermute | solution.py:471
  97.7 3.5 %collective-permute-start.14 = (f32[16,8,128]{2,1,0:T(8,128)S(1)}, f32[16,8,128]{2,1,0:T(8,128)S(1)}, u32[]{:S(2)}, u32[]{:S(2)}) collective-permute-start(f32[16,8,128]{2,1,0:T(8,128)S(1)} %get-tuple-element.43), channel_id=1, source_target_pairs={{0,1},{1,2},{2,3},{3,4},{4,5},{5,6},{6,7},{7,8},{8,9},{9,10},{10,1... | collective-permute-start | bytes 196616 | tf_op jit(solution)/shard_map/ppermute | solution.py:471
  101.1 1.9 %collective-permute-start.15 = (f32[16,8,128]{2,1,0:T(8,128)S(1)}, f32[16,8,128]{2,1,0:T(8,128)S(1)}, u32[]{:S(2)}, u32[]{:S(2)}) collective-permute-start(f32[16,8,128]{2,1,0:T(8,128)S(1)} %get-tuple-element.44), channel_id=1, source_target_pairs={{1,0},{2,1},{3,2},{4,3},{5,4},{6,5},{7,6},{8,7},{9,8},{10,9},{11,1... | collective-permute-start | bytes 196616 | tf_op jit(solution)/shard_map/ppermute | solution.py:471
  103.1 4.9 %collective-permute-done.15.refs_6_ = f32[16,8,128]{2,1,0:T(8,128)S(1)} collective-permute-done((f32[16,8,128]{2,1,0:T(8,128)S(1)}, f32[16,8,128]{2,1,0:T(8,128)S(1)}, u32[]{:S(2)}, u32[]{:S(2)}) %collective-permute-start.15) | collective-permute-done | bytes 65568 | tf_op jit(solution)/shard_map/ppermute | solution.py:471
  107.9 8.6 %shard_map.56 = (f32[8,16,512]{2,1,0:T(8,128)}, f32[8,16,512]{2,1,0:T(8,128)}) custom-call(f32[2,16,128]{2,1,0:T(8,128)S(1)} %collective-permute-done.10.refs_0_, f32[2,16,128]{2,1,0:T(8,128)S(1)} %collective-permute-done.11.refs_1_, f32[8,16,128]{2,1,0:T(8,128)S(1)} %get-tuple-element.41.refs_2_, f32[2,16,128]{2,1,0:T(8,128)S(1)} %collective-permute-done.12.refs_3_, ...), custom_call_target="tpu_custom_call" | custom-call | tf_op jit(solution)/shard_map/pallas_call | solution.py:458
  (13 shorter events, 0.3 us)
Async XLA Ops:
  0.6 1.0 copy-start
  1.6 0.9 copy-start.1
  2.5 0.7 copy-start.2
  4.2 14.7 %collective-permute-start.1 = (f32[52,16,128]{2,1,0:T(8,128)S(1)}, f32[52,16,128]{2,1,0:T(8,128)S(1)}, u32[]{:S(2)}, u32[]{:S(2)}) collective-permute-start(f32[52,16,128]{2,1,0:T(8,128)S(1)} %get-tuple-element.29), channel_id=1, source_target_pairs={{16,0},{32,16},{48,32},{64,48},{80,64},{96,80},{112,96},{128,112},... | collective-permute-start | bytes 1277960 | tf_op jit(solution)/shard_map/ppermute | solution.py:471
  7.2 12.6 %collective-permute-start = (f32[52,16,128]{2,1,0:T(8,128)S(1)}, f32[52,16,128]{2,1,0:T(8,128)S(1)}, u32[]{:S(2)}, u32[]{:S(2)}) collective-permute-start(f32[52,16,128]{2,1,0:T(8,128)S(1)} %get-tuple-element.27.up.refs_1_), channel_id=1, source_target_pairs={{0,16},{16,32},{32,48},{48,64},{64,80},{80,96},{96,112},{112,128},... | collective-permute-start | bytes 1277960 | tf_op jit(solution)/shard_map/ppermute | solution.py:471
  19.9 13.4 %collective-permute-start.2 = (f32[1088,128]{1,0:T(8,128)S(1)}, f32[1088,128]{1,0:T(8,128)S(1)}, u32[]{:S(2)}, u32[]{:S(2)}) collective-permute-start(f32[1088,128]{1,0:T(8,128)S(1)} %get-tuple-element.30), channel_id=1, source_target_pairs={{0,1},{1,2},{2,3},{3,4},{4,5},{5,6},{6,7},{7,8},{8,9},{9,10},{10,1... | collective-permute-start | bytes 1671176 | tf_op jit(solution)/shard_map/ppermute | solution.py:471
  26.8 12.1 %collective-permute-start.3 = (f32[1088,128]{1,0:T(8,128)S(1)}, f32[1088,128]{1,0:T(8,128)S(1)}, u32[]{:S(2)}, u32[]{:S(2)}) collective-permute-start(f32[1088,128]{1,0:T(8,128)S(1)} %get-tuple-element.31), channel_id=1, source_target_pairs={{1,0},{2,1},{3,2},{4,3},{5,4},{6,5},{7,6},{8,7},{9,8},{10,9},{11,1... | collective-permute-start | bytes 1671176 | tf_op jit(solution)/shard_map/ppermute | solution.py:471
  43.4 20.2 %collective-permute-start.5 = (f32[192,128]{1,0:T(8,128)S(1)}, f32[192,128]{1,0:T(8,128)S(1)}, u32[]{:S(2)}, u32[]{:S(2)}) collective-permute-start(f32[192,128]{1,0:T(8,128)S(1)} %get-tuple-element.33), channel_id=1, source_target_pairs={{0,16},{16,32},{32,48},{48,64},{64,80},{80,96},{96,112},{112,128},... | collective-permute-start | bytes 294920 | tf_op jit(solution)/shard_map/ppermute | solution.py:471
  49.6 13.9 %collective-permute-start.6 = (f32[192,128]{1,0:T(8,128)S(1)}, f32[192,128]{1,0:T(8,128)S(1)}, u32[]{:S(2)}, u32[]{:S(2)}) collective-permute-start(f32[192,128]{1,0:T(8,128)S(1)} %get-tuple-element.36), channel_id=1, source_target_pairs={{16,0},{32,16},{48,32},{64,48},{80,64},{96,80},{112,96},{128,112},... | collective-permute-start | bytes 294920 | tf_op jit(solution)/shard_map/ppermute | solution.py:471
  51.5 6.2 %collective-permute-start.4 = (f32[144,128]{1,0:T(8,128)S(1)}, f32[144,128]{1,0:T(8,128)S(1)}, u32[]{:S(2)}, u32[]{:S(2)}) collective-permute-start(f32[144,128]{1,0:T(8,128)S(1)} %get-tuple-element.32), channel_id=1, source_target_pairs={{0,32},{16,48},{32,64},{48,80},{64,96},{80,112},{96,128},{112,144}... | collective-permute-start | bytes 221192 | tf_op jit(solution)/shard_map/ppermute | solution.py:471
  54.6 8.9 %collective-permute-start.7 = (f32[144,128]{1,0:T(8,128)S(1)}, f32[144,128]{1,0:T(8,128)S(1)}, u32[]{:S(2)}, u32[]{:S(2)}) collective-permute-start(f32[144,128]{1,0:T(8,128)S(1)} %get-tuple-element.37), channel_id=1, source_target_pairs={{32,0},{48,16},{64,32},{80,48},{96,64},{112,80},{128,96},{144,112}... | collective-permute-start | bytes 221192 | tf_op jit(solution)/shard_map/ppermute | solution.py:471
  63.6 8.0 %collective-permute-start.8 = (f32[624,128]{1,0:T(8,128)S(1)}, f32[624,128]{1,0:T(8,128)S(1)}, u32[]{:S(2)}, u32[]{:S(2)}) collective-permute-start(f32[624,128]{1,0:T(8,128)S(1)} %get-tuple-element.38), channel_id=1, source_target_pairs={{0,1},{1,2},{2,3},{3,4},{4,5},{5,6},{6,7},{7,8},{8,9},{9,10},{10,1... | collective-permute-start | bytes 958472 | tf_op jit(solution)/shard_map/ppermute | solution.py:471
  67.7 9.5 %collective-permute-start.9 = (f32[624,128]{1,0:T(8,128)S(1)}, f32[624,128]{1,0:T(8,128)S(1)}, u32[]{:S(2)}, u32[]{:S(2)}) collective-permute-start(f32[624,128]{1,0:T(8,128)S(1)} %get-tuple-element.39), channel_id=1, source_target_pairs={{1,0},{2,1},{3,2},{4,3},{5,4},{6,5},{7,6},{8,7},{9,8},{10,9},{11,1... | collective-permute-start | bytes 958472 | tf_op jit(solution)/shard_map/ppermute | solution.py:471
  81.4 12.7 %collective-permute-start.11 = (f32[2,16,128]{2,1,0:T(8,128)S(1)}, f32[2,16,128]{2,1,0:T(8,128)S(1)}, u32[]{:S(2)}, u32[]{:S(2)}) collective-permute-start(f32[2,16,128]{2,1,0:T(8,128)S(1)} %get-tuple-element.40), channel_id=1, source_target_pairs={{0,16},{16,32},{32,48},{48,64},{64,80},{80,96},{96,112},{112,128},... | collective-permute-start | bytes 49160 | tf_op jit(solution)/shard_map/ppermute | solution.py:471
  84.1 10.1 %collective-permute-start.10 = (f32[2,16,128]{2,1,0:T(8,128)S(1)}, f32[2,16,128]{2,1,0:T(8,128)S(1)}, u32[]{:S(2)}, u32[]{:S(2)}) collective-permute-start(f32[2,16,128]{2,1,0:T(8,128)S(1)} %get-tuple-element.40), channel_id=1, source_target_pairs={{0,32},{16,48},{32,64},{48,80},{64,96},{80,112},{96,128},{112,144}... | collective-permute-start | bytes 49160 | tf_op jit(solution)/shard_map/ppermute | solution.py:471
  86.8 7.5 %collective-permute-start.13 = (f32[2,16,128]{2,1,0:T(8,128)S(1)}, f32[2,16,128]{2,1,0:T(8,128)S(1)}, u32[]{:S(2)}, u32[]{:S(2)}) collective-permute-start(f32[2,16,128]{2,1,0:T(8,128)S(1)} %get-tuple-element.42), channel_id=1, source_target_pairs={{32,0},{48,16},{64,32},{80,48},{96,64},{112,80},{128,96},{144,112}... | collective-permute-start | bytes 49160 | tf_op jit(solution)/shard_map/ppermute | solution.py:471
  91.1 6.6 %collective-permute-start.12 = (f32[2,16,128]{2,1,0:T(8,128)S(1)}, f32[2,16,128]{2,1,0:T(8,128)S(1)}, u32[]{:S(2)}, u32[]{:S(2)}) collective-permute-start(f32[2,16,128]{2,1,0:T(8,128)S(1)} %get-tuple-element.42), channel_id=1, source_target_pairs={{16,0},{32,16},{48,32},{64,48},{80,64},{96,80},{112,96},{128,112},... | collective-permute-start | bytes 49160 | tf_op jit(solution)/shard_map/ppermute | solution.py:471
  97.7 5.4 %collective-permute-start.14 = (f32[16,8,128]{2,1,0:T(8,128)S(1)}, f32[16,8,128]{2,1,0:T(8,128)S(1)}, u32[]{:S(2)}, u32[]{:S(2)}) collective-permute-start(f32[16,8,128]{2,1,0:T(8,128)S(1)} %get-tuple-element.43), channel_id=1, source_target_pairs={{0,1},{1,2},{2,3},{3,4},{4,5},{5,6},{6,7},{7,8},{8,9},{9,10},{10,1... | collective-permute-start | bytes 196616 | tf_op jit(solution)/shard_map/ppermute | solution.py:471
  101.1 6.8 %collective-permute-start.15 = (f32[16,8,128]{2,1,0:T(8,128)S(1)}, f32[16,8,128]{2,1,0:T(8,128)S(1)}, u32[]{:S(2)}, u32[]{:S(2)}) collective-permute-start(f32[16,8,128]{2,1,0:T(8,128)S(1)} %get-tuple-element.44), channel_id=1, source_target_pairs={{1,0},{2,1},{3,2},{4,3},{5,4},{6,5},{7,6},{8,7},{9,8},{10,9},{11,1... | collective-permute-start | bytes 196616 | tf_op jit(solution)/shard_map/ppermute | solution.py:471

commit v3 on v2

--- a/solution.py
+++ b/solution.py
@@ -175,7 +175,7 @@
             at += 5
 
 
-def fine_pre_kernel(counts, low, up, root, high, left, right, q, y, r, mid_q, mid_r, low1, high1, low2, high2, *scratch):
+def fine_pre_kernel(counts, low, up, root, high, left, right, q, y, r, mid_q, mid_r, early, late, *scratch):
     natural, w = scratch[0], scratch[1:5]
     gz, xy = lax.axis_index("gz"), lax.axis_index("xy")
     masks = row_masks(4, 16 * xy - 8, 16 * counts[1])
@@ -238,35 +238,66 @@
                 mid_q[2 * m + k, pl.ds(x, 8, 2), :] = 0.5 * sums / jnp.maximum(roots, LEAST)
 
     loop(0, 8, fold)
-    for i in range(8):
-        for near, far, first in ((low1, low2, 0), (high1, high2, 8)):
-            values = mid_q[first + i, 2:14]
-            near[12 * i : 12 * i + 12] = values
-            far[12 * i : 12 * i + 12] = values
-            values = mid_r[first + i, 2:14]
-            near[96 + 12 * i : 108 + 12 * i] = values
-            j = i - 4 if first == 0 else i
-            if 0 <= j < 4:
-                far[96 + 12 * j : 108 + 12 * j] = values
-
-
-def mid_parts(refs):
-    low2, low1, mid_q, mid_r, high1, high2 = refs
-
+    skip = jnp.where(gz % 4 == 3, 0, 2)
+    for out, start in ((early, skip), (late, 2 - skip)):
+        for i in range(16):
+            out[12 * i : 12 * i + 12] = mid_q[i, 2:14]
+        for i in range(12):
+            out[192 + 12 * i : 204 + 12 * i] = mid_r[2 * start + i, 2:14]
+
+
+def mid_pairs(count):
+    first, second = [], []
+    for i in range(count):
+        up, down = (first, second) if i % 4 != 3 else (second, first)
+        if i + 2 < count:
+            up.append((i, i + 2))
+        if i >= 2:
+            down.append((i, i - 2))
+    return first, second + [(0, 1), (count - 1, count - 2)]
+
+
+def mid_sides(count, gz, first, second, low, high):
+    @pl.when(gz % 4 != 1)
+    def _():
+        low[...] = first[...]
+        high[...] = second[...]
+
+    @pl.when(gz % 4 == 1)
+    def _():
+        low[...] = second[...]
+        high[...] = first[...]
+
+    @pl.when(gz == 1)
+    def _():
+        low[0:96] = jnp.zeros((96, LANES), F32)
+        low[96:192] = second[0:96]
+        low[192:240] = jnp.zeros((48, LANES), F32)
+        low[240:336] = second[192:288]
+
+    @pl.when(gz == count - 2)
+    def _():
+        high[0:96] = second[96:192]
+        high[96:192] = jnp.zeros((96, LANES), F32)
+        high[192:288] = second[240:336]
+        high[288:336] = jnp.zeros((48, LANES), F32)
+
+
+def mid_parts(low, high, mid_q, mid_r):
     def rows(field, z, k):
         if 8 <= z < 16:
             return (mid_q, mid_r)[field][2 * (z - 8) + k, 2:14]
-        ref, z = [(low2, z), (low1, z - 4), None, None, (high1, z - 16), (high2, z - 20)][z // 4]
-        if field == 1 and ref is low2:
-            z = z - 2
-        at = 96 * field + 12 * (2 * z + k)
-        return ref[at : at + 12]
+        at = 12 * (2 * (z if z < 8 else z - 16) + k)
+        if field == 1:
+            at = at + (192 if z >= 16 else 144)
+        return (low if z < 8 else high)[at : at + 12]
 
     return rows
 
 
-def mid_pack_kernel(*refs):
-    rows, left, right = mid_parts(refs[:6]), refs[6], refs[7]
+def mid_pack_kernel(counts, first, second, mid_q, mid_r, low, high, left, right):
+    mid_sides(counts[0], lax.axis_index("gz"), first, second, low, high)
+    rows = mid_parts(low, high, mid_q, mid_r)
     at = 0
     for z in range(24):
         for k in range(2):
@@ -283,7 +314,7 @@
 
 
 def mid_pre_kernel(counts, *refs):
-    rows, (left, right), refs = mid_parts(refs[:6]), refs[6:8], refs[8:]
+    rows, (left, right), refs = mid_parts(*refs[:4]), refs[4:6], refs[6:]
     q, y, r, coarse, coarse_low, coarse_high, coarse_root, natural = refs[:8]
     w = refs[8:]
     gz, xy = lax.axis_index("gz"), lax.axis_index("xy")
@@ -341,13 +372,13 @@
             coarse_root[m, pl.ds(x, 8, 2), :] = mean
             if 0 < m < 9:
                 coarse[m - 1, pl.ds(x, 8, 2), :] = 0.5 * sums / jnp.maximum(mean, LEAST)
-    for m in range(2):
+    for m in range(4):
         coarse_low[m] = coarse[m]
-        coarse_high[m] = coarse[6 + m]
+        coarse_high[m] = coarse[4 + m]
 
 
 def coarse_pack_kernel(*refs):
-    parts, left, right = refs[:5], refs[5], refs[6]
+    parts, left, right = refs[:3], refs[3], refs[4]
     at = 0
     for ref in parts:
         for k in range(ref.shape[0]):
@@ -357,7 +388,7 @@
 
 
 def finish_kernel(counts, *refs):
-    parts, (left, right), refs = refs[:5], refs[5:7], refs[7:]
+    parts, (left, right), refs = refs[:3], refs[3:5], refs[5:]
     coarse_root, mid_q, mid_y, mid_r, fine_q, fine_y, fine_r, out_x, out_r = refs[:9]
     natural, cq, error, spread, mq, mt, fq, ft, plain_x, plain_r, rows_x, rows_r = refs[9:21]
     cw, mw, fw = refs[21:25], refs[25:29], refs[29:33]
@@ -479,36 +510,35 @@
 def on_device(load_field, density, void_mask):
     up, down, root = call(
         scale_kernel,
-        (load_field, density, void_mask),
+        [pltpu.with_memory_space_constraint(x, pltpu.HBM) for x in (load_field, density, void_mask)],
         [(52, 16, LANES), (52, 16, LANES), (32, 16, LANES)],
         [(16, 16, 512), pltpu.VMEM((1, 2, 64), jnp.int32), pltpu.SemaphoreType.DMA((3,))],
-        pl.ANY,
+        pltpu.HBM,
     )
     low, high = send(up, "gz", 1), send(down, "gz", -1)
     to_left, to_right = call(fine_pack_kernel, (low, up, root, high), [(1088, LANES)] * 2)
     left, right = send(to_right, "xy", 1), send(to_left, "xy", -1)
     fine = (24, 16, 8, LANES)
-    fine_q, fine_y, fine_r, mid_q, mid_r, low1, high1, low2, high2 = call(
+    fine_q, fine_y, fine_r, mid_q, mid_r, first, second = call(
         with_counts(fine_pre_kernel),
         (low, up, root, high, left, right),
-        [fine, (8, 16, 8, LANES), (18, 16, 8, LANES)] + [(16, 16, LANES)] * 2 + [(192, LANES)] * 2 + [(144, LANES)] * 2,
+        [fine, (8, 16, 8, LANES), (18, 16, 8, LANES)] + [(16, 16, LANES)] * 2 + [(336, LANES)] * 2,
         [(96, 32, LANES)] + [fine] * 4,
     )
-    a1, b1 = send(low1, "gz", 1), send(high1, "gz", -1)
-    a2, b2 = send(low2, "gz", 2), send(high2, "gz", -2)
-    parts = (a2, a1, mid_q, mid_r, b1, b2)
-    to_left, to_right = call(mid_pack_kernel, parts, [(624, LANES)] * 2)
+    pairs = mid_pairs(lax.axis_size("gz"))
+    first, second = lax.ppermute(first, "gz", pairs[0]), lax.ppermute(second, "gz", pairs[1])
+    low, high, to_left, to_right = call(
+        with_counts(mid_pack_kernel), (first, second, mid_q, mid_r), [(336, LANES)] * 2 + [(624, LANES)] * 2
+    )
     left, right = send(to_right, "xy", 1), send(to_left, "xy", -1)
     mid = (24, 8, 8, LANES)
     mid_q, mid_y, mid_r, coarse, coarse_low, coarse_high, coarse_root = call(
         with_counts(mid_pre_kernel),
-        parts + (left, right),
-        [mid, (10, 8, 8, LANES), (20, 8, 8, LANES), (8, 16, LANES)] + [(2, 16, LANES)] * 2 + [(10, 16, LANES)],
+        (low, high, mid_q, mid_r, left, right),
+        [mid, (10, 8, 8, LANES), (20, 8, 8, LANES), (8, 16, LANES)] + [(4, 16, LANES)] * 2 + [(10, 16, LANES)],
         [(48, 32, LANES)] + [mid] * 4,
     )
-    a1, b1 = send(coarse_low, "gz", 1), send(coarse_high, "gz", -1)
-    a2, b2 = send(coarse_low, "gz", 2), send(coarse_high, "gz", -2)
-    parts = (a2, a1, coarse, b1, b2)
+    parts = (send(coarse_low, "gz", 2), coarse, send(coarse_high, "gz", -2))
     to_left, to_right = call(coarse_pack_kernel, parts, [(16, 8, LANES)] * 2)
     left, right = send(to_right, "xy", 1), send(to_left, "xy", -1)
     coarsest = (16, 3, 8, LANES)

time: 117 us -> 107 us (0.915)
  the two profiles are of different devices: /device:TPU:251 before, /device:TPU:245 now
where the time goes in v3:
time: 107 us; the launch traced here: 106 us
  waiting for transfers between devices  44.1 us (41%)
  starting transfers between devices  42.2 us (39%)
  Pallas kernels  19.2 us (18%)
    ppermute x10, waiting for transfers between devices, send(): return lax.ppermute(block, axis, pairs)  35.9 us
    ppermute x10, starting transfers between devices, send(): return lax.ppermute(block, axis, pairs)  33.7 us
    pallas_call x7, Pallas kernels, call(): pl.pallas_call(kernel, out_shape=[jax.ShapeDtypeStruct(s, F32) for s in o...  19.2 us
    ppermute x1, waiting for transfers between devices, on_device(): lax.ppermute(second, 'gz', pairs[1])  7.57 us
    ppermute x1, starting transfers between devices, on_device(): lax.ppermute(first, 'gz', pairs[0])  6.64 us
  transfers between devices with their start and end apart: 12, of which 10 were waited for; matrix products, arithmetic and copies ran while one was open for 0% of the time, Pallas kernels for 0%

profile of v3, /device:TPU:245, one launch (start us, length us, event | category | flops | bytes accessed | tf_op | source)
XLA Modules:
  0.0 106.3 jit_solution(13487076108929963214)
XLA Ops:
  0.6 1.7 %shard_map.50 = (f32[52,16,128]{2,1,0:T(8,128)S(1)}, f32[52,16,128]{2,1,0:T(8,128)S(1)}, f32[32,16,128]{2,1,0:T(8,128)S(1)}) custom-call(f32[8,16,512]{2,1,0:T(8,128)} %load_hbm.1, f32[8,16,512]{2,1,0:T(8,128)} %density_hbm.1, s32[1,2,64]{2,1,0:T(2,128)} %void_hbm.1), custom_call_target="tpu_custom_call" | custom-call | tf_op jit(solution)/shard_map/pallas_call | solution.py:489
  2.4 3.0 %collective-permute-start.1 = (f32[52,16,128]{2,1,0:T(8,128)S(1)}, f32[52,16,128]{2,1,0:T(8,128)S(1)}, u32[]{:S(2)}, u32[]{:S(2)}) collective-permute-start(f32[52,16,128]{2,1,0:T(8,128)S(1)} %get-tuple-element.29), channel_id=1, source_target_pairs={{16,0},{32,16},{48,32},{64,48},{80,64},{96,80},{112,96},{128,112},... | collective-permute-start | bytes 1277960 | tf_op jit(solution)/shard_map/ppermute | solution.py:502
  5.3 2.3 %collective-permute-start = (f32[52,16,128]{2,1,0:T(8,128)S(1)}, f32[52,16,128]{2,1,0:T(8,128)S(1)}, u32[]{:S(2)}, u32[]{:S(2)}) collective-permute-start(f32[52,16,128]{2,1,0:T(8,128)S(1)} %get-tuple-element.27.up.refs_1_), channel_id=1, source_target_pairs={{0,16},{16,32},{32,48},{48,64},{64,80},{80,96},{96,112},{112,128},... | collective-permute-start | bytes 1277960 | tf_op jit(solution)/shard_map/ppermute | solution.py:502
  7.7 7.3 %collective-permute-done.1.high.refs_3_ = f32[52,16,128]{2,1,0:T(8,128)S(1)} collective-permute-done((f32[52,16,128]{2,1,0:T(8,128)S(1)}, f32[52,16,128]{2,1,0:T(8,128)S(1)}, u32[]{:S(2)}, u32[]{:S(2)}) %collective-permute-start.1) | collective-permute-done | bytes 426016 | tf_op jit(solution)/shard_map/ppermute | solution.py:502
  14.9 2.6 %collective-permute-done.low.refs_0_ = f32[52,16,128]{2,1,0:T(8,128)S(1)} collective-permute-done((f32[52,16,128]{2,1,0:T(8,128)S(1)}, f32[52,16,128]{2,1,0:T(8,128)S(1)}, u32[]{:S(2)}, u32[]{:S(2)}) %collective-permute-start) | collective-permute-done | bytes 426016 | tf_op jit(solution)/shard_map/ppermute | solution.py:502
  17.6 0.1 shard_map.51
  17.7 7.0 %collective-permute-start.2 = (f32[1088,128]{1,0:T(8,128)S(1)}, f32[1088,128]{1,0:T(8,128)S(1)}, u32[]{:S(2)}, u32[]{:S(2)}) collective-permute-start(f32[1088,128]{1,0:T(8,128)S(1)} %get-tuple-element.30), channel_id=1, source_target_pairs={{0,1},{1,2},{2,3},{3,4},{4,5},{5,6},{6,7},{7,8},{8,9},{9,10},{10,1... | collective-permute-start | bytes 1671176 | tf_op jit(solution)/shard_map/ppermute | solution.py:502
  24.7 1.9 %collective-permute-start.3 = (f32[1088,128]{1,0:T(8,128)S(1)}, f32[1088,128]{1,0:T(8,128)S(1)}, u32[]{:S(2)}, u32[]{:S(2)}) collective-permute-start(f32[1088,128]{1,0:T(8,128)S(1)} %get-tuple-element.31), channel_id=1, source_target_pairs={{1,0},{2,1},{3,2},{4,3},{5,4},{6,5},{7,6},{8,7},{9,8},{10,9},{11,1... | collective-permute-start | bytes 1671176 | tf_op jit(solution)/shard_map/ppermute | solution.py:502
  26.6 4.5 %collective-permute-done.2.refs_4_ = f32[1088,128]{1,0:T(8,128)S(1)} collective-permute-done((f32[1088,128]{1,0:T(8,128)S(1)}, f32[1088,128]{1,0:T(8,128)S(1)}, u32[]{:S(2)}, u32[]{:S(2)}) %collective-permute-start.2) | collective-permute-done | bytes 557088 | tf_op jit(solution)/shard_map/ppermute | solution.py:502
  31.1 5.6 %collective-permute-done.3.refs_5_ = f32[1088,128]{1,0:T(8,128)S(1)} collective-permute-done((f32[1088,128]{1,0:T(8,128)S(1)}, f32[1088,128]{1,0:T(8,128)S(1)}, u32[]{:S(2)}, u32[]{:S(2)}) %collective-permute-start.3) | collective-permute-done | bytes 557088 | tf_op jit(solution)/shard_map/ppermute | solution.py:502
  36.7 4.5 %shard_map.52 = (f32[24,16,8,128]{3,2,1,0:T(8,128)S(1)}, f32[8,16,8,128]{3,2,1,0:T(8,128)S(1)}, f32[18,16,8,128]{3,2,1,0:T(8,128)S(1)}, f32[16,16,128]{2,1,0:T(8...) custom-call(f32[52,16,128]{2,1,0:T(8,128)S(1)} %collective-permute-done.low.refs_0_, ...), custom_call_target="tpu_custom_call" | custom-call | tf_op jit(solution)/shard_map/pallas_call | solution.py:489
  41.2 6.6 %collective-permute-start.4 = (f32[336,128]{1,0:T(8,128)S(1)}, f32[336,128]{1,0:T(8,128)S(1)}, u32[]{:S(2)}, u32[]{:S(2)}) collective-permute-start(f32[336,128]{1,0:T(8,128)S(1)} %get-tuple-element.32), channel_id=1, source_target_pairs={{0,32},{16,48},{32,64},{48,16},{64,96},{80,112},{96,128},{112,80},... | collective-permute-start | bytes 516104 | tf_op jit(solution)/shard_map/ppermute | solution.py:529
  47.8 1.9 %collective-permute-start.5 = (f32[336,128]{1,0:T(8,128)S(1)}, f32[336,128]{1,0:T(8,128)S(1)}, u32[]{:S(2)}, u32[]{:S(2)}) collective-permute-start(f32[336,128]{1,0:T(8,128)S(1)} %get-tuple-element.33), channel_id=1, source_target_pairs={{32,0},{48,80},{64,32},{80,48},{96,64},{112,144},{128,96},{144,112... | collective-permute-start | bytes 516104 | tf_op jit(solution)/shard_map/ppermute | solution.py:529
  49.8 0.6 collective-permute-done.4.refs_0_
  50.4 7.6 %collective-permute-done.5.refs_1_ = f32[336,128]{1,0:T(8,128)S(1)} collective-permute-done((f32[336,128]{1,0:T(8,128)S(1)}, f32[336,128]{1,0:T(8,128)S(1)}, u32[]{:S(2)}, u32[]{:S(2)}) %collective-permute-start.5) | collective-permute-done | bytes 172064 | tf_op jit(solution)/shard_map/ppermute | solution.py:529
  57.9 0.1 shard_map.53
  58.0 6.6 %collective-permute-start.6 = (f32[624,128]{1,0:T(8,128)S(1)}, f32[624,128]{1,0:T(8,128)S(1)}, u32[]{:S(2)}, u32[]{:S(2)}) collective-permute-start(f32[624,128]{1,0:T(8,128)S(1)} %get-tuple-element.38), channel_id=1, source_target_pairs={{0,1},{1,2},{2,3},{3,4},{4,5},{5,6},{6,7},{7,8},{8,9},{9,10},{10,1... | collective-permute-start | bytes 958472 | tf_op jit(solution)/shard_map/ppermute | solution.py:502
  64.6 1.9 %collective-permute-start.7 = (f32[624,128]{1,0:T(8,128)S(1)}, f32[624,128]{1,0:T(8,128)S(1)}, u32[]{:S(2)}, u32[]{:S(2)}) collective-permute-start(f32[624,128]{1,0:T(8,128)S(1)} %get-tuple-element.39), channel_id=1, source_target_pairs={{1,0},{2,1},{3,2},{4,3},{5,4},{6,5},{7,6},{8,7},{9,8},{10,9},{11,1... | collective-permute-start | bytes 958472 | tf_op jit(solution)/shard_map/ppermute | solution.py:502
  66.6 2.0 %collective-permute-done.6.refs_4_ = f32[624,128]{1,0:T(8,128)S(1)} collective-permute-done((f32[624,128]{1,0:T(8,128)S(1)}, f32[624,128]{1,0:T(8,128)S(1)}, u32[]{:S(2)}, u32[]{:S(2)}) %collective-permute-start.6) | collective-permute-done | bytes 319520 | tf_op jit(solution)/shard_map/ppermute | solution.py:502
  68.6 5.6 %collective-permute-done.7.refs_5_ = f32[624,128]{1,0:T(8,128)S(1)} collective-permute-done((f32[624,128]{1,0:T(8,128)S(1)}, f32[624,128]{1,0:T(8,128)S(1)}, u32[]{:S(2)}, u32[]{:S(2)}) %collective-permute-start.7) | collective-permute-done | bytes 319520 | tf_op jit(solution)/shard_map/ppermute | solution.py:502
  74.2 4.2 %shard_map.54 = (f32[24,8,8,128]{3,2,1,0:T(8,128)S(1)}, f32[10,8,8,128]{3,2,1,0:T(8,128)S(1)}, f32[20,8,8,128]{3,2,1,0:T(8,128)S(1)}, f32[8,16,128]{2,1,0:T(8,12...) custom-call(f32[336,128]{1,0:T(8,128)S(1)} %get-tuple-element.36.refs_0_, ...), custom_call_target="tpu_custom_call" | custom-call | tf_op jit(solution)/shard_map/pallas_call | solution.py:489
  78.3 1.9 %collective-permute-start.8 = (f32[4,16,128]{2,1,0:T(8,128)S(1)}, f32[4,16,128]{2,1,0:T(8,128)S(1)}, u32[]{:S(2)}, u32[]{:S(2)}) collective-permute-start(f32[4,16,128]{2,1,0:T(8,128)S(1)} %get-tuple-element.40), channel_id=1, source_target_pairs={{0,32},{16,48},{32,64},{48,80},{64,96},{80,112},{96,128},{112,144}... | collective-permute-start | bytes 98312 | tf_op jit(solution)/shard_map/ppermute | solution.py:502
  80.3 4.3 %collective-permute-start.9 = (f32[4,16,128]{2,1,0:T(8,128)S(1)}, f32[4,16,128]{2,1,0:T(8,128)S(1)}, u32[]{:S(2)}, u32[]{:S(2)}) collective-permute-start(f32[4,16,128]{2,1,0:T(8,128)S(1)} %get-tuple-element.42), channel_id=1, source_target_pairs={{32,0},{48,16},{64,32},{80,48},{96,64},{112,80},{128,96},{144,112}... | collective-permute-start | bytes 98312 | tf_op jit(solution)/shard_map/ppermute | solution.py:502
  84.5 0.0 collective-permute-done.8.refs_0_
  84.6 3.4 %collective-permute-done.9.refs_2_ = f32[4,16,128]{2,1,0:T(8,128)S(1)} collective-permute-done((f32[4,16,128]{2,1,0:T(8,128)S(1)}, f32[4,16,128]{2,1,0:T(8,128)S(1)}, u32[]{:S(2)}, u32[]{:S(2)}) %collective-permute-start.9) | collective-permute-done | bytes 32800 | tf_op jit(solution)/shard_map/ppermute | solution.py:502
  88.0 2.9 %collective-permute-start.10 = (f32[16,8,128]{2,1,0:T(8,128)S(1)}, f32[16,8,128]{2,1,0:T(8,128)S(1)}, u32[]{:S(2)}, u32[]{:S(2)}) collective-permute-start(f32[16,8,128]{2,1,0:T(8,128)S(1)} %get-tuple-element.43), channel_id=1, source_target_pairs={{0,1},{1,2},{2,3},{3,4},{4,5},{5,6},{6,7},{7,8},{8,9},{9,10},{10,1... | collective-permute-start | bytes 196616 | tf_op jit(solution)/shard_map/ppermute | solution.py:502
  90.9 1.9 %collective-permute-start.11 = (f32[16,8,128]{2,1,0:T(8,128)S(1)}, f32[16,8,128]{2,1,0:T(8,128)S(1)}, u32[]{:S(2)}, u32[]{:S(2)}) collective-permute-start(f32[16,8,128]{2,1,0:T(8,128)S(1)} %get-tuple-element.44), channel_id=1, source_target_pairs={{1,0},{2,1},{3,2},{4,3},{5,4},{6,5},{7,6},{8,7},{9,8},{10,9},{11,1... | collective-permute-start | bytes 196616 | tf_op jit(solution)/shard_map/ppermute | solution.py:502
  92.8 0.0 collective-permute-done.10.refs_3_
  92.8 4.9 %collective-permute-done.11.refs_4_ = f32[16,8,128]{2,1,0:T(8,128)S(1)} collective-permute-done((f32[16,8,128]{2,1,0:T(8,128)S(1)}, f32[16,8,128]{2,1,0:T(8,128)S(1)}, u32[]{:S(2)}, u32[]{:S(2)}) %collective-permute-start.11) | collective-permute-done | bytes 65568 | tf_op jit(solution)/shard_map/ppermute | solution.py:502
  97.7 8.6 %shard_map.56 = (f32[8,16,512]{2,1,0:T(8,128)}, f32[8,16,512]{2,1,0:T(8,128)}) custom-call(f32[4,16,128]{2,1,0:T(8,128)S(1)} %collective-permute-done.8.refs_0_, f32[8,16,128]{2,1,0:T(8,128)S(1)} %get-tuple-element.41.refs_1_, f32[4,16,128]{2,1,0:T(8,128)S(1)} %collective-permute-done.9.refs_2_, f32[16,8,128]{2,1,0:T(8,128)S(1)} %collective-permute-done.10.refs_3_, ...), custom_call_target="tpu_custom_call" | custom-call | tf_op jit(solution)/shard_map/pallas_call | solution.py:489
  (1 shorter events, 0.0 us)
Async XLA Ops:
  2.4 12.6 %collective-permute-start.1 = (f32[52,16,128]{2,1,0:T(8,128)S(1)}, f32[52,16,128]{2,1,0:T(8,128)S(1)}, u32[]{:S(2)}, u32[]{:S(2)}) collective-permute-start(f32[52,16,128]{2,1,0:T(8,128)S(1)} %get-tuple-element.29), channel_id=1, source_target_pairs={{16,0},{32,16},{48,32},{64,48},{80,64},{96,80},{112,96},{128,112},... | collective-permute-start | bytes 1277960 | tf_op jit(solution)/shard_map/ppermute | solution.py:502
  5.3 12.2 %collective-permute-start = (f32[52,16,128]{2,1,0:T(8,128)S(1)}, f32[52,16,128]{2,1,0:T(8,128)S(1)}, u32[]{:S(2)}, u32[]{:S(2)}) collective-permute-start(f32[52,16,128]{2,1,0:T(8,128)S(1)} %get-tuple-element.27.up.refs_1_), channel_id=1, source_target_pairs={{0,16},{16,32},{32,48},{48,64},{64,80},{80,96},{96,112},{112,128},... | collective-permute-start | bytes 1277960 | tf_op jit(solution)/shard_map/ppermute | solution.py:502
  17.7 13.4 %collective-permute-start.2 = (f32[1088,128]{1,0:T(8,128)S(1)}, f32[1088,128]{1,0:T(8,128)S(1)}, u32[]{:S(2)}, u32[]{:S(2)}) collective-permute-start(f32[1088,128]{1,0:T(8,128)S(1)} %get-tuple-element.30), channel_id=1, source_target_pairs={{0,1},{1,2},{2,3},{3,4},{4,5},{5,6},{6,7},{7,8},{8,9},{9,10},{10,1... | collective-permute-start | bytes 1671176 | tf_op jit(solution)/shard_map/ppermute | solution.py:502
  24.7 12.1 %collective-permute-start.3 = (f32[1088,128]{1,0:T(8,128)S(1)}, f32[1088,128]{1,0:T(8,128)S(1)}, u32[]{:S(2)}, u32[]{:S(2)}) collective-permute-start(f32[1088,128]{1,0:T(8,128)S(1)} %get-tuple-element.31), channel_id=1, source_target_pairs={{1,0},{2,1},{3,2},{4,3},{5,4},{6,5},{7,6},{8,7},{9,8},{10,9},{11,1... | collective-permute-start | bytes 1671176 | tf_op jit(solution)/shard_map/ppermute | solution.py:502
  41.2 9.2 %collective-permute-start.4 = (f32[336,128]{1,0:T(8,128)S(1)}, f32[336,128]{1,0:T(8,128)S(1)}, u32[]{:S(2)}, u32[]{:S(2)}) collective-permute-start(f32[336,128]{1,0:T(8,128)S(1)} %get-tuple-element.32), channel_id=1, source_target_pairs={{0,32},{16,48},{32,64},{48,16},{64,96},{80,112},{96,128},{112,80},... | collective-permute-start | bytes 516104 | tf_op jit(solution)/shard_map/ppermute | solution.py:529
  47.8 10.1 %collective-permute-start.5 = (f32[336,128]{1,0:T(8,128)S(1)}, f32[336,128]{1,0:T(8,128)S(1)}, u32[]{:S(2)}, u32[]{:S(2)}) collective-permute-start(f32[336,128]{1,0:T(8,128)S(1)} %get-tuple-element.33), channel_id=1, source_target_pairs={{32,0},{48,80},{64,32},{80,48},{96,64},{112,144},{128,96},{144,112... | collective-permute-start | bytes 516104 | tf_op jit(solution)/shard_map/ppermute | solution.py:529
  58.0 10.5 %collective-permute-start.6 = (f32[624,128]{1,0:T(8,128)S(1)}, f32[624,128]{1,0:T(8,128)S(1)}, u32[]{:S(2)}, u32[]{:S(2)}) collective-permute-start(f32[624,128]{1,0:T(8,128)S(1)} %get-tuple-element.38), channel_id=1, source_target_pairs={{0,1},{1,2},{2,3},{3,4},{4,5},{5,6},{6,7},{7,8},{8,9},{9,10},{10,1... | collective-permute-start | bytes 958472 | tf_op jit(solution)/shard_map/ppermute | solution.py:502
  64.6 9.5 %collective-permute-start.7 = (f32[624,128]{1,0:T(8,128)S(1)}, f32[624,128]{1,0:T(8,128)S(1)}, u32[]{:S(2)}, u32[]{:S(2)}) collective-permute-start(f32[624,128]{1,0:T(8,128)S(1)} %get-tuple-element.39), channel_id=1, source_target_pairs={{1,0},{2,1},{3,2},{4,3},{5,4},{6,5},{7,6},{8,7},{9,8},{10,9},{11,1... | collective-permute-start | bytes 958472 | tf_op jit(solution)/shard_map/ppermute | solution.py:502
  78.3 6.2 %collective-permute-start.8 = (f32[4,16,128]{2,1,0:T(8,128)S(1)}, f32[4,16,128]{2,1,0:T(8,128)S(1)}, u32[]{:S(2)}, u32[]{:S(2)}) collective-permute-start(f32[4,16,128]{2,1,0:T(8,128)S(1)} %get-tuple-element.40), channel_id=1, source_target_pairs={{0,32},{16,48},{32,64},{48,80},{64,96},{80,112},{96,128},{112,144}... | collective-permute-start | bytes 98312 | tf_op jit(solution)/shard_map/ppermute | solution.py:502
  80.3 7.7 %collective-permute-start.9 = (f32[4,16,128]{2,1,0:T(8,128)S(1)}, f32[4,16,128]{2,1,0:T(8,128)S(1)}, u32[]{:S(2)}, u32[]{:S(2)}) collective-permute-start(f32[4,16,128]{2,1,0:T(8,128)S(1)} %get-tuple-element.42), channel_id=1, source_target_pairs={{32,0},{48,16},{64,32},{80,48},{96,64},{112,80},{128,96},{144,112}... | collective-permute-start | bytes 98312 | tf_op jit(solution)/shard_map/ppermute | solution.py:502
  88.0 4.8 %collective-permute-start.10 = (f32[16,8,128]{2,1,0:T(8,128)S(1)}, f32[16,8,128]{2,1,0:T(8,128)S(1)}, u32[]{:S(2)}, u32[]{:S(2)}) collective-permute-start(f32[16,8,128]{2,1,0:T(8,128)S(1)} %get-tuple-element.43), channel_id=1, source_target_pairs={{0,1},{1,2},{2,3},{3,4},{4,5},{5,6},{6,7},{7,8},{8,9},{9,10},{10,1... | collective-permute-start | bytes 196616 | tf_op jit(solution)/shard_map/ppermute | solution.py:502
  90.9 6.8 %collective-permute-start.11 = (f32[16,8,128]{2,1,0:T(8,128)S(1)}, f32[16,8,128]{2,1,0:T(8,128)S(1)}, u32[]{:S(2)}, u32[]{:S(2)}) collective-permute-start(f32[16,8,128]{2,1,0:T(8,128)S(1)} %get-tuple-element.44), channel_id=1, source_target_pairs={{1,0},{2,1},{3,2},{4,3},{5,4},{6,5},{7,6},{8,7},{9,8},{10,9},{11,1... | collective-permute-start | bytes 196616 | tf_op jit(solution)/shard_map/ppermute | solution.py:502

commit v4 on v3

--- a/solution.py
+++ b/solution.py
@@ -49,8 +49,8 @@
     return scaled
 
 
-def loop(low, high, body, width=2):
-    turns = (high - low) // width
+def loop(low, high, body, width=24):
+    turns = (high - low) // width if high - low > width else 0
 
     def step(t, carry):
         for j in range(width):
@@ -90,7 +90,7 @@
     return here, [q[z, i] - (6.0 * here[i] - total[i]) for i in range(len(here))]
 
 
-def smooth(w, q, low, high, n, masks, z_scale, passes, finish=None):
+def smooth(w, q, low, high, n, masks, z_scale, passes, finish=None, width=24):
     for turn in range(passes):
 
         def advance(z, turn=turn):
@@ -107,7 +107,7 @@
                 for i, value in enumerate(rest):
                     w[turn + 1][z, i] = c1 * here[i] + scales[i % n] * value
 
-        loop(low + 1 + turn, high - 1 - turn, advance)
+        loop(low + 1 + turn, high - 1 - turn, advance, width)
 
 
 def weave(source, z, k, blocks, n, x):
@@ -195,7 +195,7 @@
                 q[z, 4 * k + x] = value
                 w[0][z, 4 * k + x] = FIRST * value
 
-    loop(0, 24, begin)
+    loop(0, 24, begin, 8)
 
     place = 0
     for ref, first, count in ((low, 32, 20), (root, 0, 32), (high, 32, 20)):
@@ -214,8 +214,8 @@
             for x in range(4):
                 r[z, 4 * k + x] = weave(natural, z, k, 4, 4, x)
 
-    loop(0, 18, roots)
-    smooth(w, q, 0, 24, 4, masks, z_scale, DEGREE)
+    loop(0, 18, roots, 6)
+    smooth(w, q, 0, 24, 4, masks, z_scale, DEGREE, width=8)
 
     def total(z):
         for i in range(16):

time: 107 us -> 98.1 us (0.917)
  Pallas kernels: 19.2 us -> 10.6 us
    pallas_call x7, Pallas kernels: 19.2 us -> 10.6 us  [call(): pl.pallas_call(kernel, out_shape=[jax.ShapeDtypeStruct(s, F32) for s in o...]
where the time goes in v4:
time: 98.1 us; the launch traced here: 97.7 us
  waiting for transfers between devices  44.1 us (45%)
  starting transfers between devices  42.2 us (43%)
  Pallas kernels  10.6 us (11%)
    ppermute x10, waiting for transfers between devices, send(): return lax.ppermute(block, axis, pairs)  35.9 us
    ppermute x10, starting transfers between devices, send(): return lax.ppermute(block, axis, pairs)  33.7 us
    pallas_call x7, Pallas kernels, call(): pl.pallas_call(kernel, out_shape=[jax.ShapeDtypeStruct(s, F32) for s in o...  10.6 us
    ppermute x1, waiting for transfers between devices, on_device(): lax.ppermute(second, 'gz', pairs[1])  7.57 us
    ppermute x1, starting transfers between devices, on_device(): lax.ppermute(first, 'gz', pairs[0])  6.63 us
  transfers between devices with their start and end apart: 12, of which 10 were waited for; matrix products, arithmetic and copies ran while one was open for 0% of the time, Pallas kernels for 0%

profile of v4, /device:TPU:245, one launch (start us, length us, event | category | flops | bytes accessed | tf_op | source)
XLA Modules:
  0.0 97.7 jit_solution(16467045967990106130)
XLA Ops:
  0.6 1.7 %shard_map.50 = (f32[52,16,128]{2,1,0:T(8,128)S(1)}, f32[52,16,128]{2,1,0:T(8,128)S(1)}, f32[32,16,128]{2,1,0:T(8,128)S(1)}) custom-call(f32[8,16,512]{2,1,0:T(8,128)} %load_hbm.1, f32[8,16,512]{2,1,0:T(8,128)} %density_hbm.1, s32[1,2,64]{2,1,0:T(2,128)} %void_hbm.1), custom_call_target="tpu_custom_call" | custom-call | tf_op jit(solution)/shard_map/pallas_call | solution.py:489
  2.4 3.0 %collective-permute-start.1 = (f32[52,16,128]{2,1,0:T(8,128)S(1)}, f32[52,16,128]{2,1,0:T(8,128)S(1)}, u32[]{:S(2)}, u32[]{:S(2)}) collective-permute-start(f32[52,16,128]{2,1,0:T(8,128)S(1)} %get-tuple-element.29), channel_id=1, source_target_pairs={{16,0},{32,16},{48,32},{64,48},{80,64},{96,80},{112,96},{128,112},... | collective-permute-start | bytes 1277960 | tf_op jit(solution)/shard_map/ppermute | solution.py:502
  5.3 2.3 %collective-permute-start = (f32[52,16,128]{2,1,0:T(8,128)S(1)}, f32[52,16,128]{2,1,0:T(8,128)S(1)}, u32[]{:S(2)}, u32[]{:S(2)}) collective-permute-start(f32[52,16,128]{2,1,0:T(8,128)S(1)} %get-tuple-element.27.up.refs_1_), channel_id=1, source_target_pairs={{0,16},{16,32},{32,48},{48,64},{64,80},{80,96},{96,112},{112,128},... | collective-permute-start | bytes 1277960 | tf_op jit(solution)/shard_map/ppermute | solution.py:502
  7.7 7.3 %collective-permute-done.1.high.refs_3_ = f32[52,16,128]{2,1,0:T(8,128)S(1)} collective-permute-done((f32[52,16,128]{2,1,0:T(8,128)S(1)}, f32[52,16,128]{2,1,0:T(8,128)S(1)}, u32[]{:S(2)}, u32[]{:S(2)}) %collective-permute-start.1) | collective-permute-done | bytes 426016 | tf_op jit(solution)/shard_map/ppermute | solution.py:502
  14.9 2.6 %collective-permute-done.low.refs_0_ = f32[52,16,128]{2,1,0:T(8,128)S(1)} collective-permute-done((f32[52,16,128]{2,1,0:T(8,128)S(1)}, f32[52,16,128]{2,1,0:T(8,128)S(1)}, u32[]{:S(2)}, u32[]{:S(2)}) %collective-permute-start) | collective-permute-done | bytes 426016 | tf_op jit(solution)/shard_map/ppermute | solution.py:502
  17.6 0.1 shard_map.51
  17.7 7.0 %collective-permute-start.2 = (f32[1088,128]{1,0:T(8,128)S(1)}, f32[1088,128]{1,0:T(8,128)S(1)}, u32[]{:S(2)}, u32[]{:S(2)}) collective-permute-start(f32[1088,128]{1,0:T(8,128)S(1)} %get-tuple-element.30), channel_id=1, source_target_pairs={{0,1},{1,2},{2,3},{3,4},{4,5},{5,6},{6,7},{7,8},{8,9},{9,10},{10,1... | collective-permute-start | bytes 1671176 | tf_op jit(solution)/shard_map/ppermute | solution.py:502
  24.7 1.9 %collective-permute-start.3 = (f32[1088,128]{1,0:T(8,128)S(1)}, f32[1088,128]{1,0:T(8,128)S(1)}, u32[]{:S(2)}, u32[]{:S(2)}) collective-permute-start(f32[1088,128]{1,0:T(8,128)S(1)} %get-tuple-element.31), channel_id=1, source_target_pairs={{1,0},{2,1},{3,2},{4,3},{5,4},{6,5},{7,6},{8,7},{9,8},{10,9},{11,1... | collective-permute-start | bytes 1671176 | tf_op jit(solution)/shard_map/ppermute | solution.py:502
  26.6 4.5 %collective-permute-done.2.refs_4_ = f32[1088,128]{1,0:T(8,128)S(1)} collective-permute-done((f32[1088,128]{1,0:T(8,128)S(1)}, f32[1088,128]{1,0:T(8,128)S(1)}, u32[]{:S(2)}, u32[]{:S(2)}) %collective-permute-start.2) | collective-permute-done | bytes 557088 | tf_op jit(solution)/shard_map/ppermute | solution.py:502
  31.1 5.6 %collective-permute-done.3.refs_5_ = f32[1088,128]{1,0:T(8,128)S(1)} collective-permute-done((f32[1088,128]{1,0:T(8,128)S(1)}, f32[1088,128]{1,0:T(8,128)S(1)}, u32[]{:S(2)}, u32[]{:S(2)}) %collective-permute-start.3) | collective-permute-done | bytes 557088 | tf_op jit(solution)/shard_map/ppermute | solution.py:502
  36.7 2.9 %shard_map.52 = (f32[24,16,8,128]{3,2,1,0:T(8,128)S(1)}, f32[8,16,8,128]{3,2,1,0:T(8,128)S(1)}, f32[18,16,8,128]{3,2,1,0:T(8,128)S(1)}, f32[16,16,128]{2,1,0:T(8...) custom-call(f32[52,16,128]{2,1,0:T(8,128)S(1)} %collective-permute-done.low.refs_0_, ...), custom_call_target="tpu_custom_call" | custom-call | tf_op jit(solution)/shard_map/pallas_call | solution.py:489
  39.6 6.6 %collective-permute-start.4 = (f32[336,128]{1,0:T(8,128)S(1)}, f32[336,128]{1,0:T(8,128)S(1)}, u32[]{:S(2)}, u32[]{:S(2)}) collective-permute-start(f32[336,128]{1,0:T(8,128)S(1)} %get-tuple-element.32), channel_id=1, source_target_pairs={{0,32},{16,48},{32,64},{48,16},{64,96},{80,112},{96,128},{112,80},... | collective-permute-start | bytes 516104 | tf_op jit(solution)/shard_map/ppermute | solution.py:529
  46.2 1.9 %collective-permute-start.5 = (f32[336,128]{1,0:T(8,128)S(1)}, f32[336,128]{1,0:T(8,128)S(1)}, u32[]{:S(2)}, u32[]{:S(2)}) collective-permute-start(f32[336,128]{1,0:T(8,128)S(1)} %get-tuple-element.33), channel_id=1, source_target_pairs={{32,0},{48,80},{64,32},{80,48},{96,64},{112,144},{128,96},{144,112... | collective-permute-start | bytes 516104 | tf_op jit(solution)/shard_map/ppermute | solution.py:529
  48.2 0.6 collective-permute-done.4.refs_0_
  48.8 7.6 %collective-permute-done.5.refs_1_ = f32[336,128]{1,0:T(8,128)S(1)} collective-permute-done((f32[336,128]{1,0:T(8,128)S(1)}, f32[336,128]{1,0:T(8,128)S(1)}, u32[]{:S(2)}, u32[]{:S(2)}) %collective-permute-start.5) | collective-permute-done | bytes 172064 | tf_op jit(solution)/shard_map/ppermute | solution.py:529
  56.3 0.1 shard_map.53
  56.4 6.6 %collective-permute-start.6 = (f32[624,128]{1,0:T(8,128)S(1)}, f32[624,128]{1,0:T(8,128)S(1)}, u32[]{:S(2)}, u32[]{:S(2)}) collective-permute-start(f32[624,128]{1,0:T(8,128)S(1)} %get-tuple-element.38), channel_id=1, source_target_pairs={{0,1},{1,2},{2,3},{3,4},{4,5},{5,6},{6,7},{7,8},{8,9},{9,10},{10,1... | collective-permute-start | bytes 958472 | tf_op jit(solution)/shard_map/ppermute | solution.py:502
  63.0 1.9 %collective-permute-start.7 = (f32[624,128]{1,0:T(8,128)S(1)}, f32[624,128]{1,0:T(8,128)S(1)}, u32[]{:S(2)}, u32[]{:S(2)}) collective-permute-start(f32[624,128]{1,0:T(8,128)S(1)} %get-tuple-element.39), channel_id=1, source_target_pairs={{1,0},{2,1},{3,2},{4,3},{5,4},{6,5},{7,6},{8,7},{9,8},{10,9},{11,1... | collective-permute-start | bytes 958472 | tf_op jit(solution)/shard_map/ppermute | solution.py:502
  65.0 2.0 %collective-permute-done.6.refs_4_ = f32[624,128]{1,0:T(8,128)S(1)} collective-permute-done((f32[624,128]{1,0:T(8,128)S(1)}, f32[624,128]{1,0:T(8,128)S(1)}, u32[]{:S(2)}, u32[]{:S(2)}) %collective-permute-start.6) | collective-permute-done | bytes 319520 | tf_op jit(solution)/shard_map/ppermute | solution.py:502
  66.9 5.6 %collective-permute-done.7.refs_5_ = f32[624,128]{1,0:T(8,128)S(1)} collective-permute-done((f32[624,128]{1,0:T(8,128)S(1)}, f32[624,128]{1,0:T(8,128)S(1)}, u32[]{:S(2)}, u32[]{:S(2)}) %collective-permute-start.7) | collective-permute-done | bytes 319520 | tf_op jit(solution)/shard_map/ppermute | solution.py:502
  72.5 1.5 %shard_map.54 = (f32[24,8,8,128]{3,2,1,0:T(8,128)S(1)}, f32[10,8,8,128]{3,2,1,0:T(8,128)S(1)}, f32[20,8,8,128]{3,2,1,0:T(8,128)S(1)}, f32[8,16,128]{2,1,0:T(8,12...) custom-call(f32[336,128]{1,0:T(8,128)S(1)} %get-tuple-element.36.refs_0_, ...), custom_call_target="tpu_custom_call" | custom-call | tf_op jit(solution)/shard_map/pallas_call | solution.py:489
  74.1 1.9 %collective-permute-start.8 = (f32[4,16,128]{2,1,0:T(8,128)S(1)}, f32[4,16,128]{2,1,0:T(8,128)S(1)}, u32[]{:S(2)}, u32[]{:S(2)}) collective-permute-start(f32[4,16,128]{2,1,0:T(8,128)S(1)} %get-tuple-element.40), channel_id=1, source_target_pairs={{0,32},{16,48},{32,64},{48,80},{64,96},{80,112},{96,128},{112,144}... | collective-permute-start | bytes 98312 | tf_op jit(solution)/shard_map/ppermute | solution.py:502
  76.0 4.3 %collective-permute-start.9 = (f32[4,16,128]{2,1,0:T(8,128)S(1)}, f32[4,16,128]{2,1,0:T(8,128)S(1)}, u32[]{:S(2)}, u32[]{:S(2)}) collective-permute-start(f32[4,16,128]{2,1,0:T(8,128)S(1)} %get-tuple-element.42), channel_id=1, source_target_pairs={{32,0},{48,16},{64,32},{80,48},{96,64},{112,80},{128,96},{144,112}... | collective-permute-start | bytes 98312 | tf_op jit(solution)/shard_map/ppermute | solution.py:502
  80.3 0.0 collective-permute-done.8.refs_0_
  80.3 3.4 %collective-permute-done.9.refs_2_ = f32[4,16,128]{2,1,0:T(8,128)S(1)} collective-permute-done((f32[4,16,128]{2,1,0:T(8,128)S(1)}, f32[4,16,128]{2,1,0:T(8,128)S(1)}, u32[]{:S(2)}, u32[]{:S(2)}) %collective-permute-start.9) | collective-permute-done | bytes 32800 | tf_op jit(solution)/shard_map/ppermute | solution.py:502
  83.7 2.9 %collective-permute-start.10 = (f32[16,8,128]{2,1,0:T(8,128)S(1)}, f32[16,8,128]{2,1,0:T(8,128)S(1)}, u32[]{:S(2)}, u32[]{:S(2)}) collective-permute-start(f32[16,8,128]{2,1,0:T(8,128)S(1)} %get-tuple-element.43), channel_id=1, source_target_pairs={{0,1},{1,2},{2,3},{3,4},{4,5},{5,6},{6,7},{7,8},{8,9},{9,10},{10,1... | collective-permute-start | bytes 196616 | tf_op jit(solution)/shard_map/ppermute | solution.py:502
  86.6 1.9 %collective-permute-start.11 = (f32[16,8,128]{2,1,0:T(8,128)S(1)}, f32[16,8,128]{2,1,0:T(8,128)S(1)}, u32[]{:S(2)}, u32[]{:S(2)}) collective-permute-start(f32[16,8,128]{2,1,0:T(8,128)S(1)} %get-tuple-element.44), channel_id=1, source_target_pairs={{1,0},{2,1},{3,2},{4,3},{5,4},{6,5},{7,6},{8,7},{9,8},{10,9},{11,1... | collective-permute-start | bytes 196616 | tf_op jit(solution)/shard_map/ppermute | solution.py:502
  88.5 0.0 collective-permute-done.10.refs_3_
  88.5 4.9 %collective-permute-done.11.refs_4_ = f32[16,8,128]{2,1,0:T(8,128)S(1)} collective-permute-done((f32[16,8,128]{2,1,0:T(8,128)S(1)}, f32[16,8,128]{2,1,0:T(8,128)S(1)}, u32[]{:S(2)}, u32[]{:S(2)}) %collective-permute-start.11) | collective-permute-done | bytes 65568 | tf_op jit(solution)/shard_map/ppermute | solution.py:502
  93.4 4.3 %shard_map.56 = (f32[8,16,512]{2,1,0:T(8,128)}, f32[8,16,512]{2,1,0:T(8,128)}) custom-call(f32[4,16,128]{2,1,0:T(8,128)S(1)} %collective-permute-done.8.refs_0_, f32[8,16,128]{2,1,0:T(8,128)S(1)} %get-tuple-element.41.refs_1_, f32[4,16,128]{2,1,0:T(8,128)S(1)} %collective-permute-done.9.refs_2_, f32[16,8,128]{2,1,0:T(8,128)S(1)} %collective-permute-done.10.refs_3_, ...), custom_call_target="tpu_custom_call" | custom-call | tf_op jit(solution)/shard_map/pallas_call | solution.py:489
  (1 shorter events, 0.0 us)
Async XLA Ops:
  2.4 12.6 %collective-permute-start.1 = (f32[52,16,128]{2,1,0:T(8,128)S(1)}, f32[52,16,128]{2,1,0:T(8,128)S(1)}, u32[]{:S(2)}, u32[]{:S(2)}) collective-permute-start(f32[52,16,128]{2,1,0:T(8,128)S(1)} %get-tuple-element.29), channel_id=1, source_target_pairs={{16,0},{32,16},{48,32},{64,48},{80,64},{96,80},{112,96},{128,112},... | collective-permute-start | bytes 1277960 | tf_op jit(solution)/shard_map/ppermute | solution.py:502
  5.3 12.2 %collective-permute-start = (f32[52,16,128]{2,1,0:T(8,128)S(1)}, f32[52,16,128]{2,1,0:T(8,128)S(1)}, u32[]{:S(2)}, u32[]{:S(2)}) collective-permute-start(f32[52,16,128]{2,1,0:T(8,128)S(1)} %get-tuple-element.27.up.refs_1_), channel_id=1, source_target_pairs={{0,16},{16,32},{32,48},{48,64},{64,80},{80,96},{96,112},{112,128},... | collective-permute-start | bytes 1277960 | tf_op jit(solution)/shard_map/ppermute | solution.py:502
  17.7 13.4 %collective-permute-start.2 = (f32[1088,128]{1,0:T(8,128)S(1)}, f32[1088,128]{1,0:T(8,128)S(1)}, u32[]{:S(2)}, u32[]{:S(2)}) collective-permute-start(f32[1088,128]{1,0:T(8,128)S(1)} %get-tuple-element.30), channel_id=1, source_target_pairs={{0,1},{1,2},{2,3},{3,4},{4,5},{5,6},{6,7},{7,8},{8,9},{9,10},{10,1... | collective-permute-start | bytes 1671176 | tf_op jit(solution)/shard_map/ppermute | solution.py:502
  24.7 12.1 %collective-permute-start.3 = (f32[1088,128]{1,0:T(8,128)S(1)}, f32[1088,128]{1,0:T(8,128)S(1)}, u32[]{:S(2)}, u32[]{:S(2)}) collective-permute-start(f32[1088,128]{1,0:T(8,128)S(1)} %get-tuple-element.31), channel_id=1, source_target_pairs={{1,0},{2,1},{3,2},{4,3},{5,4},{6,5},{7,6},{8,7},{9,8},{10,9},{11,1... | collective-permute-start | bytes 1671176 | tf_op jit(solution)/shard_map/ppermute | solution.py:502
  39.6 9.2 %collective-permute-start.4 = (f32[336,128]{1,0:T(8,128)S(1)}, f32[336,128]{1,0:T(8,128)S(1)}, u32[]{:S(2)}, u32[]{:S(2)}) collective-permute-start(f32[336,128]{1,0:T(8,128)S(1)} %get-tuple-element.32), channel_id=1, source_target_pairs={{0,32},{16,48},{32,64},{48,16},{64,96},{80,112},{96,128},{112,80},... | collective-permute-start | bytes 516104 | tf_op jit(solution)/shard_map/ppermute | solution.py:529
  46.2 10.1 %collective-permute-start.5 = (f32[336,128]{1,0:T(8,128)S(1)}, f32[336,128]{1,0:T(8,128)S(1)}, u32[]{:S(2)}, u32[]{:S(2)}) collective-permute-start(f32[336,128]{1,0:T(8,128)S(1)} %get-tuple-element.33), channel_id=1, source_target_pairs={{32,0},{48,80},{64,32},{80,48},{96,64},{112,144},{128,96},{144,112... | collective-permute-start | bytes 516104 | tf_op jit(solution)/shard_map/ppermute | solution.py:529
  56.4 10.5 %collective-permute-start.6 = (f32[624,128]{1,0:T(8,128)S(1)}, f32[624,128]{1,0:T(8,128)S(1)}, u32[]{:S(2)}, u32[]{:S(2)}) collective-permute-start(f32[624,128]{1,0:T(8,128)S(1)} %get-tuple-element.38), channel_id=1, source_target_pairs={{0,1},{1,2},{2,3},{3,4},{4,5},{5,6},{6,7},{7,8},{8,9},{9,10},{10,1... | collective-permute-start | bytes 958472 | tf_op jit(solution)/shard_map/ppermute | solution.py:502
  63.0 9.5 %collective-permute-start.7 = (f32[624,128]{1,0:T(8,128)S(1)}, f32[624,128]{1,0:T(8,128)S(1)}, u32[]{:S(2)}, u32[]{:S(2)}) collective-permute-start(f32[624,128]{1,0:T(8,128)S(1)} %get-tuple-element.39), channel_id=1, source_target_pairs={{1,0},{2,1},{3,2},{4,3},{5,4},{6,5},{7,6},{8,7},{9,8},{10,9},{11,1... | collective-permute-start | bytes 958472 | tf_op jit(solution)/shard_map/ppermute | solution.py:502
  74.1 6.2 %collective-permute-start.8 = (f32[4,16,128]{2,1,0:T(8,128)S(1)}, f32[4,16,128]{2,1,0:T(8,128)S(1)}, u32[]{:S(2)}, u32[]{:S(2)}) collective-permute-start(f32[4,16,128]{2,1,0:T(8,128)S(1)} %get-tuple-element.40), channel_id=1, source_target_pairs={{0,32},{16,48},{32,64},{48,80},{64,96},{80,112},{96,128},{112,144}... | collective-permute-start | bytes 98312 | tf_op jit(solution)/shard_map/ppermute | solution.py:502
  76.0 7.7 %collective-permute-start.9 = (f32[4,16,128]{2,1,0:T(8,128)S(1)}, f32[4,16,128]{2,1,0:T(8,128)S(1)}, u32[]{:S(2)}, u32[]{:S(2)}) collective-permute-start(f32[4,16,128]{2,1,0:T(8,128)S(1)} %get-tuple-element.42), channel_id=1, source_target_pairs={{32,0},{48,16},{64,32},{80,48},{96,64},{112,80},{128,96},{144,112}... | collective-permute-start | bytes 98312 | tf_op jit(solution)/shard_map/ppermute | solution.py:502
  83.7 4.8 %collective-permute-start.10 = (f32[16,8,128]{2,1,0:T(8,128)S(1)}, f32[16,8,128]{2,1,0:T(8,128)S(1)}, u32[]{:S(2)}, u32[]{:S(2)}) collective-permute-start(f32[16,8,128]{2,1,0:T(8,128)S(1)} %get-tuple-element.43), channel_id=1, source_target_pairs={{0,1},{1,2},{2,3},{3,4},{4,5},{5,6},{6,7},{7,8},{8,9},{9,10},{10,1... | collective-permute-start | bytes 196616 | tf_op jit(solution)/shard_map/ppermute | solution.py:502
  86.6 6.8 %collective-permute-start.11 = (f32[16,8,128]{2,1,0:T(8,128)S(1)}, f32[16,8,128]{2,1,0:T(8,128)S(1)}, u32[]{:S(2)}, u32[]{:S(2)}) collective-permute-start(f32[16,8,128]{2,1,0:T(8,128)S(1)} %get-tuple-element.44), channel_id=1, source_target_pairs={{1,0},{2,1},{3,2},{4,3},{5,4},{6,5},{7,6},{8,7},{9,8},{10,9},{11,1... | collective-permute-start | bytes 196616 | tf_op jit(solution)/shard_map/ppermute | solution.py:502

commit v5 on v4

--- a/solution.py
+++ b/solution.py
@@ -31,6 +31,10 @@
 
 def iota(shape, dim):
     return lax.broadcasted_iota(jnp.int32, shape, dim)
+
+
+def inner(xy, count):
+    return jnp.where(xy > 0, F32(1.0), F32(0.0)), jnp.where(xy < count - 1, F32(1.0), F32(0.0))
 
 
 def row_masks(n, base, count):
@@ -178,15 +182,16 @@
 def fine_pre_kernel(counts, low, up, root, high, left, right, q, y, r, mid_q, mid_r, early, late, *scratch):
     natural, w = scratch[0], scratch[1:5]
     gz, xy = lax.axis_index("gz"), lax.axis_index("xy")
+    on_left, on_right = inner(xy, counts[1])
     masks = row_masks(4, 16 * xy - 8, 16 * counts[1])
     z_scale = z_mask(8 * gz - 8, 8 * counts[0])
 
     for n, ref in enumerate((low, up, high)):
         for i in range(32):
             j = 32 * n + i
-            natural[j, 0:8] = left[8 * j : 8 * j + 8]
+            natural[j, 0:8] = on_left * left[8 * j : 8 * j + 8]
             natural[j, 8:24] = ref[i]
-            natural[j, 24:32] = right[8 * j : 8 * j + 8]
+            natural[j, 24:32] = on_right * right[8 * j : 8 * j + 8]
 
     def begin(z):
         for k in range(4):
@@ -205,8 +210,8 @@
             natural[place, 24:32] = jnp.zeros((8, LANES), F32)
             if 4 <= place < 68:
                 j = 768 + 5 * (place - 4)
-                natural[place, 3:8] = left[j : j + 5]
-                natural[place, 24:29] = right[j : j + 5]
+                natural[place, 3:8] = on_left * left[j : j + 5]
+                natural[place, 24:29] = on_right * right[j : j + 5]
             place += 1
 
     def roots(z):
@@ -318,14 +323,15 @@
     q, y, r, coarse, coarse_low, coarse_high, coarse_root, natural = refs[:8]
     w = refs[8:]
     gz, xy = lax.axis_index("gz"), lax.axis_index("xy")
+    on_left, on_right = inner(xy, counts[1])
     masks = row_masks(4, 8 * xy - 10, 8 * counts[1])
     z_scale = z_mask(4 * gz - 10, 4 * counts[0])
     for z in range(24):
         for k in range(2):
             i = 2 * z + k
-            natural[i, 0:8] = left[8 * i : 8 * i + 8]
+            natural[i, 0:8] = on_left * left[8 * i : 8 * i + 8]
             natural[i, 8:20] = rows(0, z, k)
-            natural[i, 20:28] = right[8 * i : 8 * i + 8]
+            natural[i, 20:28] = on_right * right[8 * i : 8 * i + 8]
             natural[i, 28:32] = jnp.zeros((4, LANES), F32)
 
     def begin(z):
@@ -341,9 +347,9 @@
             i = 2 * z + k
             natural[i, 0:8] = jnp.zeros((8, LANES), F32)
             natural[i, 24:32] = jnp.zeros((8, LANES), F32)
-            natural[i, 2:8] = left[384 + 6 * i : 390 + 6 * i]
+            natural[i, 2:8] = on_left * left[384 + 6 * i : 390 + 6 * i]
             natural[i, 8:20] = rows(1, z + 2, k)
-            natural[i, 20:26] = right[384 + 6 * i : 390 + 6 * i]
+            natural[i, 20:26] = on_right * right[384 + 6 * i : 390 + 6 * i]
 
     def roots(z):
         for k in range(2):
@@ -394,12 +400,14 @@
     cw, mw, fw = refs[21:25], refs[25:29], refs[29:33]
     gz, xy = lax.axis_index("gz"), lax.axis_index("xy")
 
+    on_left, on_right = inner(xy, counts[1])
+
     at = 0
     for ref in parts:
         for k in range(ref.shape[0]):
-            natural[at, 0:4] = left[at, 2:6]
+            natural[at, 0:4] = on_left * left[at, 2:6]
             natural[at, 4:14] = ref[k, 2:12]
-            natural[at, 14:18] = right[at, 0:4]
+            natural[at, 14:18] = on_right * right[at, 0:4]
             natural[at, 18:24] = jnp.zeros((6, LANES), F32)
             for x in range(3):
                 value = weave(natural, at, 0, 1, 3, x)
@@ -502,6 +510,13 @@
     return lax.ppermute(block, axis, pairs)
 
 
+def turn(to_left, to_right):
+    count = lax.axis_size("xy")
+    left = lax.ppermute(to_right, "xy", [(i, (i + 1) % count) for i in range(count)])
+    right = lax.ppermute(to_left, "xy", [(i, (i - 1) % count) for i in range(count)])
+    return left, right
+
+
 def with_counts(kernel):
     counts = (lax.axis_size("gz"), lax.axis_size("xy"))
     return lambda *refs: kernel(counts, *refs)
@@ -517,7 +532,7 @@
     )
     low, high = send(up, "gz", 1), send(down, "gz", -1)
     to_left, to_right = call(fine_pack_kernel, (low, up, root, high), [(1088, LANES)] * 2)
-    left, right = send(to_right, "xy", 1), send(to_left, "xy", -1)
+    left, right = turn(to_left, to_right)
     fine = (24, 16, 8, LANES)
     fine_q, fine_y, fine_r, mid_q, mid_r, first, second = call(
         with_counts(fine_pre_kernel),
@@ -530,7 +545,7 @@
     low, high, to_left, to_right = call(
         with_counts(mid_pack_kernel), (first, second, mid_q, mid_r), [(336, LANES)] * 2 + [(624, LANES)] * 2
     )
-    left, right = send(to_right, "xy", 1), send(to_left, "xy", -1)
+    left, right = turn(to_left, to_right)
     mid = (24, 8, 8, LANES)
     mid_q, mid_y, mid_r, coarse, coarse_low, coarse_high, coarse_root = call(
         with_counts(mid_pre_kernel),
@@ -540,7 +555,7 @@
     )
     parts = (send(coarse_low, "gz", 2), coarse, send(coarse_high, "gz", -2))
     to_left, to_right = call(coarse_pack_kernel, parts, [(16, 8, LANES)] * 2)
-    left, right = send(to_right, "xy", 1), send(to_left, "xy", -1)
+    left, right = turn(to_left, to_right)
     coarsest = (16, 3, 8, LANES)
     return tuple(
         call(

time: 98.1 us -> 86.8 us (0.88)
  starting transfers between devices: 42.2 us -> 30.9 us
    ppermute x0 -> x6, waiting for transfers between devices: none -> 22.7 us  [the longest x3 11.7 us: turn(): lax.ppermute(to_right, 'xy', [(i, (i + 1) % count) for i in range(count)])]
    ppermute x10 -> x4, waiting for transfers between devices: 35.9 us -> 13.3 us  [send(): return lax.ppermute(block, axis, pairs)]
    ppermute x10 -> x4, starting transfers between devices: 33.7 us -> 11.5 us  [send(): return lax.ppermute(block, axis, pairs)]
    ppermute x0 -> x6, starting transfers between devices: none -> 10.9 us  [the longest x3 10.9 us: turn(): lax.ppermute(to_right, 'xy', [(i, (i + 1) % count) for i in range(count)])]
  transfers between devices with their start and end apart: 12 -> 12, of which waited for: 10 -> 11; matrix products, arithmetic and copies ran while one was open for 0% -> 0% of each run, Pallas kernels for 0% -> 0%
where the time goes in v5:
time: 86.8 us; the launch traced here: 86.5 us
  waiting for transfers between devices  44.2 us (51%)
  starting transfers between devices  30.9 us (36%)
  Pallas kernels  10.7 us (12%)
    ppermute x4, waiting for transfers between devices, send(): return lax.ppermute(block, axis, pairs)  13.3 us
    ppermute x3, waiting for transfers between devices, turn(): lax.ppermute(to_right, 'xy', [(i, (i + 1) % count) for i in range(count)])  11.7 us
    ppermute x4, starting transfers between devices, send(): return lax.ppermute(block, axis, pairs)  11.5 us
    ppermute x3, waiting for transfers between devices, turn(): lax.ppermute(to_left, 'xy', [(i, (i - 1) % count) for i in range(count)])  10.9 us
    ppermute x3, starting transfers between devices, turn(): lax.ppermute(to_right, 'xy', [(i, (i + 1) % count) for i in range(count)])  10.9 us
    pallas_call x7, Pallas kernels, call(): pl.pallas_call(kernel, out_shape=[jax.ShapeDtypeStruct(s, F32) for s in o...  10.7 us
    ppermute x1, waiting for transfers between devices, on_device(): lax.ppermute(second, 'gz', pairs[1])  7.44 us
    ppermute x1, starting transfers between devices, on_device(): lax.ppermute(first, 'gz', pairs[0])  6.63 us
  transfers between devices with their start and end apart: 12, of which 11 were waited for; matrix products, arithmetic and copies ran while one was open for 0% of the time, Pallas kernels for 0%

profile of v5, /device:TPU:245, one launch (start us, length us, event | category | flops | bytes accessed | tf_op | source)
XLA Modules:
  0.0 86.5 jit_solution(2467881751563383473)
XLA Ops:
  0.6 1.7 %shard_map.50 = (f32[52,16,128]{2,1,0:T(8,128)S(1)}, f32[52,16,128]{2,1,0:T(8,128)S(1)}, f32[32,16,128]{2,1,0:T(8,128)S(1)}) custom-call(f32[8,16,512]{2,1,0:T(8,128)} %load_hbm.1, f32[8,16,512]{2,1,0:T(8,128)} %density_hbm.1, s32[1,2,64]{2,1,0:T(2,128)} %void_hbm.1), custom_call_target="tpu_custom_call" | custom-call | tf_op jit(solution)/shard_map/pallas_call | solution.py:497
  2.4 3.0 %collective-permute-start.1 = (f32[52,16,128]{2,1,0:T(8,128)S(1)}, f32[52,16,128]{2,1,0:T(8,128)S(1)}, u32[]{:S(2)}, u32[]{:S(2)}) collective-permute-start(f32[52,16,128]{2,1,0:T(8,128)S(1)} %get-tuple-element.29), channel_id=1, source_target_pairs={{16,0},{32,16},{48,32},{64,48},{80,64},{96,80},{112,96},{128,112},... | collective-permute-start | bytes 1277960 | tf_op jit(solution)/shard_map/ppermute | solution.py:510
  5.3 2.3 %collective-permute-start = (f32[52,16,128]{2,1,0:T(8,128)S(1)}, f32[52,16,128]{2,1,0:T(8,128)S(1)}, u32[]{:S(2)}, u32[]{:S(2)}) collective-permute-start(f32[52,16,128]{2,1,0:T(8,128)S(1)} %get-tuple-element.27.up.refs_1_), channel_id=1, source_target_pairs={{0,16},{16,32},{32,48},{48,64},{64,80},{80,96},{96,112},{112,128},... | collective-permute-start | bytes 1277960 | tf_op jit(solution)/shard_map/ppermute | solution.py:510
  7.7 7.3 %collective-permute-done.1.high.refs_3_ = f32[52,16,128]{2,1,0:T(8,128)S(1)} collective-permute-done((f32[52,16,128]{2,1,0:T(8,128)S(1)}, f32[52,16,128]{2,1,0:T(8,128)S(1)}, u32[]{:S(2)}, u32[]{:S(2)}) %collective-permute-start.1) | collective-permute-done | bytes 426016 | tf_op jit(solution)/shard_map/ppermute | solution.py:510
  14.9 2.6 %collective-permute-done.low.refs_0_ = f32[52,16,128]{2,1,0:T(8,128)S(1)} collective-permute-done((f32[52,16,128]{2,1,0:T(8,128)S(1)}, f32[52,16,128]{2,1,0:T(8,128)S(1)}, u32[]{:S(2)}, u32[]{:S(2)}) %collective-permute-start) | collective-permute-done | bytes 426016 | tf_op jit(solution)/shard_map/ppermute | solution.py:510
  17.6 0.1 shard_map.51
  17.7 5.1 %collective-permute-start.2 = (f32[1088,128]{1,0:T(8,128)S(1)}, f32[1088,128]{1,0:T(8,128)S(1)}, u32[]{:S(2)}, u32[]{:S(2)}) collective-permute-start(f32[1088,128]{1,0:T(8,128)S(1)} %get-tuple-element.30), channel_id=1, source_target_pairs={{0,1},{1,2},{2,3},{3,4},{4,5},{5,6},{6,7},{7,8},{8,9},{9,10},{10,1... | collective-permute-start | bytes 1671176 | tf_op jit(solution)/shard_map/ppermute | solution.py:515
  22.8 0.0 collective-permute-start.3
  22.8 6.5 %collective-permute-done.2.refs_4_ = f32[1088,128]{1,0:T(8,128)S(1)} collective-permute-done((f32[1088,128]{1,0:T(8,128)S(1)}, f32[1088,128]{1,0:T(8,128)S(1)}, u32[]{:S(2)}, u32[]{:S(2)}) %collective-permute-start.2) | collective-permute-done | bytes 557088 | tf_op jit(solution)/shard_map/ppermute | solution.py:515
  29.2 3.7 %collective-permute-done.3.refs_5_ = f32[1088,128]{1,0:T(8,128)S(1)} collective-permute-done((f32[1088,128]{1,0:T(8,128)S(1)}, f32[1088,128]{1,0:T(8,128)S(1)}, u32[]{:S(2)}, u32[]{:S(2)}) %collective-permute-start.3) | collective-permute-done | bytes 557088 | tf_op jit(solution)/shard_map/ppermute | solution.py:516
  32.9 2.9 %shard_map.52 = (f32[24,16,8,128]{3,2,1,0:T(8,128)S(1)}, f32[8,16,8,128]{3,2,1,0:T(8,128)S(1)}, f32[18,16,8,128]{3,2,1,0:T(8,128)S(1)}, f32[16,16,128]{2,1,0:T(8...) custom-call(f32[52,16,128]{2,1,0:T(8,128)S(1)} %collective-permute-done.low.refs_0_, ...), custom_call_target="tpu_custom_call" | custom-call | tf_op jit(solution)/shard_map/pallas_call | solution.py:497
  35.8 6.6 %collective-permute-start.4 = (f32[336,128]{1,0:T(8,128)S(1)}, f32[336,128]{1,0:T(8,128)S(1)}, u32[]{:S(2)}, u32[]{:S(2)}) collective-permute-start(f32[336,128]{1,0:T(8,128)S(1)} %get-tuple-element.32), channel_id=1, source_target_pairs={{0,32},{16,48},{32,64},{48,16},{64,96},{80,112},{96,128},{112,80},... | collective-permute-start | bytes 516104 | tf_op jit(solution)/shard_map/ppermute | solution.py:544
  42.4 1.9 %collective-permute-start.5 = (f32[336,128]{1,0:T(8,128)S(1)}, f32[336,128]{1,0:T(8,128)S(1)}, u32[]{:S(2)}, u32[]{:S(2)}) collective-permute-start(f32[336,128]{1,0:T(8,128)S(1)} %get-tuple-element.33), channel_id=1, source_target_pairs={{32,0},{48,80},{64,32},{80,48},{96,64},{112,144},{128,96},{144,112... | collective-permute-start | bytes 516104 | tf_op jit(solution)/shard_map/ppermute | solution.py:544
  44.4 0.8 collective-permute-done.4.refs_0_
  45.1 7.4 %collective-permute-done.5.refs_1_ = f32[336,128]{1,0:T(8,128)S(1)} collective-permute-done((f32[336,128]{1,0:T(8,128)S(1)}, f32[336,128]{1,0:T(8,128)S(1)}, u32[]{:S(2)}, u32[]{:S(2)}) %collective-permute-start.5) | collective-permute-done | bytes 172064 | tf_op jit(solution)/shard_map/ppermute | solution.py:544
  52.6 0.1 shard_map.53
  52.7 4.7 %collective-permute-start.6 = (f32[624,128]{1,0:T(8,128)S(1)}, f32[624,128]{1,0:T(8,128)S(1)}, u32[]{:S(2)}, u32[]{:S(2)}) collective-permute-start(f32[624,128]{1,0:T(8,128)S(1)} %get-tuple-element.38), channel_id=1, source_target_pairs={{0,1},{1,2},{2,3},{3,4},{4,5},{5,6},{6,7},{7,8},{8,9},{9,10},{10,1... | collective-permute-start | bytes 958472 | tf_op jit(solution)/shard_map/ppermute | solution.py:515
  57.3 0.0 collective-permute-start.7
  57.3 3.9 %collective-permute-done.6.refs_4_ = f32[624,128]{1,0:T(8,128)S(1)} collective-permute-done((f32[624,128]{1,0:T(8,128)S(1)}, f32[624,128]{1,0:T(8,128)S(1)}, u32[]{:S(2)}, u32[]{:S(2)}) %collective-permute-start.6) | collective-permute-done | bytes 319520 | tf_op jit(solution)/shard_map/ppermute | solution.py:515
  61.3 3.7 %collective-permute-done.7.refs_5_ = f32[624,128]{1,0:T(8,128)S(1)} collective-permute-done((f32[624,128]{1,0:T(8,128)S(1)}, f32[624,128]{1,0:T(8,128)S(1)}, u32[]{:S(2)}, u32[]{:S(2)}) %collective-permute-start.7) | collective-permute-done | bytes 319520 | tf_op jit(solution)/shard_map/ppermute | solution.py:516
  65.0 1.5 %shard_map.54 = (f32[24,8,8,128]{3,2,1,0:T(8,128)S(1)}, f32[10,8,8,128]{3,2,1,0:T(8,128)S(1)}, f32[20,8,8,128]{3,2,1,0:T(8,128)S(1)}, f32[8,16,128]{2,1,0:T(8,12...) custom-call(f32[336,128]{1,0:T(8,128)S(1)} %get-tuple-element.36.refs_0_, ...), custom_call_target="tpu_custom_call" | custom-call | tf_op jit(solution)/shard_map/pallas_call | solution.py:497
  66.5 1.9 %collective-permute-start.8 = (f32[4,16,128]{2,1,0:T(8,128)S(1)}, f32[4,16,128]{2,1,0:T(8,128)S(1)}, u32[]{:S(2)}, u32[]{:S(2)}) collective-permute-start(f32[4,16,128]{2,1,0:T(8,128)S(1)} %get-tuple-element.40), channel_id=1, source_target_pairs={{0,32},{16,48},{32,64},{48,80},{64,96},{80,112},{96,128},{112,144}... | collective-permute-start | bytes 98312 | tf_op jit(solution)/shard_map/ppermute | solution.py:510
  68.4 4.3 %collective-permute-start.9 = (f32[4,16,128]{2,1,0:T(8,128)S(1)}, f32[4,16,128]{2,1,0:T(8,128)S(1)}, u32[]{:S(2)}, u32[]{:S(2)}) collective-permute-start(f32[4,16,128]{2,1,0:T(8,128)S(1)} %get-tuple-element.42), channel_id=1, source_target_pairs={{32,0},{48,16},{64,32},{80,48},{96,64},{112,80},{128,96},{144,112}... | collective-permute-start | bytes 98312 | tf_op jit(solution)/shard_map/ppermute | solution.py:510
  72.7 0.0 collective-permute-done.8.refs_0_
  72.7 3.4 %collective-permute-done.9.refs_2_ = f32[4,16,128]{2,1,0:T(8,128)S(1)} collective-permute-done((f32[4,16,128]{2,1,0:T(8,128)S(1)}, f32[4,16,128]{2,1,0:T(8,128)S(1)}, u32[]{:S(2)}, u32[]{:S(2)}) %collective-permute-start.9) | collective-permute-done | bytes 32800 | tf_op jit(solution)/shard_map/ppermute | solution.py:510
  76.1 1.2 %collective-permute-start.10 = (f32[16,8,128]{2,1,0:T(8,128)S(1)}, f32[16,8,128]{2,1,0:T(8,128)S(1)}, u32[]{:S(2)}, u32[]{:S(2)}) collective-permute-start(f32[16,8,128]{2,1,0:T(8,128)S(1)} %get-tuple-element.43), channel_id=1, source_target_pairs={{0,1},{1,2},{2,3},{3,4},{4,5},{5,6},{6,7},{7,8},{8,9},{9,10},{10,1... | collective-permute-start | bytes 196616 | tf_op jit(solution)/shard_map/ppermute | solution.py:515
  77.3 0.0 collective-permute-start.11
  77.3 1.3 %collective-permute-done.10.refs_3_ = f32[16,8,128]{2,1,0:T(8,128)S(1)} collective-permute-done((f32[16,8,128]{2,1,0:T(8,128)S(1)}, f32[16,8,128]{2,1,0:T(8,128)S(1)}, u32[]{:S(2)}, u32[]{:S(2)}) %collective-permute-start.10) | collective-permute-done | bytes 65568 | tf_op jit(solution)/shard_map/ppermute | solution.py:515
  78.6 3.6 %collective-permute-done.11.refs_4_ = f32[16,8,128]{2,1,0:T(8,128)S(1)} collective-permute-done((f32[16,8,128]{2,1,0:T(8,128)S(1)}, f32[16,8,128]{2,1,0:T(8,128)S(1)}, u32[]{:S(2)}, u32[]{:S(2)}) %collective-permute-start.11) | collective-permute-done | bytes 65568 | tf_op jit(solution)/shard_map/ppermute | solution.py:516
  82.2 4.3 %shard_map.56 = (f32[8,16,512]{2,1,0:T(8,128)}, f32[8,16,512]{2,1,0:T(8,128)}) custom-call(f32[4,16,128]{2,1,0:T(8,128)S(1)} %collective-permute-done.8.refs_0_, f32[8,16,128]{2,1,0:T(8,128)S(1)} %get-tuple-element.41.refs_1_, f32[4,16,128]{2,1,0:T(8,128)S(1)} %collective-permute-done.9.refs_2_, f32[16,8,128]{2,1,0:T(8,128)S(1)} %collective-permute-done.10.refs_3_, ...), custom_call_target="tpu_custom_call" | custom-call | tf_op jit(solution)/shard_map/pallas_call | solution.py:497
  (1 shorter events, 0.0 us)
Async XLA Ops:
  2.4 12.6 %collective-permute-start.1 = (f32[52,16,128]{2,1,0:T(8,128)S(1)}, f32[52,16,128]{2,1,0:T(8,128)S(1)}, u32[]{:S(2)}, u32[]{:S(2)}) collective-permute-start(f32[52,16,128]{2,1,0:T(8,128)S(1)} %get-tuple-element.29), channel_id=1, source_target_pairs={{16,0},{32,16},{48,32},{64,48},{80,64},{96,80},{112,96},{128,112},... | collective-permute-start | bytes 1277960 | tf_op jit(solution)/shard_map/ppermute | solution.py:510
  5.3 12.2 %collective-permute-start = (f32[52,16,128]{2,1,0:T(8,128)S(1)}, f32[52,16,128]{2,1,0:T(8,128)S(1)}, u32[]{:S(2)}, u32[]{:S(2)}) collective-permute-start(f32[52,16,128]{2,1,0:T(8,128)S(1)} %get-tuple-element.27.up.refs_1_), channel_id=1, source_target_pairs={{0,16},{16,32},{32,48},{48,64},{64,80},{80,96},{96,112},{112,128},... | collective-permute-start | bytes 1277960 | tf_op jit(solution)/shard_map/ppermute | solution.py:510
  17.7 11.5 %collective-permute-start.2 = (f32[1088,128]{1,0:T(8,128)S(1)}, f32[1088,128]{1,0:T(8,128)S(1)}, u32[]{:S(2)}, u32[]{:S(2)}) collective-permute-start(f32[1088,128]{1,0:T(8,128)S(1)} %get-tuple-element.30), channel_id=1, source_target_pairs={{0,1},{1,2},{2,3},{3,4},{4,5},{5,6},{6,7},{7,8},{8,9},{9,10},{10,1... | collective-permute-start | bytes 1671176 | tf_op jit(solution)/shard_map/ppermute | solution.py:515
  22.8 10.2 %collective-permute-start.3 = (f32[1088,128]{1,0:T(8,128)S(1)}, f32[1088,128]{1,0:T(8,128)S(1)}, u32[]{:S(2)}, u32[]{:S(2)}) collective-permute-start(f32[1088,128]{1,0:T(8,128)S(1)} %get-tuple-element.31), channel_id=1, source_target_pairs={{0,15},{1,0},{2,1},{3,2},{4,3},{5,4},{6,5},{7,6},{8,7},{9,8},{10,9... | collective-permute-start | bytes 1671176 | tf_op jit(solution)/shard_map/ppermute | solution.py:516
  35.8 9.3 %collective-permute-start.4 = (f32[336,128]{1,0:T(8,128)S(1)}, f32[336,128]{1,0:T(8,128)S(1)}, u32[]{:S(2)}, u32[]{:S(2)}) collective-permute-start(f32[336,128]{1,0:T(8,128)S(1)} %get-tuple-element.32), channel_id=1, source_target_pairs={{0,32},{16,48},{32,64},{48,16},{64,96},{80,112},{96,128},{112,80},... | collective-permute-start | bytes 516104 | tf_op jit(solution)/shard_map/ppermute | solution.py:544
  42.4 10.1 %collective-permute-start.5 = (f32[336,128]{1,0:T(8,128)S(1)}, f32[336,128]{1,0:T(8,128)S(1)}, u32[]{:S(2)}, u32[]{:S(2)}) collective-permute-start(f32[336,128]{1,0:T(8,128)S(1)} %get-tuple-element.33), channel_id=1, source_target_pairs={{32,0},{48,80},{64,32},{80,48},{96,64},{112,144},{128,96},{144,112... | collective-permute-start | bytes 516104 | tf_op jit(solution)/shard_map/ppermute | solution.py:544
  52.7 8.6 %collective-permute-start.6 = (f32[624,128]{1,0:T(8,128)S(1)}, f32[624,128]{1,0:T(8,128)S(1)}, u32[]{:S(2)}, u32[]{:S(2)}) collective-permute-start(f32[624,128]{1,0:T(8,128)S(1)} %get-tuple-element.38), channel_id=1, source_target_pairs={{0,1},{1,2},{2,3},{3,4},{4,5},{5,6},{6,7},{7,8},{8,9},{9,10},{10,1... | collective-permute-start | bytes 958472 | tf_op jit(solution)/shard_map/ppermute | solution.py:515
  57.3 7.6 %collective-permute-start.7 = (f32[624,128]{1,0:T(8,128)S(1)}, f32[624,128]{1,0:T(8,128)S(1)}, u32[]{:S(2)}, u32[]{:S(2)}) collective-permute-start(f32[624,128]{1,0:T(8,128)S(1)} %get-tuple-element.39), channel_id=1, source_target_pairs={{0,15},{1,0},{2,1},{3,2},{4,3},{5,4},{6,5},{7,6},{8,7},{9,8},{10,9... | collective-permute-start | bytes 958472 | tf_op jit(solution)/shard_map/ppermute | solution.py:516
  66.5 6.2 %collective-permute-start.8 = (f32[4,16,128]{2,1,0:T(8,128)S(1)}, f32[4,16,128]{2,1,0:T(8,128)S(1)}, u32[]{:S(2)}, u32[]{:S(2)}) collective-permute-start(f32[4,16,128]{2,1,0:T(8,128)S(1)} %get-tuple-element.40), channel_id=1, source_target_pairs={{0,32},{16,48},{32,64},{48,80},{64,96},{80,112},{96,128},{112,144}... | collective-permute-start | bytes 98312 | tf_op jit(solution)/shard_map/ppermute | solution.py:510
  68.4 7.7 %collective-permute-start.9 = (f32[4,16,128]{2,1,0:T(8,128)S(1)}, f32[4,16,128]{2,1,0:T(8,128)S(1)}, u32[]{:S(2)}, u32[]{:S(2)}) collective-permute-start(f32[4,16,128]{2,1,0:T(8,128)S(1)} %get-tuple-element.42), channel_id=1, source_target_pairs={{32,0},{48,16},{64,32},{80,48},{96,64},{112,80},{128,96},{144,112}... | collective-permute-start | bytes 98312 | tf_op jit(solution)/shard_map/ppermute | solution.py:510
  76.1 2.5 %collective-permute-start.10 = (f32[16,8,128]{2,1,0:T(8,128)S(1)}, f32[16,8,128]{2,1,0:T(8,128)S(1)}, u32[]{:S(2)}, u32[]{:S(2)}) collective-permute-start(f32[16,8,128]{2,1,0:T(8,128)S(1)} %get-tuple-element.43), channel_id=1, source_target_pairs={{0,1},{1,2},{2,3},{3,4},{4,5},{5,6},{6,7},{7,8},{8,9},{9,10},{10,1... | collective-permute-start | bytes 196616 | tf_op jit(solution)/shard_map/ppermute | solution.py:515
  77.3 4.9 %collective-permute-start.11 = (f32[16,8,128]{2,1,0:T(8,128)S(1)}, f32[16,8,128]{2,1,0:T(8,128)S(1)}, u32[]{:S(2)}, u32[]{:S(2)}) collective-permute-start(f32[16,8,128]{2,1,0:T(8,128)S(1)} %get-tuple-element.44), channel_id=1, source_target_pairs={{0,15},{1,0},{2,1},{3,2},{4,3},{5,4},{6,5},{7,6},{8,7},{9,8},{10,9... | collective-permute-start | bytes 196616 | tf_op jit(solution)/shard_map/ppermute | solution.py:516

commit v6 on v5

--- a/solution.py
+++ b/solution.py
@@ -133,7 +133,30 @@
     return jnp.where(same, 1.0, 0.0).astype(jnp.bfloat16)
 
 
-def scale_kernel(load_hbm, density_hbm, void_hbm, up, down, root, both, void, sems):
+CORNER = [8, 8, 8, 8, 7, 6, 5, 4]
+
+
+def corner_plan(blocks, first, last, rows):
+    plan, at = [], 0
+    for side in range(2):
+        for layer in range(8):
+            away = 8 - layer if side == 0 else layer + 1
+            if not first <= away <= last:
+                continue
+            for k in range(blocks):
+                count = rows if rows else CORNER[away - 1]
+                plan.append((side, layer, k, count, at))
+                at += count
+    return plan, at
+
+
+FINE_Q, FINE_Q_ROWS = corner_plan(4, 1, 8, 0)
+FINE_R, FINE_R_ROWS = corner_plan(4, 1, 4, 4)
+MID_Q, MID_Q_ROWS = corner_plan(2, 1, 8, 0)
+MID_R, MID_R_ROWS = corner_plan(2, 1, 6, 6)
+
+
+def scale_kernel(load_hbm, density_hbm, void_hbm, up, down, root, left, right, both, void, sems):
     copies = [
         pltpu.make_async_copy(load_hbm, both.at[pl.ds(0, 8)], sems.at[0]),
         pltpu.make_async_copy(density_hbm, both.at[pl.ds(8, 8)], sems.at[1]),
@@ -159,39 +182,52 @@
             up[4 * z + k] = q
             down[4 * z + k] = q
             root[4 * z + k] = r
+            i = 4 * z + k
+            left[8 * i : 8 * i + 8] = q[0:8]
+            right[8 * i : 8 * i + 8] = q[8:16]
+            left[256 + 5 * i : 261 + 5 * i] = r[0:5]
+            right[256 + 5 * i : 261 + 5 * i] = r[11:16]
             if z >= 3:
                 up[4 * (5 + z) + k] = r
             if z < 5:
                 down[4 * (8 + z) + k] = r
 
 
-def fine_pack_kernel(low, up, root, high, left, right):
-    at = 0
-    for ref in (low, up, high):
-        for i in range(32):
-            left[at : at + 8] = ref[i, 0:8]
-            right[at : at + 8] = ref[i, 8:16]
-            at += 8
-    for ref, first, count in ((low, 36, 16), (root, 0, 32), (high, 32, 16)):
-        for i in range(first, first + count):
-            left[at : at + 5] = ref[i, 0:5]
-            right[at : at + 5] = ref[i, 11:16]
-            at += 5
-
-
-def fine_pre_kernel(counts, low, up, root, high, left, right, q, y, r, mid_q, mid_r, early, late, *scratch):
+def fine_pack_kernel(low, high, left, right):
+    for side, layer, k, n, at in FINE_Q:
+        ref, i = (low, high)[side], 4 * layer + k
+        left[at : at + n] = ref[i, 0:n]
+        right[at : at + n] = ref[i, 16 - n : 16]
+    for side, layer, k, n, at in FINE_R:
+        ref, i = (low, high)[side], 32 + 4 * (layer - 3 if side == 0 else layer) + k
+        at += FINE_Q_ROWS
+        left[at : at + n] = ref[i, 0:n]
+        right[at : at + n] = ref[i, 16 - n : 16]
+
+
+def fine_pre_kernel(
+    counts, low, up, root, high, left, right, far_left, far_right, q, y, r, mid_q, mid_r, early, late, mid_left, mid_right, *scratch
+):
     natural, w = scratch[0], scratch[1:5]
     gz, xy = lax.axis_index("gz"), lax.axis_index("xy")
     on_left, on_right = inner(xy, counts[1])
     masks = row_masks(4, 16 * xy - 8, 16 * counts[1])
     z_scale = z_mask(8 * gz - 8, 8 * counts[0])
 
+    blank = jnp.zeros((8, LANES), F32)
     for n, ref in enumerate((low, up, high)):
         for i in range(32):
-            j = 32 * n + i
-            natural[j, 0:8] = on_left * left[8 * j : 8 * j + 8]
-            natural[j, 8:24] = ref[i]
-            natural[j, 24:32] = on_right * right[8 * j : 8 * j + 8]
+            natural[32 * n + i, 8:24] = ref[i]
+    for i in range(32):
+        natural[32 + i, 0:8] = on_left * left[8 * i : 8 * i + 8]
+        natural[32 + i, 24:32] = on_right * right[8 * i : 8 * i + 8]
+    for side, layer, k, n, at in FINE_Q:
+        j = 64 * side + 4 * layer + k
+        if n < 8:
+            natural[j, 0:8] = blank
+            natural[j, 24:32] = blank
+        natural[j, 8 - n : 8] = on_left * far_left[at : at + n]
+        natural[j, 24 : 24 + n] = on_right * far_right[at : at + n]
 
     def begin(z):
         for k in range(4):
@@ -205,14 +241,18 @@
     place = 0
     for ref, first, count in ((low, 32, 20), (root, 0, 32), (high, 32, 20)):
         for i in range(first, first + count):
-            natural[place, 0:8] = jnp.zeros((8, LANES), F32)
+            natural[place, 0:8] = blank
             natural[place, 8:24] = ref[i]
-            natural[place, 24:32] = jnp.zeros((8, LANES), F32)
-            if 4 <= place < 68:
-                j = 768 + 5 * (place - 4)
-                natural[place, 3:8] = on_left * left[j : j + 5]
-                natural[place, 24:29] = on_right * right[j : j + 5]
+            natural[place, 24:32] = blank
             place += 1
+    for i in range(32):
+        natural[20 + i, 3:8] = on_left * left[256 + 5 * i : 261 + 5 * i]
+        natural[20 + i, 24:29] = on_right * right[256 + 5 * i : 261 + 5 * i]
+    for side, layer, k, n, at in FINE_R:
+        j = 4 * (layer - 3 if side == 0 else 13 + layer) + k
+        at += FINE_Q_ROWS
+        natural[j, 8 - n : 8] = on_left * far_left[at : at + n]
+        natural[j, 24 : 24 + n] = on_right * far_right[at : at + n]
 
     def roots(z):
         for k in range(4):
@@ -249,6 +289,11 @@
             out[12 * i : 12 * i + 12] = mid_q[i, 2:14]
         for i in range(12):
             out[192 + 12 * i : 204 + 12 * i] = mid_r[2 * start + i, 2:14]
+    for i in range(16):
+        mid_right[8 * i : 8 * i + 8] = mid_q[i, 2:10]
+        mid_left[8 * i : 8 * i + 8] = mid_q[i, 6:14]
+        mid_right[128 + 6 * i : 134 + 6 * i] = mid_r[i, 4:10]
+        mid_left[128 + 6 * i : 134 + 6 * i] = mid_r[i, 6:12]
 
 
 def mid_pairs(count):
@@ -288,51 +333,42 @@
         high[288:336] = jnp.zeros((48, LANES), F32)
 
 
-def mid_parts(low, high, mid_q, mid_r):
-    def rows(field, z, k):
-        if 8 <= z < 16:
-            return (mid_q, mid_r)[field][2 * (z - 8) + k, 2:14]
-        at = 12 * (2 * (z if z < 8 else z - 16) + k)
-        if field == 1:
-            at = at + (192 if z >= 16 else 144)
-        return (low if z < 8 else high)[at : at + 12]
-
-    return rows
-
-
-def mid_pack_kernel(counts, first, second, mid_q, mid_r, low, high, left, right):
+def mid_rows(low, high, field, side, layer, k, start, stop):
+    at = 12 * (2 * layer + k) + (0 if field == 0 else 144 if side == 0 else 192)
+    return (low, high)[side][at + start : at + stop]
+
+
+def mid_pack_kernel(counts, first, second, low, high, left, right):
     mid_sides(counts[0], lax.axis_index("gz"), first, second, low, high)
-    rows = mid_parts(low, high, mid_q, mid_r)
-    at = 0
-    for z in range(24):
-        for k in range(2):
-            value = rows(0, z, k)
-            right[at : at + 8] = value[0:8]
-            left[at : at + 8] = value[4:12]
-            at += 8
-    for z in range(2, 22):
-        for k in range(2):
-            value = rows(1, z, k)
-            right[at : at + 6] = value[2:8]
-            left[at : at + 6] = value[4:10]
-            at += 6
+    for field, plan, base in ((0, MID_Q, 0), (1, MID_R, MID_Q_ROWS)):
+        for side, layer, k, n, at in plan:
+            at += base
+            right[at : at + n] = mid_rows(low, high, field, side, layer, k, 8 - n, 8)
+            left[at : at + n] = mid_rows(low, high, field, side, layer, k, 4, 4 + n)
 
 
 def mid_pre_kernel(counts, *refs):
-    rows, (left, right), refs = mid_parts(*refs[:4]), refs[4:6], refs[6:]
+    (low, high, own_q, own_r, left, right, far_left, far_right), refs = refs[:8], refs[8:]
     q, y, r, coarse, coarse_low, coarse_high, coarse_root, natural = refs[:8]
     w = refs[8:]
     gz, xy = lax.axis_index("gz"), lax.axis_index("xy")
     on_left, on_right = inner(xy, counts[1])
     masks = row_masks(4, 8 * xy - 10, 8 * counts[1])
     z_scale = z_mask(4 * gz - 10, 4 * counts[0])
-    for z in range(24):
-        for k in range(2):
-            i = 2 * z + k
-            natural[i, 0:8] = on_left * left[8 * i : 8 * i + 8]
-            natural[i, 8:20] = rows(0, z, k)
-            natural[i, 20:28] = on_right * right[8 * i : 8 * i + 8]
-            natural[i, 28:32] = jnp.zeros((4, LANES), F32)
+    blank = jnp.zeros((8, LANES), F32)
+    for i in range(16):
+        natural[16 + i, 0:8] = on_left * left[8 * i : 8 * i + 8]
+        natural[16 + i, 24:32] = blank
+        natural[16 + i, 8:20] = own_q[i, 2:14]
+        natural[16 + i, 20:28] = on_right * right[8 * i : 8 * i + 8]
+    for side, layer, k, n, at in MID_Q:
+        i = 32 * side + 2 * layer + k
+        natural[i, 0:8] = blank
+        natural[i, 24:32] = blank
+        natural[i, 8 - n : 8] = on_left * far_left[at : at + n]
+        natural[i, 8:20] = mid_rows(low, high, 0, side, layer, k, 0, 12)
+        natural[i, 20:28] = blank
+        natural[i, 20 : 20 + n] = on_right * far_right[at : at + n]
 
     def begin(z):
         for k in range(2):
@@ -342,14 +378,19 @@
                 w[0][z, 4 * k + x] = FIRST * value
 
     loop(0, 24, begin)
-    for z in range(20):
-        for k in range(2):
-            i = 2 * z + k
-            natural[i, 0:8] = jnp.zeros((8, LANES), F32)
-            natural[i, 24:32] = jnp.zeros((8, LANES), F32)
-            natural[i, 2:8] = on_left * left[384 + 6 * i : 390 + 6 * i]
-            natural[i, 8:20] = rows(1, z + 2, k)
-            natural[i, 20:26] = on_right * right[384 + 6 * i : 390 + 6 * i]
+    for i in range(40):
+        natural[i, 0:8] = blank
+        natural[i, 24:32] = blank
+    for i in range(16):
+        natural[12 + i, 2:8] = on_left * left[128 + 6 * i : 134 + 6 * i]
+        natural[12 + i, 8:20] = own_r[i, 2:14]
+        natural[12 + i, 20:26] = on_right * right[128 + 6 * i : 134 + 6 * i]
+    for side, layer, k, n, at in MID_R:
+        i = 2 * (layer - 2 if side == 0 else 14 + layer) + k
+        at += MID_Q_ROWS
+        natural[i, 8 - n : 8] = on_left * far_left[at : at + n]
+        natural[i, 8:20] = mid_rows(low, high, 1, side, layer, k, 0, 12)
+        natural[i, 20 : 20 + n] = on_right * far_right[at : at + n]
 
     def roots(z):
         for k in range(2):
@@ -523,33 +564,37 @@
 
 
 def on_device(load_field, density, void_mask):
-    up, down, root = call(
+    up, down, root, to_left, to_right = call(
         scale_kernel,
         [pltpu.with_memory_space_constraint(x, pltpu.HBM) for x in (load_field, density, void_mask)],
-        [(52, 16, LANES), (52, 16, LANES), (32, 16, LANES)],
+        [(52, 16, LANES), (52, 16, LANES), (32, 16, LANES)] + [(416, LANES)] * 2,
         [(16, 16, 512), pltpu.VMEM((1, 2, 64), jnp.int32), pltpu.SemaphoreType.DMA((3,))],
         pltpu.HBM,
     )
     low, high = send(up, "gz", 1), send(down, "gz", -1)
-    to_left, to_right = call(fine_pack_kernel, (low, up, root, high), [(1088, LANES)] * 2)
     left, right = turn(to_left, to_right)
+    low, high, left, right = lax.optimization_barrier((low, high, left, right))
+    to_left, to_right = call(fine_pack_kernel, (low, high), [(FINE_Q_ROWS + FINE_R_ROWS, LANES)] * 2)
+    far_left, far_right = turn(to_left, to_right)
     fine = (24, 16, 8, LANES)
-    fine_q, fine_y, fine_r, mid_q, mid_r, first, second = call(
+    fine_q, fine_y, fine_r, mid_q, mid_r, first, second, to_left, to_right = call(
         with_counts(fine_pre_kernel),
-        (low, up, root, high, left, right),
-        [fine, (8, 16, 8, LANES), (18, 16, 8, LANES)] + [(16, 16, LANES)] * 2 + [(336, LANES)] * 2,
+        (low, up, root, high, left, right, far_left, far_right),
+        [fine, (8, 16, 8, LANES), (18, 16, 8, LANES)] + [(16, 16, LANES)] * 2 + [(336, LANES)] * 2 + [(224, LANES)] * 2,
         [(96, 32, LANES)] + [fine] * 4,
     )
     pairs = mid_pairs(lax.axis_size("gz"))
     first, second = lax.ppermute(first, "gz", pairs[0]), lax.ppermute(second, "gz", pairs[1])
+    left, right = turn(to_left, to_right)
+    first, second, left, right = lax.optimization_barrier((first, second, left, right))
     low, high, to_left, to_right = call(
-        with_counts(mid_pack_kernel), (first, second, mid_q, mid_r), [(336, LANES)] * 2 + [(624, LANES)] * 2
+        with_counts(mid_pack_kernel), (first, second), [(336, LANES)] * 2 + [(MID_Q_ROWS + MID_R_ROWS, LANES)] * 2
     )
-    left, right = turn(to_left, to_right)
+    far_left, far_right = turn(to_left, to_right)
     mid = (24, 8, 8, LANES)
     mid_q, mid_y, mid_r, coarse, coarse_low, coarse_high, coarse_root = call(
         with_counts(mid_pre_kernel),
-        (low, high, mid_q, mid_r, left, right),
+        (low, high, mid_q, mid_r, left, right, far_left, far_right),
         [mid, (10, 8, 8, LANES), (20, 8, 8, LANES), (8, 16, LANES)] + [(4, 16, LANES)] * 2 + [(10, 16, LANES)],
         [(48, 32, LANES)] + [mid] * 4,
     )

time: 86.8 us -> 82.6 us (0.952)
  waiting for transfers between devices: 44.2 us -> 35.9 us
  starting transfers between devices: 30.9 us -> 34.9 us
    ppermute x4, waiting for transfers between devices: 13.3 us -> 3.4 us  [send(): return lax.ppermute(block, axis, pairs)]
    ppermute x3 -> x5, waiting for transfers between devices: 10.9 us -> 18.3 us  [turn(): lax.ppermute(to_left, 'xy', [(i, (i - 1) % count) for i in range(count)])]
    ppermute x1, waiting for transfers between devices: 7.44 us -> 2.44 us  [on_device(): lax.ppermute(second, 'gz', pairs[1])]
    ppermute x3 -> x5, starting transfers between devices: 10.9 us -> 14.7 us  [turn(): lax.ppermute(to_right, 'xy', [(i, (i + 1) % count) for i in range(count)])]
    ppermute x3 -> x5, waiting for transfers between devices: 11.7 us -> 11.8 us  [turn(): lax.ppermute(to_right, 'xy', [(i, (i + 1) % count) for i in range(count)])]
  transfers between devices with their start and end apart: 12 -> 16, of which waited for: 11 -> 12; matrix products, arithmetic and copies ran while one was open for 0% -> 0% of each run, Pallas kernels for 0% -> 0%
where the time goes in v6:
time: 82.6 us; the launch traced here: 82.3 us
  waiting for transfers between devices  35.9 us (43%)
  starting transfers between devices  34.9 us (42%)
  Pallas kernels  10.8 us (13%)
    ppermute x5, waiting for transfers between devices, turn(): lax.ppermute(to_left, 'xy', [(i, (i - 1) % count) for i in range(count)])  18.3 us
    ppermute x5, starting transfers between devices, turn(): lax.ppermute(to_right, 'xy', [(i, (i + 1) % count) for i in range(count)])  14.7 us
    ppermute x5, waiting for transfers between devices, turn(): lax.ppermute(to_right, 'xy', [(i, (i + 1) % count) for i in range(count)])  11.8 us
    ppermute x4, starting transfers between devices, send(): return lax.ppermute(block, axis, pairs)  11.5 us
    pallas_call x7, Pallas kernels, call(): pl.pallas_call(kernel, out_shape=[jax.ShapeDtypeStruct(s, F32) for s in o...  10.8 us
    ppermute x1, starting transfers between devices, on_device(): lax.ppermute(first, 'gz', pairs[0])  6.64 us
    ppermute x4, waiting for transfers between devices, send(): return lax.ppermute(block, axis, pairs)  3.4 us
    ppermute x1, waiting for transfers between devices, on_device(): lax.ppermute(second, 'gz', pairs[1])  2.44 us
  transfers between devices with their start and end apart: 16, of which 12 were waited for; matrix products, arithmetic and copies ran while one was open for 0% of the time, Pallas kernels for 0%

profile of v6, /device:TPU:245, one launch (start us, length us, event | category | flops | bytes accessed | tf_op | source)
XLA Modules:
  0.0 82.3 jit_solution(13614593227451763741)
XLA Ops:
  0.6 1.7 %shard_map.50 = (f32[52,16,128]{2,1,0:T(8,128)S(1)}, f32[52,16,128]{2,1,0:T(8,128)S(1)}, f32[32,16,128]{2,1,0:T(8,128)S(1)}, f32[416,128]{1,0:T(8,128)S(1)}, f32[416,128]{1,0:T(8,128)S(1)}) custom-call(f32[8,16,512]{2,1,0:T(8,128)} %load_hbm.1, f32[8,16,512]{2,1,0:T(8,128)} %density_hbm.1, s32[1,2,64]{2,1,0:T(2,128)} %void_hbm.1), custom_call_target="tpu_custom_call" | custom-call | tf_op jit(solution)/shard_map/pallas_call | solution.py:538
  2.4 3.0 %collective-permute-start.1 = (f32[52,16,128]{2,1,0:T(8,128)S(1)}, f32[52,16,128]{2,1,0:T(8,128)S(1)}, u32[]{:S(2)}, u32[]{:S(2)}) collective-permute-start(f32[52,16,128]{2,1,0:T(8,128)S(1)} %get-tuple-element.40), channel_id=1, source_target_pairs={{16,0},{32,16},{48,32},{64,48},{80,64},{96,80},{112,96},{128,112},... | collective-permute-start | bytes 1277960 | tf_op jit(solution)/shard_map/ppermute | solution.py:551
  5.3 2.3 %collective-permute-start = (f32[52,16,128]{2,1,0:T(8,128)S(1)}, f32[52,16,128]{2,1,0:T(8,128)S(1)}, u32[]{:S(2)}, u32[]{:S(2)}) collective-permute-start(f32[52,16,128]{2,1,0:T(8,128)S(1)} %get-tuple-element.39.refs_1_), channel_id=1, source_target_pairs={{0,16},{16,32},{32,48},{48,64},{64,80},{80,96},{96,112},{112,128},... | collective-permute-start | bytes 1277960 | tf_op jit(solution)/shard_map/ppermute | solution.py:551
  7.7 4.4 %collective-permute-start.2 = (f32[416,128]{1,0:T(8,128)S(1)}, f32[416,128]{1,0:T(8,128)S(1)}, u32[]{:S(2)}, u32[]{:S(2)}) collective-permute-start(f32[416,128]{1,0:T(8,128)S(1)} %get-tuple-element.41), channel_id=1, source_target_pairs={{0,1},{1,2},{2,3},{3,4},{4,5},{5,6},{6,7},{7,8},{8,9},{9,10},{10,1... | collective-permute-start | bytes 638984 | tf_op jit(solution)/shard_map/ppermute | solution.py:556
  12.1 2.8 %collective-permute-done.2.refs_4_ = f32[416,128]{1,0:T(8,128)S(1)} collective-permute-done((f32[416,128]{1,0:T(8,128)S(1)}, f32[416,128]{1,0:T(8,128)S(1)}, u32[]{:S(2)}, u32[]{:S(2)}) %collective-permute-start.2) | collective-permute-done | bytes 213024 | tf_op jit(solution)/shard_map/ppermute | solution.py:556
  14.9 3.7 %collective-permute-done.3.refs_5_ = f32[416,128]{1,0:T(8,128)S(1)} collective-permute-done((f32[416,128]{1,0:T(8,128)S(1)}, f32[416,128]{1,0:T(8,128)S(1)}, u32[]{:S(2)}, u32[]{:S(2)}) %collective-permute-start.3) | collective-permute-done | bytes 213024 | tf_op jit(solution)/shard_map/ppermute | solution.py:557
  18.6 0.0 collective-permute-done.1.high.refs_3_
  18.6 0.0 collective-permute-done.low.refs_0_
  18.6 0.1 shard_map.51
  18.6 4.1 %collective-permute-start.4 = (f32[560,128]{1,0:T(8,128)S(1)}, f32[560,128]{1,0:T(8,128)S(1)}, u32[]{:S(2)}, u32[]{:S(2)}) collective-permute-start(f32[560,128]{1,0:T(8,128)S(1)} %get-tuple-element.48), channel_id=1, source_target_pairs={{0,1},{1,2},{2,3},{3,4},{4,5},{5,6},{6,7},{7,8},{8,9},{9,10},{10,1... | collective-permute-start | bytes 860168 | tf_op jit(solution)/shard_map/ppermute | solution.py:556
  22.7 3.6 %collective-permute-done.4.refs_6_ = f32[560,128]{1,0:T(8,128)S(1)} collective-permute-done((f32[560,128]{1,0:T(8,128)S(1)}, f32[560,128]{1,0:T(8,128)S(1)}, u32[]{:S(2)}, u32[]{:S(2)}) %collective-permute-start.4) | collective-permute-done | bytes 286752 | tf_op jit(solution)/shard_map/ppermute | solution.py:556
  26.3 3.7 %collective-permute-done.5.refs_7_ = f32[560,128]{1,0:T(8,128)S(1)} collective-permute-done((f32[560,128]{1,0:T(8,128)S(1)}, f32[560,128]{1,0:T(8,128)S(1)}, u32[]{:S(2)}, u32[]{:S(2)}) %collective-permute-start.5) | collective-permute-done | bytes 286752 | tf_op jit(solution)/shard_map/ppermute | solution.py:557
  30.0 2.9 %shard_map.52 = (f32[24,16,8,128]{3,2,1,0:T(8,128)S(1)}, f32[8,16,8,128]{3,2,1,0:T(8,128)S(1)}, f32[18,16,8,128]{3,2,1,0:T(8,128)S(1)}, f32[16,16,128]{2,1,0:T(8...) custom-call(f32[52,16,128]{2,1,0:T(8,128)S(1)} %collective-permute-d, ...), custom_call_target="tpu_custom_call" | custom-call | tf_op jit(solution)/shard_map/pallas_call | solution.py:538
  32.9 6.6 %collective-permute-start.6 = (f32[336,128]{1,0:T(8,128)S(1)}, f32[336,128]{1,0:T(8,128)S(1)}, u32[]{:S(2)}, u32[]{:S(2)}) collective-permute-start(f32[336,128]{1,0:T(8,128)S(1)} %get-tuple-element.50), channel_id=1, source_target_pairs={{0,32},{16,48},{32,64},{48,16},{64,96},{80,112},{96,128},{112,80},... | collective-permute-start | bytes 516104 | tf_op jit(solution)/shard_map/ppermute | solution.py:587
  39.6 1.9 %collective-permute-start.7 = (f32[336,128]{1,0:T(8,128)S(1)}, f32[336,128]{1,0:T(8,128)S(1)}, u32[]{:S(2)}, u32[]{:S(2)}) collective-permute-start(f32[336,128]{1,0:T(8,128)S(1)} %get-tuple-element.51), channel_id=1, source_target_pairs={{32,0},{48,80},{64,32},{80,48},{96,64},{112,144},{128,96},{144,112... | collective-permute-start | bytes 516104 | tf_op jit(solution)/shard_map/ppermute | solution.py:587
  41.5 0.3 collective-permute-start.8
  41.8 0.2 collective-permute-start.9
  42.0 1.6 %collective-permute-done.8.refs_4_ = f32[224,128]{1,0:T(8,128)S(1)} collective-permute-done((f32[224,128]{1,0:T(8,128)S(1)}, f32[224,128]{1,0:T(8,128)S(1)}, u32[]{:S(2)}, u32[]{:S(2)}) %collective-permute-start.8) | collective-permute-done | bytes 114720 | tf_op jit(solution)/shard_map/ppermute | solution.py:556
  43.6 3.6 %collective-permute-done.9.refs_5_ = f32[224,128]{1,0:T(8,128)S(1)} collective-permute-done((f32[224,128]{1,0:T(8,128)S(1)}, f32[224,128]{1,0:T(8,128)S(1)}, u32[]{:S(2)}, u32[]{:S(2)}) %collective-permute-start.9) | collective-permute-done | bytes 114720 | tf_op jit(solution)/shard_map/ppermute | solution.py:557
  47.2 2.4 %collective-permute-done.7.refs_1_ = f32[336,128]{1,0:T(8,128)S(1)} collective-permute-done((f32[336,128]{1,0:T(8,128)S(1)}, f32[336,128]{1,0:T(8,128)S(1)}, u32[]{:S(2)}, u32[]{:S(2)}) %collective-permute-start.7) | collective-permute-done | bytes 172064 | tf_op jit(solution)/shard_map/ppermute | solution.py:587
  49.7 0.1 shard_map.53
  49.8 4.7 %collective-permute-start.10 = (f32[360,128]{1,0:T(8,128)S(1)}, f32[360,128]{1,0:T(8,128)S(1)}, u32[]{:S(2)}, u32[]{:S(2)}) collective-permute-start(f32[360,128]{1,0:T(8,128)S(1)} %get-tuple-element.62), channel_id=1, source_target_pairs={{0,1},{1,2},{2,3},{3,4},{4,5},{5,6},{6,7},{7,8},{8,9},{9,10},{10,1... | collective-permute-start | bytes 552968 | tf_op jit(solution)/shard_map/ppermute | solution.py:556
  54.4 2.5 %collective-permute-done.10.refs_6_ = f32[360,128]{1,0:T(8,128)S(1)} collective-permute-done((f32[360,128]{1,0:T(8,128)S(1)}, f32[360,128]{1,0:T(8,128)S(1)}, u32[]{:S(2)}, u32[]{:S(2)}) %collective-permute-start.10) | collective-permute-done | bytes 184352 | tf_op jit(solution)/shard_map/ppermute | solution.py:556
  56.9 3.7 %collective-permute-done.11.refs_7_ = f32[360,128]{1,0:T(8,128)S(1)} collective-permute-done((f32[360,128]{1,0:T(8,128)S(1)}, f32[360,128]{1,0:T(8,128)S(1)}, u32[]{:S(2)}, u32[]{:S(2)}) %collective-permute-start.11) | collective-permute-done | bytes 184352 | tf_op jit(solution)/shard_map/ppermute | solution.py:557
  60.6 1.6 %shard_map.54 = (f32[24,8,8,128]{3,2,1,0:T(8,128)S(1)}, f32[10,8,8,128]{3,2,1,0:T(8,128)S(1)}, f32[20,8,8,128]{3,2,1,0:T(8,128)S(1)}, f32[8,16,128]{2,1,0:T(8,12...) custom-call(f32[336,128]{1,0:T(8,128)S(1)} %get-tuple-element.56.refs_0_, ...), custom_call_target="tpu_custom_call" | custom-call | tf_op jit(solution)/shard_map/pallas_call | solution.py:538
  62.2 1.9 %collective-permute-start.12 = (f32[4,16,128]{2,1,0:T(8,128)S(1)}, f32[4,16,128]{2,1,0:T(8,128)S(1)}, u32[]{:S(2)}, u32[]{:S(2)}) collective-permute-start(f32[4,16,128]{2,1,0:T(8,128)S(1)} %get-tuple-element.64), channel_id=1, source_target_pairs={{0,32},{16,48},{32,64},{48,80},{64,96},{80,112},{96,128},{112,144}... | collective-permute-start | bytes 98312 | tf_op jit(solution)/shard_map/ppermute | solution.py:551
  64.1 4.3 %collective-permute-start.13 = (f32[4,16,128]{2,1,0:T(8,128)S(1)}, f32[4,16,128]{2,1,0:T(8,128)S(1)}, u32[]{:S(2)}, u32[]{:S(2)}) collective-permute-start(f32[4,16,128]{2,1,0:T(8,128)S(1)} %get-tuple-element.66), channel_id=1, source_target_pairs={{32,0},{48,16},{64,32},{80,48},{96,64},{112,80},{128,96},{144,112}... | collective-permute-start | bytes 98312 | tf_op jit(solution)/shard_map/ppermute | solution.py:551
  68.4 3.4 %collective-permute-done.13.refs_2_ = f32[4,16,128]{2,1,0:T(8,128)S(1)} collective-permute-done((f32[4,16,128]{2,1,0:T(8,128)S(1)}, f32[4,16,128]{2,1,0:T(8,128)S(1)}, u32[]{:S(2)}, u32[]{:S(2)}) %collective-permute-start.13) | collective-permute-done | bytes 32800 | tf_op jit(solution)/shard_map/ppermute | solution.py:551
  71.8 1.2 %collective-permute-start.14 = (f32[16,8,128]{2,1,0:T(8,128)S(1)}, f32[16,8,128]{2,1,0:T(8,128)S(1)}, u32[]{:S(2)}, u32[]{:S(2)}) collective-permute-start(f32[16,8,128]{2,1,0:T(8,128)S(1)} %get-tuple-element.67), channel_id=1, source_target_pairs={{0,1},{1,2},{2,3},{3,4},{4,5},{5,6},{6,7},{7,8},{8,9},{9,10},{10,1... | collective-permute-start | bytes 196616 | tf_op jit(solution)/shard_map/ppermute | solution.py:556
  73.0 1.3 %collective-permute-done.14.refs_3_ = f32[16,8,128]{2,1,0:T(8,128)S(1)} collective-permute-done((f32[16,8,128]{2,1,0:T(8,128)S(1)}, f32[16,8,128]{2,1,0:T(8,128)S(1)}, u32[]{:S(2)}, u32[]{:S(2)}) %collective-permute-start.14) | collective-permute-done | bytes 65568 | tf_op jit(solution)/shard_map/ppermute | solution.py:556
  74.3 3.6 %collective-permute-done.15.refs_4_ = f32[16,8,128]{2,1,0:T(8,128)S(1)} collective-permute-done((f32[16,8,128]{2,1,0:T(8,128)S(1)}, f32[16,8,128]{2,1,0:T(8,128)S(1)}, u32[]{:S(2)}, u32[]{:S(2)}) %collective-permute-start.15) | collective-permute-done | bytes 65568 | tf_op jit(solution)/shard_map/ppermute | solution.py:557
  77.9 4.4 %shard_map.56 = (f32[8,16,512]{2,1,0:T(8,128)}, f32[8,16,512]{2,1,0:T(8,128)}) custom-call(f32[4,16,128]{2,1,0:T(8,128)S(1)} %collective-permute-done.12.refs_0_, f32[8,16,128]{2,1,0:T(8,128)S(1)} %get-tuple-element.65.refs_1_, f32[4,16,128]{2,1,0:T(8,128)S(1)} %collective-permute-done.13.refs_2_, f32[16,8,128]{2,1,0:T(8,128)S(1)} %collective-permute-done.14.refs_3_, ...), custom_call_target="tpu_custom_call" | custom-call | tf_op jit(solution)/shard_map/pallas_call | solution.py:538
  (7 shorter events, 0.0 us)
Async XLA Ops:
  2.4 16.2 %collective-permute-start.1 = (f32[52,16,128]{2,1,0:T(8,128)S(1)}, f32[52,16,128]{2,1,0:T(8,128)S(1)}, u32[]{:S(2)}, u32[]{:S(2)}) collective-permute-start(f32[52,16,128]{2,1,0:T(8,128)S(1)} %get-tuple-element.40), channel_id=1, source_target_pairs={{16,0},{32,16},{48,32},{64,48},{80,64},{96,80},{112,96},{128,112},... | collective-permute-start | bytes 1277960 | tf_op jit(solution)/shard_map/ppermute | solution.py:551
  5.3 13.2 %collective-permute-start = (f32[52,16,128]{2,1,0:T(8,128)S(1)}, f32[52,16,128]{2,1,0:T(8,128)S(1)}, u32[]{:S(2)}, u32[]{:S(2)}) collective-permute-start(f32[52,16,128]{2,1,0:T(8,128)S(1)} %get-tuple-element.39.refs_1_), channel_id=1, source_target_pairs={{0,16},{16,32},{32,48},{48,64},{64,80},{80,96},{96,112},{112,128},... | collective-permute-start | bytes 1277960 | tf_op jit(solution)/shard_map/ppermute | solution.py:551
  7.7 7.2 %collective-permute-start.2 = (f32[416,128]{1,0:T(8,128)S(1)}, f32[416,128]{1,0:T(8,128)S(1)}, u32[]{:S(2)}, u32[]{:S(2)}) collective-permute-start(f32[416,128]{1,0:T(8,128)S(1)} %get-tuple-element.41), channel_id=1, source_target_pairs={{0,1},{1,2},{2,3},{3,4},{4,5},{5,6},{6,7},{7,8},{8,9},{9,10},{10,1... | collective-permute-start | bytes 638984 | tf_op jit(solution)/shard_map/ppermute | solution.py:556
  12.1 6.5 %collective-permute-start.3 = (f32[416,128]{1,0:T(8,128)S(1)}, f32[416,128]{1,0:T(8,128)S(1)}, u32[]{:S(2)}, u32[]{:S(2)}) collective-permute-start(f32[416,128]{1,0:T(8,128)S(1)} %get-tuple-element.42), channel_id=1, source_target_pairs={{0,15},{1,0},{2,1},{3,2},{4,3},{5,4},{6,5},{7,6},{8,7},{9,8},{10,9... | collective-permute-start | bytes 638984 | tf_op jit(solution)/shard_map/ppermute | solution.py:557
  18.6 7.7 %collective-permute-start.4 = (f32[560,128]{1,0:T(8,128)S(1)}, f32[560,128]{1,0:T(8,128)S(1)}, u32[]{:S(2)}, u32[]{:S(2)}) collective-permute-start(f32[560,128]{1,0:T(8,128)S(1)} %get-tuple-element.48), channel_id=1, source_target_pairs={{0,1},{1,2},{2,3},{3,4},{4,5},{5,6},{6,7},{7,8},{8,9},{9,10},{10,1... | collective-permute-start | bytes 860168 | tf_op jit(solution)/shard_map/ppermute | solution.py:556
  22.7 7.3 %collective-permute-start.5 = (f32[560,128]{1,0:T(8,128)S(1)}, f32[560,128]{1,0:T(8,128)S(1)}, u32[]{:S(2)}, u32[]{:S(2)}) collective-permute-start(f32[560,128]{1,0:T(8,128)S(1)} %get-tuple-element.49), channel_id=1, source_target_pairs={{0,15},{1,0},{2,1},{3,2},{4,3},{5,4},{6,5},{7,6},{8,7},{9,8},{10,9... | collective-permute-start | bytes 860168 | tf_op jit(solution)/shard_map/ppermute | solution.py:557
  32.9 14.3 %collective-permute-start.6 = (f32[336,128]{1,0:T(8,128)S(1)}, f32[336,128]{1,0:T(8,128)S(1)}, u32[]{:S(2)}, u32[]{:S(2)}) collective-permute-start(f32[336,128]{1,0:T(8,128)S(1)} %get-tuple-element.50), channel_id=1, source_target_pairs={{0,32},{16,48},{32,64},{48,16},{64,96},{80,112},{96,128},{112,80},... | collective-permute-start | bytes 516104 | tf_op jit(solution)/shard_map/ppermute | solution.py:587
  39.6 10.1 %collective-permute-start.7 = (f32[336,128]{1,0:T(8,128)S(1)}, f32[336,128]{1,0:T(8,128)S(1)}, u32[]{:S(2)}, u32[]{:S(2)}) collective-permute-start(f32[336,128]{1,0:T(8,128)S(1)} %get-tuple-element.51), channel_id=1, source_target_pairs={{32,0},{48,80},{64,32},{80,48},{96,64},{112,144},{128,96},{144,112... | collective-permute-start | bytes 516104 | tf_op jit(solution)/shard_map/ppermute | solution.py:587
  41.5 2.1 %collective-permute-start.8 = (f32[224,128]{1,0:T(8,128)S(1)}, f32[224,128]{1,0:T(8,128)S(1)}, u32[]{:S(2)}, u32[]{:S(2)}) collective-permute-start(f32[224,128]{1,0:T(8,128)S(1)} %get-tuple-element.52), channel_id=1, source_target_pairs={{0,1},{1,2},{2,3},{3,4},{4,5},{5,6},{6,7},{7,8},{8,9},{9,10},{10,1... | collective-permute-start | bytes 344072 | tf_op jit(solution)/shard_map/ppermute | solution.py:556
  41.8 5.4 %collective-permute-start.9 = (f32[224,128]{1,0:T(8,128)S(1)}, f32[224,128]{1,0:T(8,128)S(1)}, u32[]{:S(2)}, u32[]{:S(2)}) collective-permute-start(f32[224,128]{1,0:T(8,128)S(1)} %get-tuple-element.53), channel_id=1, source_target_pairs={{0,15},{1,0},{2,1},{3,2},{4,3},{5,4},{6,5},{7,6},{8,7},{9,8},{10,9... | collective-permute-start | bytes 344072 | tf_op jit(solution)/shard_map/ppermute | solution.py:557
  49.8 7.1 %collective-permute-start.10 = (f32[360,128]{1,0:T(8,128)S(1)}, f32[360,128]{1,0:T(8,128)S(1)}, u32[]{:S(2)}, u32[]{:S(2)}) collective-permute-start(f32[360,128]{1,0:T(8,128)S(1)} %get-tuple-element.62), channel_id=1, source_target_pairs={{0,1},{1,2},{2,3},{3,4},{4,5},{5,6},{6,7},{7,8},{8,9},{9,10},{10,1... | collective-permute-start | bytes 552968 | tf_op jit(solution)/shard_map/ppermute | solution.py:556
  54.4 6.2 %collective-permute-start.11 = (f32[360,128]{1,0:T(8,128)S(1)}, f32[360,128]{1,0:T(8,128)S(1)}, u32[]{:S(2)}, u32[]{:S(2)}) collective-permute-start(f32[360,128]{1,0:T(8,128)S(1)} %get-tuple-element.63), channel_id=1, source_target_pairs={{0,15},{1,0},{2,1},{3,2},{4,3},{5,4},{6,5},{7,6},{8,7},{9,8},{10,9... | collective-permute-start | bytes 552968 | tf_op jit(solution)/shard_map/ppermute | solution.py:557
  62.2 6.2 %collective-permute-start.12 = (f32[4,16,128]{2,1,0:T(8,128)S(1)}, f32[4,16,128]{2,1,0:T(8,128)S(1)}, u32[]{:S(2)}, u32[]{:S(2)}) collective-permute-start(f32[4,16,128]{2,1,0:T(8,128)S(1)} %get-tuple-element.64), channel_id=1, source_target_pairs={{0,32},{16,48},{32,64},{48,80},{64,96},{80,112},{96,128},{112,144}... | collective-permute-start | bytes 98312 | tf_op jit(solution)/shard_map/ppermute | solution.py:551
  64.1 7.7 %collective-permute-start.13 = (f32[4,16,128]{2,1,0:T(8,128)S(1)}, f32[4,16,128]{2,1,0:T(8,128)S(1)}, u32[]{:S(2)}, u32[]{:S(2)}) collective-permute-start(f32[4,16,128]{2,1,0:T(8,128)S(1)} %get-tuple-element.66), channel_id=1, source_target_pairs={{32,0},{48,16},{64,32},{80,48},{96,64},{112,80},{128,96},{144,112}... | collective-permute-start | bytes 98312 | tf_op jit(solution)/shard_map/ppermute | solution.py:551
  71.8 2.5 %collective-permute-start.14 = (f32[16,8,128]{2,1,0:T(8,128)S(1)}, f32[16,8,128]{2,1,0:T(8,128)S(1)}, u32[]{:S(2)}, u32[]{:S(2)}) collective-permute-start(f32[16,8,128]{2,1,0:T(8,128)S(1)} %get-tuple-element.67), channel_id=1, source_target_pairs={{0,1},{1,2},{2,3},{3,4},{4,5},{5,6},{6,7},{7,8},{8,9},{9,10},{10,1... | collective-permute-start | bytes 196616 | tf_op jit(solution)/shard_map/ppermute | solution.py:556
  73.0 4.9 %collective-permute-start.15 = (f32[16,8,128]{2,1,0:T(8,128)S(1)}, f32[16,8,128]{2,1,0:T(8,128)S(1)}, u32[]{:S(2)}, u32[]{:S(2)}) collective-permute-start(f32[16,8,128]{2,1,0:T(8,128)S(1)} %get-tuple-element.68), channel_id=1, source_target_pairs={{0,15},{1,0},{2,1},{3,2},{4,3},{5,4},{6,5},{7,6},{8,7},{9,8},{10,9... | collective-permute-start | bytes 196616 | tf_op jit(solution)/shard_map/ppermute | solution.py:557

commit v7 on v6

--- a/solution.py
+++ b/solution.py
@@ -26,7 +26,15 @@
     return pairs
 
 
-COEFFICIENTS = coefficients()
+def recurrences():
+    out, c1_old, c2_old = [], 0.0, FIRST
+    for c1, c2 in coefficients():
+        out.append((c1 + c2 / c2_old - 6.0 * c2, c2 * c1_old / c2_old, c2))
+        c1_old, c2_old = c1, c2
+    return out, (1.0 / c2_old - 6.0, c1_old / c2_old)
+
+
+STEPS, LAST = recurrences()
 
 
 def iota(shape, dim):
@@ -94,37 +102,32 @@
     return here, [q[z, i] - (6.0 * here[i] - total[i]) for i in range(len(here))]
 
 
-def smooth(w, q, low, high, n, masks, z_scale, passes, finish=None, width=24):
-    for turn in range(passes):
-
-        def advance(z, turn=turn):
-            here, rest = applied(w[turn], z, n, q)
-            if finish is not None and turn == DEGREE - 1:
-                finish(z, rest)
-                return
-            if turn < passes - 1 or passes == DEGREE:
-                for i, value in enumerate(rest):
-                    q[z, i] = value
-            if turn < DEGREE - 1:
-                c1, c2 = COEFFICIENTS[turn]
-                scales = [z_scale(z, c2) * mask for mask in masks]
-                for i, value in enumerate(rest):
-                    w[turn + 1][z, i] = c1 * here[i] + scales[i % n] * value
+def smooth(w, low, high, n, masks, z_scale, width=24):
+    for turn, (a, b, c) in enumerate(STEPS):
+
+        def advance(z, turn=turn, a=a, b=b, c=c):
+            here, total = around(w[turn], z, n)
+            scales = [z_scale(z, c) * mask for mask in masks]
+            for i in range(len(here)):
+                value = a * here[i] + scales[i % n] * total[i]
+                w[turn + 1][z, i] = value if turn == 0 else value - b * w[turn - 1][z, i]
 
         loop(low + 1 + turn, high - 1 - turn, advance, width)
+
+
+def remains(w, z, n):
+    here, total = around(w[DEGREE - 1], z, n)
+    return [(LAST[0] * here[i] + total[i]) - LAST[1] * w[DEGREE - 2][z, i] for i in range(len(here))]
 
 
 def weave(source, z, k, blocks, n, x):
     return source[z * blocks + k, pl.ds(x, 8, n), :]
 
 
-def exact_product(left, right):
+def moved(left, right):
     high = left.astype(jnp.bfloat16)
-    rest = left - high.astype(F32)
-    middle = rest.astype(jnp.bfloat16)
-    low = (rest - middle.astype(F32)).astype(jnp.bfloat16)
-    parts = [jnp.dot(part, right, preferred_element_type=F32) for part in (high, middle, low)]
-    return (parts[2] + parts[1]) + parts[0]
+    low = (left - high.astype(F32)).astype(jnp.bfloat16)
+    return jnp.dot(high, right, preferred_element_type=F32) + jnp.dot(low, right, preferred_element_type=F32)
 
 
 def weave_matrix(dim):
@@ -172,7 +175,7 @@
     voids = jnp.dot(bricks.astype(jnp.bfloat16), spread, preferred_element_type=F32)
     copies[0].wait()
     copies[1].wait()
-    fields = exact_product(both[...].reshape(256, 512), matrix)
+    fields = moved(both[...].reshape(256, 512), matrix)
     for z in range(8):
         for k in range(4):
             b = fields[16 * z : 16 * z + 16, LANES * k : LANES * k + LANES]
@@ -232,9 +235,7 @@
     def begin(z):
         for k in range(4):
             for x in range(4):
-                value = weave(natural, z, k, 4, 4, x)
-                q[z, 4 * k + x] = value
-                w[0][z, 4 * k + x] = FIRST * value
+                w[0][z, 4 * k + x] = FIRST * weave(natural, z, k, 4, 4, x)
 
     loop(0, 24, begin, 8)
 
@@ -260,7 +261,13 @@
                 r[z, 4 * k + x] = weave(natural, z, k, 4, 4, x)
 
     loop(0, 18, roots, 6)
-    smooth(w, q, 0, 24, 4, masks, z_scale, DEGREE, width=8)
+    smooth(w, 0, 24, 4, masks, z_scale, 8)
+
+    def rest(z):
+        for i, value in enumerate(remains(w, z, 4)):
+            q[z, i] = value
+
+    loop(4, 20, rest, 8)
 
     def total(z):
         for i in range(16):
@@ -373,9 +380,7 @@
     def begin(z):
         for k in range(2):
             for x in range(4):
-                value = weave(natural, z, k, 2, 4, x)
-                q[z, 4 * k + x] = value
-                w[0][z, 4 * k + x] = FIRST * value
+                w[0][z, 4 * k + x] = FIRST * weave(natural, z, k, 2, 4, x)
 
     loop(0, 24, begin)
     for i in range(40):
@@ -398,7 +403,13 @@
                 r[z, 4 * k + x] = weave(natural, z, k, 2, 4, x)
 
     loop(0, 20, roots)
-    smooth(w, q, 0, 24, 4, masks, z_scale, DEGREE)
+    smooth(w, 0, 24, 4, masks, z_scale)
+
+    def rest(z):
+        for i, value in enumerate(remains(w, z, 4)):
+            q[z, i] = value
+
+    loop(4, 20, rest)
 
     def total(z):
         for i in range(8):
@@ -437,8 +448,9 @@
 def finish_kernel(counts, *refs):
     parts, (left, right), refs = refs[:3], refs[3:5], refs[5:]
     coarse_root, mid_q, mid_y, mid_r, fine_q, fine_y, fine_r, out_x, out_r = refs[:9]
-    natural, cq, error, spread, mq, mt, fq, ft, plain_x, plain_r, rows_x, rows_r = refs[9:21]
-    cw, mw, fw = refs[21:25], refs[25:29], refs[29:33]
+    natural, error, spread, mt, ft, plain_x, plain_r, rows_x, rows_r = refs[9:18]
+    cw, mw, fw = refs[18:22], refs[22:26], refs[26:30]
+    ready_x, ready_r, sems = refs[30:]
     gz, xy = lax.axis_index("gz"), lax.axis_index("xy")
 
     on_left, on_right = inner(xy, counts[1])
@@ -451,12 +463,10 @@
             natural[at, 14:18] = on_right * right[at, 0:4]
             natural[at, 18:24] = jnp.zeros((6, LANES), F32)
             for x in range(3):
-                value = weave(natural, at, 0, 1, 3, x)
-                cq[at, x] = value
-                cw[0][at, x] = FIRST * value
+                cw[0][at, x] = FIRST * weave(natural, at, 0, 1, 3, x)
             at += 1
     masks = row_masks(3, 4 * xy - 7, 4 * counts[1])
-    smooth(cw, cq, 0, 16, 3, masks, z_mask(2 * gz - 7, 2 * counts[0]), DEGREE - 1)
+    smooth(cw, 0, 16, 3, masks, z_mask(2 * gz - 7, 2 * counts[0]))
     for k in range(10):
         for x in range(3):
             total = (cw[0][k + 3, x] + cw[1][k + 3, x]) + (cw[2][k + 3, x] + cw[3][k + 3, x])
@@ -477,11 +487,10 @@
         _, rest = applied(mt, z, 4, mid_q)
         scales = [z_scale(z, FIRST) * mask for mask in masks]
         for i, value in enumerate(rest):
-            mq[z, i] = value
             mw[0][z, i] = scales[i % 4] * value
 
     loop(4, 20, mid_correct)
-    smooth(mw, mq, 4, 20, 4, masks, z_scale, DEGREE - 1)
+    smooth(mw, 4, 20, 4, masks, z_scale)
 
     def mid_error(z):
         for k in range(2):
@@ -501,7 +510,7 @@
                     ft[2 * k + 2, i] = fine_r[jnp.maximum(2 * k - 1, 0), i] * value
                     ft[2 * k + 3, i] = fine_r[jnp.minimum(2 * k, 17), i] * value
 
-    loop(0, 10, fine_prolong, 1)
+    loop(0, 10, fine_prolong, 10)
     masks = row_masks(4, 16 * xy - 8, 16 * counts[1])
     z_scale = z_mask(8 * gz - 8, 8 * counts[0])
 
@@ -509,32 +518,43 @@
         _, rest = applied(ft, z, 4, fine_q)
         scales = [z_scale(z, FIRST) * mask for mask in masks]
         for i, value in enumerate(rest):
-            fq[z, i] = value
             fw[0][z, i] = scales[i % 4] * value
 
     loop(4, 20, fine_correct)
 
-    def finish(z, rest):
-        for k in range(4):
-            for x in range(4):
-                i = 4 * k + x
-                r = fine_r[z - 3, i]
-                total = (fw[0][z, i] + fw[1][z, i]) + (fw[2][z, i] + fw[3][z, i])
-                total = total + (fine_y[z - 8, i] + ft[z, i])
-                plain_x[4 * (z - 8) + k, pl.ds(x, 8, 4), :] = total / r
-                plain_r[4 * (z - 8) + k, pl.ds(x, 8, 4), :] = r * rest[i]
-
-    smooth(fw, fq, 4, 20, 4, masks, z_scale, DEGREE, finish)
+    smooth(fw, 4, 20, 4, masks, z_scale)
     matrix = weave_matrix(1)
-    for plain, rows, out in ((plain_x, rows_x, out_x), (plain_r, rows_r, out_r)):
+
+    def leave(plain, rows, ready, out, sem):
         for z in range(8):
             for k in range(4):
                 rows[16 * z : 16 * z + 16, LANES * k : LANES * k + LANES] = plain[4 * z + k, 8:24]
-        out[...] = exact_product(rows[...], matrix).reshape(8, 16, 512)
-
-
-def call(kernel, operands, out_shapes, scratch=(), space=pltpu.VMEM):
-    whole = pl.BlockSpec(memory_space=pltpu.VMEM)
+        ready[...] = moved(rows[...], matrix).reshape(8, 16, 512)
+        copy = pltpu.make_async_copy(ready, out, sem)
+        copy.start()
+        return copy
+
+    for z in range(8, 16):
+        for k in range(4):
+            for x in range(4):
+                i = 4 * k + x
+                total = (fw[0][z, i] + fw[1][z, i]) + (fw[2][z, i] + fw[3][z, i])
+                total = total + (fine_y[z - 8, i] + ft[z, i])
+                plain_x[4 * (z - 8) + k, pl.ds(x, 8, 4), :] = total / fine_r[z - 3, i]
+    first = leave(plain_x, rows_x, ready_x, out_x, sems.at[0])
+    for z in range(8, 16):
+        rest = remains(fw, z, 4)
+        for k in range(4):
+            for x in range(4):
+                i = 4 * k + x
+                plain_r[4 * (z - 8) + k, pl.ds(x, 8, 4), :] = fine_r[z - 3, i] * rest[i]
+    second = leave(plain_r, rows_r, ready_r, out_r, sems.at[1])
+    first.wait()
+    second.wait()
+
+
+def call(kernel, operands, out_shapes, scratch=(), space=pltpu.VMEM, out_space=pltpu.VMEM):
+    whole = pl.BlockSpec(memory_space=out_space)
     return pl.pallas_call(
         kernel,
         out_shape=[jax.ShapeDtypeStruct(s, F32) for s in out_shapes],
@@ -607,12 +627,15 @@
             with_counts(finish_kernel),
             parts + (left, right, coarse_root, mid_q, mid_y, mid_r, fine_q, fine_y, fine_r),
             [(8, 16, 512), (8, 16, 512)],
-            [(16, 24, LANES), coarsest, (10, 16, LANES), (20, 32, LANES), mid, mid, fine, fine]
+            [(16, 24, LANES), (10, 16, LANES), (20, 32, LANES), mid, fine]
             + [(32, 32, LANES)] * 2
             + [(128, 512)] * 2
             + [coarsest] * 4
             + [mid] * 4
-            + [fine] * 4,
+            + [fine] * 4
+            + [(8, 16, 512)] * 2
+            + [pltpu.SemaphoreType.DMA((2,))],
+            out_space=pl.ANY,
         )
     )
 

time: 82.6 us -> 81.6 us (0.988)
  Pallas kernels: 10.8 us -> 9.84 us
    pallas_call x7, Pallas kernels: 10.8 us -> 9.84 us  [call(): pl.pallas_call(kernel, out_shape=[jax.ShapeDtypeStruct(s, F32) for s in o...]
where the time goes in v7:
time: 81.6 us; the launch traced here: 81.3 us
  waiting for transfers between devices  35.9 us (44%)
  starting transfers between devices  34.9 us (43%)
  Pallas kernels  9.84 us (12%)
    ppermute x5, waiting for transfers between devices, turn(): lax.ppermute(to_left, 'xy', [(i, (i - 1) % count) for i in range(count)])  18.3 us
    ppermute x5, starting transfers between devices, turn(): lax.ppermute(to_right, 'xy', [(i, (i + 1) % count) for i in range(count)])  14.7 us
    ppermute x5, waiting for transfers between devices, turn(): lax.ppermute(to_right, 'xy', [(i, (i + 1) % count) for i in range(count)])  11.8 us
    ppermute x4, starting transfers between devices, send(): return lax.ppermute(block, axis, pairs)  11.5 us
    pallas_call x7, Pallas kernels, call(): pl.pallas_call(kernel, out_shape=[jax.ShapeDtypeStruct(s, F32) for s in o...  9.84 us
    ppermute x1, starting transfers between devices, on_device(): lax.ppermute(first, 'gz', pairs[0])  6.64 us
    ppermute x4, waiting for transfers between devices, send(): return lax.ppermute(block, axis, pairs)  3.4 us
    ppermute x1, waiting for transfers between devices, on_device(): lax.ppermute(second, 'gz', pairs[1])  2.44 us
  transfers between devices with their start and end apart: 16, of which 12 were waited for; matrix products, arithmetic and copies ran while one was open for 0% of the time, Pallas kernels for 0%

profile of v7, /device:TPU:245, one launch (start us, length us, event | category | flops | bytes accessed | tf_op | source)
XLA Modules:
  0.0 81.3 jit_solution(4156709285720615154)
XLA Ops:
  0.6 1.6 %shard_map.50 = (f32[52,16,128]{2,1,0:T(8,128)S(1)}, f32[52,16,128]{2,1,0:T(8,128)S(1)}, f32[32,16,128]{2,1,0:T(8,128)S(1)}, f32[416,128]{1,0:T(8,128)S(1)}, f32[416,128]{1,0:T(8,128)S(1)}) custom-call(f32[8,16,512]{2,1,0:T(8,128)} %load_hbm.1, f32[8,16,512]{2,1,0:T(8,128)} %density_hbm.1, s32[1,2,64]{2,1,0:T(2,128)} %void_hbm.1), custom_call_target="tpu_custom_call" | custom-call | tf_op jit(solution)/shard_map/pallas_call | solution.py:558
  2.2 3.0 %collective-permute-start.1 = (f32[52,16,128]{2,1,0:T(8,128)S(1)}, f32[52,16,128]{2,1,0:T(8,128)S(1)}, u32[]{:S(2)}, u32[]{:S(2)}) collective-permute-start(f32[52,16,128]{2,1,0:T(8,128)S(1)} %get-tuple-element.40), channel_id=1, source_target_pairs={{16,0},{32,16},{48,32},{64,48},{80,64},{96,80},{112,96},{128,112},... | collective-permute-start | bytes 1277960 | tf_op jit(solution)/shard_map/ppermute | solution.py:571
  5.2 2.3 %collective-permute-start = (f32[52,16,128]{2,1,0:T(8,128)S(1)}, f32[52,16,128]{2,1,0:T(8,128)S(1)}, u32[]{:S(2)}, u32[]{:S(2)}) collective-permute-start(f32[52,16,128]{2,1,0:T(8,128)S(1)} %get-tuple-element.39.refs_1_), channel_id=1, source_target_pairs={{0,16},{16,32},{32,48},{48,64},{64,80},{80,96},{96,112},{112,128},... | collective-permute-start | bytes 1277960 | tf_op jit(solution)/shard_map/ppermute | solution.py:571
  7.5 4.4 %collective-permute-start.2 = (f32[416,128]{1,0:T(8,128)S(1)}, f32[416,128]{1,0:T(8,128)S(1)}, u32[]{:S(2)}, u32[]{:S(2)}) collective-permute-start(f32[416,128]{1,0:T(8,128)S(1)} %get-tuple-element.41), channel_id=1, source_target_pairs={{0,1},{1,2},{2,3},{3,4},{4,5},{5,6},{6,7},{7,8},{8,9},{9,10},{10,1... | collective-permute-start | bytes 638984 | tf_op jit(solution)/shard_map/ppermute | solution.py:576
  12.0 2.8 %collective-permute-done.2.refs_4_ = f32[416,128]{1,0:T(8,128)S(1)} collective-permute-done((f32[416,128]{1,0:T(8,128)S(1)}, f32[416,128]{1,0:T(8,128)S(1)}, u32[]{:S(2)}, u32[]{:S(2)}) %collective-permute-start.2) | collective-permute-done | bytes 213024 | tf_op jit(solution)/shard_map/ppermute | solution.py:576
  14.8 3.7 %collective-permute-done.3.refs_5_ = f32[416,128]{1,0:T(8,128)S(1)} collective-permute-done((f32[416,128]{1,0:T(8,128)S(1)}, f32[416,128]{1,0:T(8,128)S(1)}, u32[]{:S(2)}, u32[]{:S(2)}) %collective-permute-start.3) | collective-permute-done | bytes 213024 | tf_op jit(solution)/shard_map/ppermute | solution.py:577
  18.4 0.1 shard_map.51
  18.5 4.1 %collective-permute-start.4 = (f32[560,128]{1,0:T(8,128)S(1)}, f32[560,128]{1,0:T(8,128)S(1)}, u32[]{:S(2)}, u32[]{:S(2)}) collective-permute-start(f32[560,128]{1,0:T(8,128)S(1)} %get-tuple-element.48), channel_id=1, source_target_pairs={{0,1},{1,2},{2,3},{3,4},{4,5},{5,6},{6,7},{7,8},{8,9},{9,10},{10,1... | collective-permute-start | bytes 860168 | tf_op jit(solution)/shard_map/ppermute | solution.py:576
  22.6 0.0 collective-permute-start.5
  22.6 3.6 %collective-permute-done.4.refs_6_ = f32[560,128]{1,0:T(8,128)S(1)} collective-permute-done((f32[560,128]{1,0:T(8,128)S(1)}, f32[560,128]{1,0:T(8,128)S(1)}, u32[]{:S(2)}, u32[]{:S(2)}) %collective-permute-start.4) | collective-permute-done | bytes 286752 | tf_op jit(solution)/shard_map/ppermute | solution.py:576
  26.2 3.7 %collective-permute-done.5.refs_7_ = f32[560,128]{1,0:T(8,128)S(1)} collective-permute-done((f32[560,128]{1,0:T(8,128)S(1)}, f32[560,128]{1,0:T(8,128)S(1)}, u32[]{:S(2)}, u32[]{:S(2)}) %collective-permute-start.5) | collective-permute-done | bytes 286752 | tf_op jit(solution)/shard_map/ppermute | solution.py:577
  29.9 2.7 %shard_map.52 = (f32[24,16,8,128]{3,2,1,0:T(8,128)S(1)}, f32[8,16,8,128]{3,2,1,0:T(8,128)S(1)}, f32[18,16,8,128]{3,2,1,0:T(8,128)S(1)}, f32[16,16,128]{2,1,0:T(8...) custom-call(f32[52,16,128]{2,1,0:T(8,128)S(1)} %collective-permute-d, ...), custom_call_target="tpu_custom_call" | custom-call | tf_op jit(solution)/shard_map/pallas_call | solution.py:558
  32.6 6.6 %collective-permute-start.6 = (f32[336,128]{1,0:T(8,128)S(1)}, f32[336,128]{1,0:T(8,128)S(1)}, u32[]{:S(2)}, u32[]{:S(2)}) collective-permute-start(f32[336,128]{1,0:T(8,128)S(1)} %get-tuple-element.50), channel_id=1, source_target_pairs={{0,32},{16,48},{32,64},{48,16},{64,96},{80,112},{96,128},{112,80},... | collective-permute-start | bytes 516104 | tf_op jit(solution)/shard_map/ppermute | solution.py:607
  39.2 1.9 %collective-permute-start.7 = (f32[336,128]{1,0:T(8,128)S(1)}, f32[336,128]{1,0:T(8,128)S(1)}, u32[]{:S(2)}, u32[]{:S(2)}) collective-permute-start(f32[336,128]{1,0:T(8,128)S(1)} %get-tuple-element.51), channel_id=1, source_target_pairs={{32,0},{48,80},{64,32},{80,48},{96,64},{112,144},{128,96},{144,112... | collective-permute-start | bytes 516104 | tf_op jit(solution)/shard_map/ppermute | solution.py:607
  41.2 0.3 collective-permute-start.8
  41.5 0.2 collective-permute-start.9
  41.7 1.6 %collective-permute-done.8.refs_4_ = f32[224,128]{1,0:T(8,128)S(1)} collective-permute-done((f32[224,128]{1,0:T(8,128)S(1)}, f32[224,128]{1,0:T(8,128)S(1)}, u32[]{:S(2)}, u32[]{:S(2)}) %collective-permute-start.8) | collective-permute-done | bytes 114720 | tf_op jit(solution)/shard_map/ppermute | solution.py:576
  43.3 3.6 %collective-permute-done.9.refs_5_ = f32[224,128]{1,0:T(8,128)S(1)} collective-permute-done((f32[224,128]{1,0:T(8,128)S(1)}, f32[224,128]{1,0:T(8,128)S(1)}, u32[]{:S(2)}, u32[]{:S(2)}) %collective-permute-start.9) | collective-permute-done | bytes 114720 | tf_op jit(solution)/shard_map/ppermute | solution.py:577
  46.9 2.4 %collective-permute-done.7.refs_1_ = f32[336,128]{1,0:T(8,128)S(1)} collective-permute-done((f32[336,128]{1,0:T(8,128)S(1)}, f32[336,128]{1,0:T(8,128)S(1)}, u32[]{:S(2)}, u32[]{:S(2)}) %collective-permute-start.7) | collective-permute-done | bytes 172064 | tf_op jit(solution)/shard_map/ppermute | solution.py:607
  49.3 0.1 shard_map.53
  49.4 4.7 %collective-permute-start.10 = (f32[360,128]{1,0:T(8,128)S(1)}, f32[360,128]{1,0:T(8,128)S(1)}, u32[]{:S(2)}, u32[]{:S(2)}) collective-permute-start(f32[360,128]{1,0:T(8,128)S(1)} %get-tuple-element.62), channel_id=1, source_target_pairs={{0,1},{1,2},{2,3},{3,4},{4,5},{5,6},{6,7},{7,8},{8,9},{9,10},{10,1... | collective-permute-start | bytes 552968 | tf_op jit(solution)/shard_map/ppermute | solution.py:576
  54.1 0.0 collective-permute-start.11
  54.1 2.5 %collective-permute-done.10.refs_6_ = f32[360,128]{1,0:T(8,128)S(1)} collective-permute-done((f32[360,128]{1,0:T(8,128)S(1)}, f32[360,128]{1,0:T(8,128)S(1)}, u32[]{:S(2)}, u32[]{:S(2)}) %collective-permute-start.10) | collective-permute-done | bytes 184352 | tf_op jit(solution)/shard_map/ppermute | solution.py:576
  56.6 3.7 %collective-permute-done.11.refs_7_ = f32[360,128]{1,0:T(8,128)S(1)} collective-permute-done((f32[360,128]{1,0:T(8,128)S(1)}, f32[360,128]{1,0:T(8,128)S(1)}, u32[]{:S(2)}, u32[]{:S(2)}) %collective-permute-start.11) | collective-permute-done | bytes 184352 | tf_op jit(solution)/shard_map/ppermute | solution.py:577
  60.3 1.4 %shard_map.54 = (f32[24,8,8,128]{3,2,1,0:T(8,128)S(1)}, f32[10,8,8,128]{3,2,1,0:T(8,128)S(1)}, f32[20,8,8,128]{3,2,1,0:T(8,128)S(1)}, f32[8,16,128]{2,1,0:T(8,12...) custom-call(f32[336,128]{1,0:T(8,128)S(1)} %get-tuple-element.56.refs_0_, ...), custom_call_target="tpu_custom_call" | custom-call | tf_op jit(solution)/shard_map/pallas_call | solution.py:558
  61.7 1.9 %collective-permute-start.12 = (f32[4,16,128]{2,1,0:T(8,128)S(1)}, f32[4,16,128]{2,1,0:T(8,128)S(1)}, u32[]{:S(2)}, u32[]{:S(2)}) collective-permute-start(f32[4,16,128]{2,1,0:T(8,128)S(1)} %get-tuple-element.64), channel_id=1, source_target_pairs={{0,32},{16,48},{32,64},{48,80},{64,96},{80,112},{96,128},{112,144}... | collective-permute-start | bytes 98312 | tf_op jit(solution)/shard_map/ppermute | solution.py:571
  63.6 4.3 %collective-permute-start.13 = (f32[4,16,128]{2,1,0:T(8,128)S(1)}, f32[4,16,128]{2,1,0:T(8,128)S(1)}, u32[]{:S(2)}, u32[]{:S(2)}) collective-permute-start(f32[4,16,128]{2,1,0:T(8,128)S(1)} %get-tuple-element.66), channel_id=1, source_target_pairs={{32,0},{48,16},{64,32},{80,48},{96,64},{112,80},{128,96},{144,112}... | collective-permute-start | bytes 98312 | tf_op jit(solution)/shard_map/ppermute | solution.py:571
  67.9 3.4 %collective-permute-done.13.refs_2_ = f32[4,16,128]{2,1,0:T(8,128)S(1)} collective-permute-done((f32[4,16,128]{2,1,0:T(8,128)S(1)}, f32[4,16,128]{2,1,0:T(8,128)S(1)}, u32[]{:S(2)}, u32[]{:S(2)}) %collective-permute-start.13) | collective-permute-done | bytes 32800 | tf_op jit(solution)/shard_map/ppermute | solution.py:571
  71.3 1.2 %collective-permute-start.14 = (f32[16,8,128]{2,1,0:T(8,128)S(1)}, f32[16,8,128]{2,1,0:T(8,128)S(1)}, u32[]{:S(2)}, u32[]{:S(2)}) collective-permute-start(f32[16,8,128]{2,1,0:T(8,128)S(1)} %get-tuple-element.67), channel_id=1, source_target_pairs={{0,1},{1,2},{2,3},{3,4},{4,5},{5,6},{6,7},{7,8},{8,9},{9,10},{10,1... | collective-permute-start | bytes 196616 | tf_op jit(solution)/shard_map/ppermute | solution.py:576
  72.5 1.3 %collective-permute-done.14.refs_3_ = f32[16,8,128]{2,1,0:T(8,128)S(1)} collective-permute-done((f32[16,8,128]{2,1,0:T(8,128)S(1)}, f32[16,8,128]{2,1,0:T(8,128)S(1)}, u32[]{:S(2)}, u32[]{:S(2)}) %collective-permute-start.14) | collective-permute-done | bytes 65568 | tf_op jit(solution)/shard_map/ppermute | solution.py:576
  73.8 3.6 %collective-permute-done.15.refs_4_ = f32[16,8,128]{2,1,0:T(8,128)S(1)} collective-permute-done((f32[16,8,128]{2,1,0:T(8,128)S(1)}, f32[16,8,128]{2,1,0:T(8,128)S(1)}, u32[]{:S(2)}, u32[]{:S(2)}) %collective-permute-start.15) | collective-permute-done | bytes 65568 | tf_op jit(solution)/shard_map/ppermute | solution.py:577
  77.4 4.0 %shard_map.56 = (f32[8,16,512]{2,1,0:T(8,128)}, f32[8,16,512]{2,1,0:T(8,128)}) custom-call(f32[4,16,128]{2,1,0:T(8,128)S(1)} %collective-permute-done.12.refs_0_, f32[8,16,128]{2,1,0:T(8,128)S(1)} %get-tuple-element.65.refs_1_, f32[4,16,128]{2,1,0:T(8,128)S(1)} %collective-permute-done.13.refs_2_, f32[16,8,128]{2,1,0:T(8,128)S(1)} %collective-permute-done.14.refs_3_, ...), custom_call_target="tpu_custom_call" | custom-call | tf_op jit(solution)/shard_map/pallas_call | solution.py:558
  (7 shorter events, 0.0 us)
Async XLA Ops:
  2.2 16.2 %collective-permute-start.1 = (f32[52,16,128]{2,1,0:T(8,128)S(1)}, f32[52,16,128]{2,1,0:T(8,128)S(1)}, u32[]{:S(2)}, u32[]{:S(2)}) collective-permute-start(f32[52,16,128]{2,1,0:T(8,128)S(1)} %get-tuple-element.40), channel_id=1, source_target_pairs={{16,0},{32,16},{48,32},{64,48},{80,64},{96,80},{112,96},{128,112},... | collective-permute-start | bytes 1277960 | tf_op jit(solution)/shard_map/ppermute | solution.py:571
  5.2 13.2 %collective-permute-start = (f32[52,16,128]{2,1,0:T(8,128)S(1)}, f32[52,16,128]{2,1,0:T(8,128)S(1)}, u32[]{:S(2)}, u32[]{:S(2)}) collective-permute-start(f32[52,16,128]{2,1,0:T(8,128)S(1)} %get-tuple-element.39.refs_1_), channel_id=1, source_target_pairs={{0,16},{16,32},{32,48},{48,64},{64,80},{80,96},{96,112},{112,128},... | collective-permute-start | bytes 1277960 | tf_op jit(solution)/shard_map/ppermute | solution.py:571
  7.5 7.2 %collective-permute-start.2 = (f32[416,128]{1,0:T(8,128)S(1)}, f32[416,128]{1,0:T(8,128)S(1)}, u32[]{:S(2)}, u32[]{:S(2)}) collective-permute-start(f32[416,128]{1,0:T(8,128)S(1)} %get-tuple-element.41), channel_id=1, source_target_pairs={{0,1},{1,2},{2,3},{3,4},{4,5},{5,6},{6,7},{7,8},{8,9},{9,10},{10,1... | collective-permute-start | bytes 638984 | tf_op jit(solution)/shard_map/ppermute | solution.py:576
  12.0 6.5 %collective-permute-start.3 = (f32[416,128]{1,0:T(8,128)S(1)}, f32[416,128]{1,0:T(8,128)S(1)}, u32[]{:S(2)}, u32[]{:S(2)}) collective-permute-start(f32[416,128]{1,0:T(8,128)S(1)} %get-tuple-element.42), channel_id=1, source_target_pairs={{0,15},{1,0},{2,1},{3,2},{4,3},{5,4},{6,5},{7,6},{8,7},{9,8},{10,9... | collective-permute-start | bytes 638984 | tf_op jit(solution)/shard_map/ppermute | solution.py:577
  18.5 7.7 %collective-permute-start.4 = (f32[560,128]{1,0:T(8,128)S(1)}, f32[560,128]{1,0:T(8,128)S(1)}, u32[]{:S(2)}, u32[]{:S(2)}) collective-permute-start(f32[560,128]{1,0:T(8,128)S(1)} %get-tuple-element.48), channel_id=1, source_target_pairs={{0,1},{1,2},{2,3},{3,4},{4,5},{5,6},{6,7},{7,8},{8,9},{9,10},{10,1... | collective-permute-start | bytes 860168 | tf_op jit(solution)/shard_map/ppermute | solution.py:576
  22.6 7.3 %collective-permute-start.5 = (f32[560,128]{1,0:T(8,128)S(1)}, f32[560,128]{1,0:T(8,128)S(1)}, u32[]{:S(2)}, u32[]{:S(2)}) collective-permute-start(f32[560,128]{1,0:T(8,128)S(1)} %get-tuple-element.49), channel_id=1, source_target_pairs={{0,15},{1,0},{2,1},{3,2},{4,3},{5,4},{6,5},{7,6},{8,7},{9,8},{10,9... | collective-permute-start | bytes 860168 | tf_op jit(solution)/shard_map/ppermute | solution.py:577
  32.6 14.3 %collective-permute-start.6 = (f32[336,128]{1,0:T(8,128)S(1)}, f32[336,128]{1,0:T(8,128)S(1)}, u32[]{:S(2)}, u32[]{:S(2)}) collective-permute-start(f32[336,128]{1,0:T(8,128)S(1)} %get-tuple-element.50), channel_id=1, source_target_pairs={{0,32},{16,48},{32,64},{48,16},{64,96},{80,112},{96,128},{112,80},... | collective-permute-start | bytes 516104 | tf_op jit(solution)/shard_map/ppermute | solution.py:607
  39.2 10.1 %collective-permute-start.7 = (f32[336,128]{1,0:T(8,128)S(1)}, f32[336,128]{1,0:T(8,128)S(1)}, u32[]{:S(2)}, u32[]{:S(2)}) collective-permute-start(f32[336,128]{1,0:T(8,128)S(1)} %get-tuple-element.51), channel_id=1, source_target_pairs={{32,0},{48,80},{64,32},{80,48},{96,64},{112,144},{128,96},{144,112... | collective-permute-start | bytes 516104 | tf_op jit(solution)/shard_map/ppermute | solution.py:607
  41.2 2.1 %collective-permute-start.8 = (f32[224,128]{1,0:T(8,128)S(1)}, f32[224,128]{1,0:T(8,128)S(1)}, u32[]{:S(2)}, u32[]{:S(2)}) collective-permute-start(f32[224,128]{1,0:T(8,128)S(1)} %get-tuple-element.52), channel_id=1, source_target_pairs={{0,1},{1,2},{2,3},{3,4},{4,5},{5,6},{6,7},{7,8},{8,9},{9,10},{10,1... | collective-permute-start | bytes 344072 | tf_op jit(solution)/shard_map/ppermute | solution.py:576
  41.5 5.4 %collective-permute-start.9 = (f32[224,128]{1,0:T(8,128)S(1)}, f32[224,128]{1,0:T(8,128)S(1)}, u32[]{:S(2)}, u32[]{:S(2)}) collective-permute-start(f32[224,128]{1,0:T(8,128)S(1)} %get-tuple-element.53), channel_id=1, source_target_pairs={{0,15},{1,0},{2,1},{3,2},{4,3},{5,4},{6,5},{7,6},{8,7},{9,8},{10,9... | collective-permute-start | bytes 344072 | tf_op jit(solution)/shard_map/ppermute | solution.py:577
  49.4 7.1 %collective-permute-start.10 = (f32[360,128]{1,0:T(8,128)S(1)}, f32[360,128]{1,0:T(8,128)S(1)}, u32[]{:S(2)}, u32[]{:S(2)}) collective-permute-start(f32[360,128]{1,0:T(8,128)S(1)} %get-tuple-element.62), channel_id=1, source_target_pairs={{0,1},{1,2},{2,3},{3,4},{4,5},{5,6},{6,7},{7,8},{8,9},{9,10},{10,1... | collective-permute-start | bytes 552968 | tf_op jit(solution)/shard_map/ppermute | solution.py:576
  54.1 6.2 %collective-permute-start.11 = (f32[360,128]{1,0:T(8,128)S(1)}, f32[360,128]{1,0:T(8,128)S(1)}, u32[]{:S(2)}, u32[]{:S(2)}) collective-permute-start(f32[360,128]{1,0:T(8,128)S(1)} %get-tuple-element.63), channel_id=1, source_target_pairs={{0,15},{1,0},{2,1},{3,2},{4,3},{5,4},{6,5},{7,6},{8,7},{9,8},{10,9... | collective-permute-start | bytes 552968 | tf_op jit(solution)/shard_map/ppermute | solution.py:577
  61.7 6.2 %collective-permute-start.12 = (f32[4,16,128]{2,1,0:T(8,128)S(1)}, f32[4,16,128]{2,1,0:T(8,128)S(1)}, u32[]{:S(2)}, u32[]{:S(2)}) collective-permute-start(f32[4,16,128]{2,1,0:T(8,128)S(1)} %get-tuple-element.64), channel_id=1, source_target_pairs={{0,32},{16,48},{32,64},{48,80},{64,96},{80,112},{96,128},{112,144}... | collective-permute-start | bytes 98312 | tf_op jit(solution)/shard_map/ppermute | solution.py:571
  63.6 7.7 %collective-permute-start.13 = (f32[4,16,128]{2,1,0:T(8,128)S(1)}, f32[4,16,128]{2,1,0:T(8,128)S(1)}, u32[]{:S(2)}, u32[]{:S(2)}) collective-permute-start(f32[4,16,128]{2,1,0:T(8,128)S(1)} %get-tuple-element.66), channel_id=1, source_target_pairs={{32,0},{48,16},{64,32},{80,48},{96,64},{112,80},{128,96},{144,112}... | collective-permute-start | bytes 98312 | tf_op jit(solution)/shard_map/ppermute | solution.py:571
  71.3 2.5 %collective-permute-start.14 = (f32[16,8,128]{2,1,0:T(8,128)S(1)}, f32[16,8,128]{2,1,0:T(8,128)S(1)}, u32[]{:S(2)}, u32[]{:S(2)}) collective-permute-start(f32[16,8,128]{2,1,0:T(8,128)S(1)} %get-tuple-element.67), channel_id=1, source_target_pairs={{0,1},{1,2},{2,3},{3,4},{4,5},{5,6},{6,7},{7,8},{8,9},{9,10},{10,1... | collective-permute-start | bytes 196616 | tf_op jit(solution)/shard_map/ppermute | solution.py:576
  72.5 4.9 %collective-permute-start.15 = (f32[16,8,128]{2,1,0:T(8,128)S(1)}, f32[16,8,128]{2,1,0:T(8,128)S(1)}, u32[]{:S(2)}, u32[]{:S(2)}) collective-permute-start(f32[16,8,128]{2,1,0:T(8,128)S(1)} %get-tuple-element.68), channel_id=1, source_target_pairs={{0,15},{1,0},{2,1},{3,2},{4,3},{5,4},{6,5},{7,6},{8,7},{9,8},{10,9... | collective-permute-start | bytes 196616 | tf_op jit(solution)/shard_map/ppermute | solution.py:577

commit v8 on v7

--- a/solution.py
+++ b/solution.py
@@ -156,7 +156,7 @@
 FINE_Q, FINE_Q_ROWS = corner_plan(4, 1, 8, 0)
 FINE_R, FINE_R_ROWS = corner_plan(4, 1, 4, 4)
 MID_Q, MID_Q_ROWS = corner_plan(2, 1, 8, 0)
-MID_R, MID_R_ROWS = corner_plan(2, 1, 6, 6)
+MID_R, MID_R_ROWS = corner_plan(2, 1, 6, 8)
 
 
 def scale_kernel(load_hbm, density_hbm, void_hbm, up, down, root, left, right, both, void, sems):
@@ -295,7 +295,7 @@
         for i in range(16):
             out[12 * i : 12 * i + 12] = mid_q[i, 2:14]
         for i in range(12):
-            out[192 + 12 * i : 204 + 12 * i] = mid_r[2 * start + i, 2:14]
+            out[192 + 8 * i : 200 + 8 * i] = mid_r[2 * start + i, 4:12]
     for i in range(16):
         mid_right[8 * i : 8 * i + 8] = mid_q[i, 2:10]
         mid_left[8 * i : 8 * i + 8] = mid_q[i, 6:14]
@@ -329,29 +329,36 @@
     def _():
         low[0:96] = jnp.zeros((96, LANES), F32)
         low[96:192] = second[0:96]
-        low[192:240] = jnp.zeros((48, LANES), F32)
-        low[240:336] = second[192:288]
+        low[192:224] = jnp.zeros((32, LANES), F32)
+        low[224:288] = second[192:256]
 
     @pl.when(gz == count - 2)
     def _():
         high[0:96] = second[96:192]
         high[96:192] = jnp.zeros((96, LANES), F32)
-        high[192:288] = second[240:336]
-        high[288:336] = jnp.zeros((48, LANES), F32)
-
-
-def mid_rows(low, high, field, side, layer, k, start, stop):
-    at = 12 * (2 * layer + k) + (0 if field == 0 else 144 if side == 0 else 192)
+        high[192:256] = second[224:288]
+        high[256:288] = jnp.zeros((32, LANES), F32)
+
+
+def mid_rows(low, high, side, layer, k, start, stop):
+    at = 12 * (2 * layer + k)
     return (low, high)[side][at + start : at + stop]
+
+
+def mid_root_rows(low, high, side, layer, k):
+    at = 192 + 8 * (2 * (layer - 2 if side == 0 else layer) + k)
+    return (low, high)[side][at : at + 8]
 
 
 def mid_pack_kernel(counts, first, second, low, high, left, right):
     mid_sides(counts[0], lax.axis_index("gz"), first, second, low, high)
-    for field, plan, base in ((0, MID_Q, 0), (1, MID_R, MID_Q_ROWS)):
-        for side, layer, k, n, at in plan:
-            at += base
-            right[at : at + n] = mid_rows(low, high, field, side, layer, k, 8 - n, 8)
-            left[at : at + n] = mid_rows(low, high, field, side, layer, k, 4, 4 + n)
+    for side, layer, k, n, at in MID_Q:
+        right[at : at + n] = mid_rows(low, high, side, layer, k, 8 - n, 8)
+        left[at : at + n] = mid_rows(low, high, side, layer, k, 4, 4 + n)
+    for side, layer, k, n, at in MID_R:
+        at += MID_Q_ROWS
+        right[at : at + n] = mid_root_rows(low, high, side, layer, k)
+        left[at : at + n] = mid_root_rows(low, high, side, layer, k)
 
 
 def mid_pre_kernel(counts, *refs):
@@ -373,7 +380,7 @@
         natural[i, 0:8] = blank
         natural[i, 24:32] = blank
         natural[i, 8 - n : 8] = on_left * far_left[at : at + n]
-        natural[i, 8:20] = mid_rows(low, high, 0, side, layer, k, 0, 12)
+        natural[i, 8:20] = mid_rows(low, high, side, layer, k, 0, 12)
         natural[i, 20:28] = blank
         natural[i, 20 : 20 + n] = on_right * far_right[at : at + n]
 
@@ -393,9 +400,9 @@
     for side, layer, k, n, at in MID_R:
         i = 2 * (layer - 2 if side == 0 else 14 + layer) + k
         at += MID_Q_ROWS
-        natural[i, 8 - n : 8] = on_left * far_left[at : at + n]
-        natural[i, 8:20] = mid_rows(low, high, 1, side, layer, k, 0, 12)
-        natural[i, 20 : 20 + n] = on_right * far_right[at : at + n]
+        natural[i, 2:10] = on_left * far_left[at : at + n]
+        natural[i, 10:18] = mid_root_rows(low, high, side, layer, k)
+        natural[i, 18:26] = on_right * far_right[at : at + n]
 
     def roots(z):
         for k in range(2):
@@ -600,7 +607,7 @@
     fine_q, fine_y, fine_r, mid_q, mid_r, first, second, to_left, to_right = call(
         with_counts(fine_pre_kernel),
         (low, up, root, high, left, right, far_left, far_right),
-        [fine, (8, 16, 8, LANES), (18, 16, 8, LANES)] + [(16, 16, LANES)] * 2 + [(336, LANES)] * 2 + [(224, LANES)] * 2,
+        [fine, (8, 16, 8, LANES), (18, 16, 8, LANES)] + [(16, 16, LANES)] * 2 + [(288, LANES)] * 2 + [(224, LANES)] * 2,
         [(96, 32, LANES)] + [fine] * 4,
     )
     pairs = mid_pairs(lax.axis_size("gz"))
@@ -608,7 +615,7 @@
     left, right = turn(to_left, to_right)
     first, second, left, right = lax.optimization_barrier((first, second, left, right))
     low, high, to_left, to_right = call(
-        with_counts(mid_pack_kernel), (first, second), [(336, LANES)] * 2 + [(MID_Q_ROWS + MID_R_ROWS, LANES)] * 2
+        with_counts(mid_pack_kernel), (first, second), [(288, LANES)] * 2 + [(MID_Q_ROWS + MID_R_ROWS, LANES)] * 2
     )
     far_left, far_right = turn(to_left, to_right)
     mid = (24, 8, 8, LANES)

time: 81.6 us -> 80.8 us (level)
    ppermute x1, waiting for transfers between devices: 2.44 us -> 1.62 us  [on_device(): lax.ppermute(second, 'gz', pairs[1])]
where the time goes in v8:
time: 80.8 us; the launch traced here: 80.5 us
  waiting for transfers between devices  35.3 us (44%)
  starting transfers between devices  34.7 us (43%)
  Pallas kernels  9.82 us (12%)
    ppermute x5, waiting for transfers between devices, turn(): lax.ppermute(to_left, 'xy', [(i, (i - 1) % count) for i in range(count)])  18.3 us
    ppermute x5, starting transfers between devices, turn(): lax.ppermute(to_right, 'xy', [(i, (i + 1) % count) for i in range(count)])  14.4 us
    ppermute x5, waiting for transfers between devices, turn(): lax.ppermute(to_right, 'xy', [(i, (i + 1) % count) for i in range(count)])  12 us
    ppermute x4, starting transfers between devices, send(): return lax.ppermute(block, axis, pairs)  11.5 us
    pallas_call x7, Pallas kernels, call(): pl.pallas_call(kernel, out_shape=[jax.ShapeDtypeStruct(s, F32) for s in o...  9.82 us
    ppermute x1, starting transfers between devices, on_device(): lax.ppermute(first, 'gz', pairs[0])  6.64 us
    ppermute x4, waiting for transfers between devices, send(): return lax.ppermute(block, axis, pairs)  3.4 us
    ppermute x1, starting transfers between devices, on_device(): lax.ppermute(second, 'gz', pairs[1])  1.92 us
  transfers between devices with their start and end apart: 16, of which 12 were waited for; matrix products, arithmetic and copies ran while one was open for 0% of the time, Pallas kernels for 0%

profile of v8, /device:TPU:245, one launch (start us, length us, event | category | flops | bytes accessed | tf_op | source)
XLA Modules:
  0.0 80.5 jit_solution(7297999667562843764)
XLA Ops:
  0.6 1.6 %shard_map.50 = (f32[52,16,128]{2,1,0:T(8,128)S(1)}, f32[52,16,128]{2,1,0:T(8,128)S(1)}, f32[32,16,128]{2,1,0:T(8,128)S(1)}, f32[416,128]{1,0:T(8,128)S(1)}, f32[416,128]{1,0:T(8,128)S(1)}) custom-call(f32[8,16,512]{2,1,0:T(8,128)} %load_hbm.1, f32[8,16,512]{2,1,0:T(8,128)} %density_hbm.1, s32[1,2,64]{2,1,0:T(2,128)} %void_hbm.1), custom_call_target="tpu_custom_call" | custom-call | tf_op jit(solution)/shard_map/pallas_call | solution.py:565
  2.2 3.0 %collective-permute-start.1 = (f32[52,16,128]{2,1,0:T(8,128)S(1)}, f32[52,16,128]{2,1,0:T(8,128)S(1)}, u32[]{:S(2)}, u32[]{:S(2)}) collective-permute-start(f32[52,16,128]{2,1,0:T(8,128)S(1)} %get-tuple-element.40), channel_id=1, source_target_pairs={{16,0},{32,16},{48,32},{64,48},{80,64},{96,80},{112,96},{128,112},... | collective-permute-start | bytes 1277960 | tf_op jit(solution)/shard_map/ppermute | solution.py:578
  5.2 2.3 %collective-permute-start = (f32[52,16,128]{2,1,0:T(8,128)S(1)}, f32[52,16,128]{2,1,0:T(8,128)S(1)}, u32[]{:S(2)}, u32[]{:S(2)}) collective-permute-start(f32[52,16,128]{2,1,0:T(8,128)S(1)} %get-tuple-element.39.refs_1_), channel_id=1, source_target_pairs={{0,16},{16,32},{32,48},{48,64},{64,80},{80,96},{96,112},{112,128},... | collective-permute-start | bytes 1277960 | tf_op jit(solution)/shard_map/ppermute | solution.py:578
  7.5 4.4 %collective-permute-start.2 = (f32[416,128]{1,0:T(8,128)S(1)}, f32[416,128]{1,0:T(8,128)S(1)}, u32[]{:S(2)}, u32[]{:S(2)}) collective-permute-start(f32[416,128]{1,0:T(8,128)S(1)} %get-tuple-element.41), channel_id=1, source_target_pairs={{0,1},{1,2},{2,3},{3,4},{4,5},{5,6},{6,7},{7,8},{8,9},{9,10},{10,1... | collective-permute-start | bytes 638984 | tf_op jit(solution)/shard_map/ppermute | solution.py:583
  12.0 2.8 %collective-permute-done.2.refs_4_ = f32[416,128]{1,0:T(8,128)S(1)} collective-permute-done((f32[416,128]{1,0:T(8,128)S(1)}, f32[416,128]{1,0:T(8,128)S(1)}, u32[]{:S(2)}, u32[]{:S(2)}) %collective-permute-start.2) | collective-permute-done | bytes 213024 | tf_op jit(solution)/shard_map/ppermute | solution.py:583
  14.8 3.7 %collective-permute-done.3.refs_5_ = f32[416,128]{1,0:T(8,128)S(1)} collective-permute-done((f32[416,128]{1,0:T(8,128)S(1)}, f32[416,128]{1,0:T(8,128)S(1)}, u32[]{:S(2)}, u32[]{:S(2)}) %collective-permute-start.3) | collective-permute-done | bytes 213024 | tf_op jit(solution)/shard_map/ppermute | solution.py:584
  18.4 0.1 shard_map.51
  18.5 4.1 %collective-permute-start.4 = (f32[560,128]{1,0:T(8,128)S(1)}, f32[560,128]{1,0:T(8,128)S(1)}, u32[]{:S(2)}, u32[]{:S(2)}) collective-permute-start(f32[560,128]{1,0:T(8,128)S(1)} %get-tuple-element.48), channel_id=1, source_target_pairs={{0,1},{1,2},{2,3},{3,4},{4,5},{5,6},{6,7},{7,8},{8,9},{9,10},{10,1... | collective-permute-start | bytes 860168 | tf_op jit(solution)/shard_map/ppermute | solution.py:583
  22.6 0.0 collective-permute-start.5
  22.6 3.6 %collective-permute-done.4.refs_6_ = f32[560,128]{1,0:T(8,128)S(1)} collective-permute-done((f32[560,128]{1,0:T(8,128)S(1)}, f32[560,128]{1,0:T(8,128)S(1)}, u32[]{:S(2)}, u32[]{:S(2)}) %collective-permute-start.4) | collective-permute-done | bytes 286752 | tf_op jit(solution)/shard_map/ppermute | solution.py:583
  26.2 3.7 %collective-permute-done.5.refs_7_ = f32[560,128]{1,0:T(8,128)S(1)} collective-permute-done((f32[560,128]{1,0:T(8,128)S(1)}, f32[560,128]{1,0:T(8,128)S(1)}, u32[]{:S(2)}, u32[]{:S(2)}) %collective-permute-start.5) | collective-permute-done | bytes 286752 | tf_op jit(solution)/shard_map/ppermute | solution.py:584
  29.9 2.7 %shard_map.52 = (f32[24,16,8,128]{3,2,1,0:T(8,128)S(1)}, f32[8,16,8,128]{3,2,1,0:T(8,128)S(1)}, f32[18,16,8,128]{3,2,1,0:T(8,128)S(1)}, f32[16,16,128]{2,1,0:T(8...) custom-call(f32[52,16,128]{2,1,0:T(8,128)S(1)} %collective-permute-d, ...), custom_call_target="tpu_custom_call" | custom-call | tf_op jit(solution)/shard_map/pallas_call | solution.py:565
  32.6 6.6 %collective-permute-start.6 = (f32[288,128]{1,0:T(8,128)S(1)}, f32[288,128]{1,0:T(8,128)S(1)}, u32[]{:S(2)}, u32[]{:S(2)}) collective-permute-start(f32[288,128]{1,0:T(8,128)S(1)} %get-tuple-element.50), channel_id=1, source_target_pairs={{0,32},{16,48},{32,64},{48,16},{64,96},{80,112},{96,128},{112,80},... | collective-permute-start | bytes 442376 | tf_op jit(solution)/shard_map/ppermute | solution.py:614
  39.2 1.9 %collective-permute-start.7 = (f32[288,128]{1,0:T(8,128)S(1)}, f32[288,128]{1,0:T(8,128)S(1)}, u32[]{:S(2)}, u32[]{:S(2)}) collective-permute-start(f32[288,128]{1,0:T(8,128)S(1)} %get-tuple-element.51), channel_id=1, source_target_pairs={{32,0},{48,80},{64,32},{80,48},{96,64},{112,144},{128,96},{144,112... | collective-permute-start | bytes 442376 | tf_op jit(solution)/shard_map/ppermute | solution.py:614
  41.2 0.3 collective-permute-start.8
  41.5 0.2 collective-permute-start.9
  41.7 1.6 %collective-permute-done.8.refs_4_ = f32[224,128]{1,0:T(8,128)S(1)} collective-permute-done((f32[224,128]{1,0:T(8,128)S(1)}, f32[224,128]{1,0:T(8,128)S(1)}, u32[]{:S(2)}, u32[]{:S(2)}) %collective-permute-start.8) | collective-permute-done | bytes 114720 | tf_op jit(solution)/shard_map/ppermute | solution.py:583
  43.3 3.6 %collective-permute-done.9.refs_5_ = f32[224,128]{1,0:T(8,128)S(1)} collective-permute-done((f32[224,128]{1,0:T(8,128)S(1)}, f32[224,128]{1,0:T(8,128)S(1)}, u32[]{:S(2)}, u32[]{:S(2)}) %collective-permute-start.9) | collective-permute-done | bytes 114720 | tf_op jit(solution)/shard_map/ppermute | solution.py:584
  46.9 0.0 collective-permute-done.6.refs_0_
  46.9 1.6 %collective-permute-done.7.refs_1_ = f32[288,128]{1,0:T(8,128)S(1)} collective-permute-done((f32[288,128]{1,0:T(8,128)S(1)}, f32[288,128]{1,0:T(8,128)S(1)}, u32[]{:S(2)}, u32[]{:S(2)}) %collective-permute-start.7) | collective-permute-done | bytes 147488 | tf_op jit(solution)/shard_map/ppermute | solution.py:614
  48.5 0.1 shard_map.53
  48.6 4.4 %collective-permute-start.10 = (f32[408,128]{1,0:T(8,128)S(1)}, f32[408,128]{1,0:T(8,128)S(1)}, u32[]{:S(2)}, u32[]{:S(2)}) collective-permute-start(f32[408,128]{1,0:T(8,128)S(1)} %get-tuple-element.62), channel_id=1, source_target_pairs={{0,1},{1,2},{2,3},{3,4},{4,5},{5,6},{6,7},{7,8},{8,9},{9,10},{10,1... | collective-permute-start | bytes 626696 | tf_op jit(solution)/shard_map/ppermute | solution.py:583
  53.0 2.7 %collective-permute-done.10.refs_6_ = f32[408,128]{1,0:T(8,128)S(1)} collective-permute-done((f32[408,128]{1,0:T(8,128)S(1)}, f32[408,128]{1,0:T(8,128)S(1)}, u32[]{:S(2)}, u32[]{:S(2)}) %collective-permute-start.10) | collective-permute-done | bytes 208928 | tf_op jit(solution)/shard_map/ppermute | solution.py:583
  55.8 3.7 %collective-permute-done.11.refs_7_ = f32[408,128]{1,0:T(8,128)S(1)} collective-permute-done((f32[408,128]{1,0:T(8,128)S(1)}, f32[408,128]{1,0:T(8,128)S(1)}, u32[]{:S(2)}, u32[]{:S(2)}) %collective-permute-start.11) | collective-permute-done | bytes 208928 | tf_op jit(solution)/shard_map/ppermute | solution.py:584
  59.5 1.4 %shard_map.54 = (f32[24,8,8,128]{3,2,1,0:T(8,128)S(1)}, f32[10,8,8,128]{3,2,1,0:T(8,128)S(1)}, f32[20,8,8,128]{3,2,1,0:T(8,128)S(1)}, f32[8,16,128]{2,1,0:T(8,12...) custom-call(f32[288,128]{1,0:T(8,128)S(1)} %get-tuple-element.56.refs_0_, ...), custom_call_target="tpu_custom_call" | custom-call | tf_op jit(solution)/shard_map/pallas_call | solution.py:565
  60.9 1.9 %collective-permute-start.12 = (f32[4,16,128]{2,1,0:T(8,128)S(1)}, f32[4,16,128]{2,1,0:T(8,128)S(1)}, u32[]{:S(2)}, u32[]{:S(2)}) collective-permute-start(f32[4,16,128]{2,1,0:T(8,128)S(1)} %get-tuple-element.64), channel_id=1, source_target_pairs={{0,32},{16,48},{32,64},{48,80},{64,96},{80,112},{96,128},{112,144}... | collective-permute-start | bytes 98312 | tf_op jit(solution)/shard_map/ppermute | solution.py:578
  62.8 4.3 %collective-permute-start.13 = (f32[4,16,128]{2,1,0:T(8,128)S(1)}, f32[4,16,128]{2,1,0:T(8,128)S(1)}, u32[]{:S(2)}, u32[]{:S(2)}) collective-permute-start(f32[4,16,128]{2,1,0:T(8,128)S(1)} %get-tuple-element.66), channel_id=1, source_target_pairs={{32,0},{48,16},{64,32},{80,48},{96,64},{112,80},{128,96},{144,112}... | collective-permute-start | bytes 98312 | tf_op jit(solution)/shard_map/ppermute | solution.py:578
  67.1 3.4 %collective-permute-done.13.refs_2_ = f32[4,16,128]{2,1,0:T(8,128)S(1)} collective-permute-done((f32[4,16,128]{2,1,0:T(8,128)S(1)}, f32[4,16,128]{2,1,0:T(8,128)S(1)}, u32[]{:S(2)}, u32[]{:S(2)}) %collective-permute-start.13) | collective-permute-done | bytes 32800 | tf_op jit(solution)/shard_map/ppermute | solution.py:578
  70.5 1.2 %collective-permute-start.14 = (f32[16,8,128]{2,1,0:T(8,128)S(1)}, f32[16,8,128]{2,1,0:T(8,128)S(1)}, u32[]{:S(2)}, u32[]{:S(2)}) collective-permute-start(f32[16,8,128]{2,1,0:T(8,128)S(1)} %get-tuple-element.67), channel_id=1, source_target_pairs={{0,1},{1,2},{2,3},{3,4},{4,5},{5,6},{6,7},{7,8},{8,9},{9,10},{10,1... | collective-permute-start | bytes 196616 | tf_op jit(solution)/shard_map/ppermute | solution.py:583
  71.6 1.3 %collective-permute-done.14.refs_3_ = f32[16,8,128]{2,1,0:T(8,128)S(1)} collective-permute-done((f32[16,8,128]{2,1,0:T(8,128)S(1)}, f32[16,8,128]{2,1,0:T(8,128)S(1)}, u32[]{:S(2)}, u32[]{:S(2)}) %collective-permute-start.14) | collective-permute-done | bytes 65568 | tf_op jit(solution)/shard_map/ppermute | solution.py:583
  73.0 3.6 %collective-permute-done.15.refs_4_ = f32[16,8,128]{2,1,0:T(8,128)S(1)} collective-permute-done((f32[16,8,128]{2,1,0:T(8,128)S(1)}, f32[16,8,128]{2,1,0:T(8,128)S(1)}, u32[]{:S(2)}, u32[]{:S(2)}) %collective-permute-start.15) | collective-permute-done | bytes 65568 | tf_op jit(solution)/shard_map/ppermute | solution.py:584
  76.5 4.0 %shard_map.56 = (f32[8,16,512]{2,1,0:T(8,128)}, f32[8,16,512]{2,1,0:T(8,128)}) custom-call(f32[4,16,128]{2,1,0:T(8,128)S(1)} %collective-permute-done.12.refs_0_, f32[8,16,128]{2,1,0:T(8,128)S(1)} %get-tuple-element.65.refs_1_, f32[4,16,128]{2,1,0:T(8,128)S(1)} %collective-permute-done.13.refs_2_, f32[16,8,128]{2,1,0:T(8,128)S(1)} %collective-permute-done.14.refs_3_, ...), custom_call_target="tpu_custom_call" | custom-call | tf_op jit(solution)/shard_map/pallas_call | solution.py:565
  (7 shorter events, 0.0 us)
Async XLA Ops:
  2.2 16.2 %collective-permute-start.1 = (f32[52,16,128]{2,1,0:T(8,128)S(1)}, f32[52,16,128]{2,1,0:T(8,128)S(1)}, u32[]{:S(2)}, u32[]{:S(2)}) collective-permute-start(f32[52,16,128]{2,1,0:T(8,128)S(1)} %get-tuple-element.40), channel_id=1, source_target_pairs={{16,0},{32,16},{48,32},{64,48},{80,64},{96,80},{112,96},{128,112},... | collective-permute-start | bytes 1277960 | tf_op jit(solution)/shard_map/ppermute | solution.py:578
  5.2 13.2 %collective-permute-start = (f32[52,16,128]{2,1,0:T(8,128)S(1)}, f32[52,16,128]{2,1,0:T(8,128)S(1)}, u32[]{:S(2)}, u32[]{:S(2)}) collective-permute-start(f32[52,16,128]{2,1,0:T(8,128)S(1)} %get-tuple-element.39.refs_1_), channel_id=1, source_target_pairs={{0,16},{16,32},{32,48},{48,64},{64,80},{80,96},{96,112},{112,128},... | collective-permute-start | bytes 1277960 | tf_op jit(solution)/shard_map/ppermute | solution.py:578
  7.5 7.2 %collective-permute-start.2 = (f32[416,128]{1,0:T(8,128)S(1)}, f32[416,128]{1,0:T(8,128)S(1)}, u32[]{:S(2)}, u32[]{:S(2)}) collective-permute-start(f32[416,128]{1,0:T(8,128)S(1)} %get-tuple-element.41), channel_id=1, source_target_pairs={{0,1},{1,2},{2,3},{3,4},{4,5},{5,6},{6,7},{7,8},{8,9},{9,10},{10,1... | collective-permute-start | bytes 638984 | tf_op jit(solution)/shard_map/ppermute | solution.py:583
  12.0 6.5 %collective-permute-start.3 = (f32[416,128]{1,0:T(8,128)S(1)}, f32[416,128]{1,0:T(8,128)S(1)}, u32[]{:S(2)}, u32[]{:S(2)}) collective-permute-start(f32[416,128]{1,0:T(8,128)S(1)} %get-tuple-element.42), channel_id=1, source_target_pairs={{0,15},{1,0},{2,1},{3,2},{4,3},{5,4},{6,5},{7,6},{8,7},{9,8},{10,9... | collective-permute-start | bytes 638984 | tf_op jit(solution)/shard_map/ppermute | solution.py:584
  18.5 7.7 %collective-permute-start.4 = (f32[560,128]{1,0:T(8,128)S(1)}, f32[560,128]{1,0:T(8,128)S(1)}, u32[]{:S(2)}, u32[]{:S(2)}) collective-permute-start(f32[560,128]{1,0:T(8,128)S(1)} %get-tuple-element.48), channel_id=1, source_target_pairs={{0,1},{1,2},{2,3},{3,4},{4,5},{5,6},{6,7},{7,8},{8,9},{9,10},{10,1... | collective-permute-start | bytes 860168 | tf_op jit(solution)/shard_map/ppermute | solution.py:583
  22.6 7.3 %collective-permute-start.5 = (f32[560,128]{1,0:T(8,128)S(1)}, f32[560,128]{1,0:T(8,128)S(1)}, u32[]{:S(2)}, u32[]{:S(2)}) collective-permute-start(f32[560,128]{1,0:T(8,128)S(1)} %get-tuple-element.49), channel_id=1, source_target_pairs={{0,15},{1,0},{2,1},{3,2},{4,3},{5,4},{6,5},{7,6},{8,7},{9,8},{10,9... | collective-permute-start | bytes 860168 | tf_op jit(solution)/shard_map/ppermute | solution.py:584
  32.6 14.3 %collective-permute-start.6 = (f32[288,128]{1,0:T(8,128)S(1)}, f32[288,128]{1,0:T(8,128)S(1)}, u32[]{:S(2)}, u32[]{:S(2)}) collective-permute-start(f32[288,128]{1,0:T(8,128)S(1)} %get-tuple-element.50), channel_id=1, source_target_pairs={{0,32},{16,48},{32,64},{48,16},{64,96},{80,112},{96,128},{112,80},... | collective-permute-start | bytes 442376 | tf_op jit(solution)/shard_map/ppermute | solution.py:614
  39.2 9.3 %collective-permute-start.7 = (f32[288,128]{1,0:T(8,128)S(1)}, f32[288,128]{1,0:T(8,128)S(1)}, u32[]{:S(2)}, u32[]{:S(2)}) collective-permute-start(f32[288,128]{1,0:T(8,128)S(1)} %get-tuple-element.51), channel_id=1, source_target_pairs={{32,0},{48,80},{64,32},{80,48},{96,64},{112,144},{128,96},{144,112... | collective-permute-start | bytes 442376 | tf_op jit(solution)/shard_map/ppermute | solution.py:614
  41.2 2.1 %collective-permute-start.8 = (f32[224,128]{1,0:T(8,128)S(1)}, f32[224,128]{1,0:T(8,128)S(1)}, u32[]{:S(2)}, u32[]{:S(2)}) collective-permute-start(f32[224,128]{1,0:T(8,128)S(1)} %get-tuple-element.52), channel_id=1, source_target_pairs={{0,1},{1,2},{2,3},{3,4},{4,5},{5,6},{6,7},{7,8},{8,9},{9,10},{10,1... | collective-permute-start | bytes 344072 | tf_op jit(solution)/shard_map/ppermute | solution.py:583
  41.5 5.4 %collective-permute-start.9 = (f32[224,128]{1,0:T(8,128)S(1)}, f32[224,128]{1,0:T(8,128)S(1)}, u32[]{:S(2)}, u32[]{:S(2)}) collective-permute-start(f32[224,128]{1,0:T(8,128)S(1)} %get-tuple-element.53), channel_id=1, source_target_pairs={{0,15},{1,0},{2,1},{3,2},{4,3},{5,4},{6,5},{7,6},{8,7},{9,8},{10,9... | collective-permute-start | bytes 344072 | tf_op jit(solution)/shard_map/ppermute | solution.py:584
  48.6 7.2 %collective-permute-start.10 = (f32[408,128]{1,0:T(8,128)S(1)}, f32[408,128]{1,0:T(8,128)S(1)}, u32[]{:S(2)}, u32[]{:S(2)}) collective-permute-start(f32[408,128]{1,0:T(8,128)S(1)} %get-tuple-element.62), channel_id=1, source_target_pairs={{0,1},{1,2},{2,3},{3,4},{4,5},{5,6},{6,7},{7,8},{8,9},{9,10},{10,1... | collective-permute-start | bytes 626696 | tf_op jit(solution)/shard_map/ppermute | solution.py:583
  53.0 6.4 %collective-permute-start.11 = (f32[408,128]{1,0:T(8,128)S(1)}, f32[408,128]{1,0:T(8,128)S(1)}, u32[]{:S(2)}, u32[]{:S(2)}) collective-permute-start(f32[408,128]{1,0:T(8,128)S(1)} %get-tuple-element.63), channel_id=1, source_target_pairs={{0,15},{1,0},{2,1},{3,2},{4,3},{5,4},{6,5},{7,6},{8,7},{9,8},{10,9... | collective-permute-start | bytes 626696 | tf_op jit(solution)/shard_map/ppermute | solution.py:584
  60.9 6.2 %collective-permute-start.12 = (f32[4,16,128]{2,1,0:T(8,128)S(1)}, f32[4,16,128]{2,1,0:T(8,128)S(1)}, u32[]{:S(2)}, u32[]{:S(2)}) collective-permute-start(f32[4,16,128]{2,1,0:T(8,128)S(1)} %get-tuple-element.64), channel_id=1, source_target_pairs={{0,32},{16,48},{32,64},{48,80},{64,96},{80,112},{96,128},{112,144}... | collective-permute-start | bytes 98312 | tf_op jit(solution)/shard_map/ppermute | solution.py:578
  62.8 7.7 %collective-permute-start.13 = (f32[4,16,128]{2,1,0:T(8,128)S(1)}, f32[4,16,128]{2,1,0:T(8,128)S(1)}, u32[]{:S(2)}, u32[]{:S(2)}) collective-permute-start(f32[4,16,128]{2,1,0:T(8,128)S(1)} %get-tuple-element.66), channel_id=1, source_target_pairs={{32,0},{48,16},{64,32},{80,48},{96,64},{112,80},{128,96},{144,112}... | collective-permute-start | bytes 98312 | tf_op jit(solution)/shard_map/ppermute | solution.py:578
  70.5 2.5 %collective-permute-start.14 = (f32[16,8,128]{2,1,0:T(8,128)S(1)}, f32[16,8,128]{2,1,0:T(8,128)S(1)}, u32[]{:S(2)}, u32[]{:S(2)}) collective-permute-start(f32[16,8,128]{2,1,0:T(8,128)S(1)} %get-tuple-element.67), channel_id=1, source_target_pairs={{0,1},{1,2},{2,3},{3,4},{4,5},{5,6},{6,7},{7,8},{8,9},{9,10},{10,1... | collective-permute-start | bytes 196616 | tf_op jit(solution)/shard_map/ppermute | solution.py:583
  71.6 4.9 %collective-permute-start.15 = (f32[16,8,128]{2,1,0:T(8,128)S(1)}, f32[16,8,128]{2,1,0:T(8,128)S(1)}, u32[]{:S(2)}, u32[]{:S(2)}) collective-permute-start(f32[16,8,128]{2,1,0:T(8,128)S(1)} %get-tuple-element.68), channel_id=1, source_target_pairs={{0,15},{1,0},{2,1},{3,2},{4,3},{5,4},{6,5},{7,6},{8,7},{9,8},{10,9... | collective-permute-start | bytes 196616 | tf_op jit(solution)/shard_map/ppermute | solution.py:584

commit v9 on v8

--- a/solution.py
+++ b/solution.py
@@ -137,6 +137,7 @@
 
 
 CORNER = [8, 8, 8, 8, 7, 6, 5, 4]
+MID_CORNER = [8, 8, 8, 8, 7, 8, 7, 6]
 
 
 def corner_plan(blocks, first, last, rows):
@@ -147,15 +148,15 @@
             if not first <= away <= last:
                 continue
             for k in range(blocks):
-                count = rows if rows else CORNER[away - 1]
+                count = rows if isinstance(rows, int) else rows[away - 1]
                 plan.append((side, layer, k, count, at))
                 at += count
     return plan, at
 
 
-FINE_Q, FINE_Q_ROWS = corner_plan(4, 1, 8, 0)
+FINE_Q, FINE_Q_ROWS = corner_plan(4, 1, 8, CORNER)
 FINE_R, FINE_R_ROWS = corner_plan(4, 1, 4, 4)
-MID_Q, MID_Q_ROWS = corner_plan(2, 1, 8, 0)
+MID_Q, MID_Q_ROWS = corner_plan(2, 1, 8, MID_CORNER)
 MID_R, MID_R_ROWS = corner_plan(2, 1, 6, 8)
 
 
@@ -292,10 +293,13 @@
     loop(0, 8, fold)
     skip = jnp.where(gz % 4 == 3, 0, 2)
     for out, start in ((early, skip), (late, 2 - skip)):
-        for i in range(16):
-            out[12 * i : 12 * i + 12] = mid_q[i, 2:14]
+        for near in range(8):
+            layer = jnp.where(start == 2, 7 - near, near)
+            for k in range(2):
+                at, count = mid_place(near, k)
+                out[at : at + count] = mid_q[2 * layer + k, 8 - count // 2 : 8 + count // 2]
         for i in range(12):
-            out[192 + 8 * i : 200 + 8 * i] = mid_r[2 * start + i, 4:12]
+            out[168 + 8 * i : 176 + 8 * i] = mid_r[2 * start + i, 4:12]
     for i in range(16):
         mid_right[8 * i : 8 * i + 8] = mid_q[i, 2:10]
         mid_left[8 * i : 8 * i + 8] = mid_q[i, 6:14]
@@ -327,34 +331,40 @@
 
     @pl.when(gz == 1)
     def _():
-        low[0:96] = jnp.zeros((96, LANES), F32)
-        low[96:192] = second[0:96]
-        low[192:224] = jnp.zeros((32, LANES), F32)
-        low[224:288] = second[192:256]
+        for near in range(4):
+            low[24 * near : 24 * near + 24] = second[72 - 24 * near : 96 - 24 * near]
+        low[96:200] = jnp.zeros((104, LANES), F32)
+        low[200:264] = second[168:232]
 
     @pl.when(gz == count - 2)
     def _():
-        high[0:96] = second[96:192]
-        high[96:192] = jnp.zeros((96, LANES), F32)
-        high[192:256] = second[224:288]
-        high[256:288] = jnp.zeros((32, LANES), F32)
-
-
-def mid_rows(low, high, side, layer, k, start, stop):
-    at = 12 * (2 * layer + k)
-    return (low, high)[side][at + start : at + stop]
+        for near in range(4):
+            high[24 * near : 24 * near + 24] = second[72 - 24 * near : 96 - 24 * near]
+        high[96:168] = jnp.zeros((72, LANES), F32)
+        high[168:232] = second[200:264]
+        high[232:264] = jnp.zeros((32, LANES), F32)
+
+
+def mid_place(near, k):
+    return (24 * near + 12 * k, 12) if near < 5 else (120 + 16 * (near - 5) + 8 * k, 8)
+
+
+def mid_rows(low, high, side, layer, k):
+    at, count = mid_place(7 - layer if side == 0 else layer, k)
+    return (low, high)[side], at, count
 
 
 def mid_root_rows(low, high, side, layer, k):
-    at = 192 + 8 * (2 * (layer - 2 if side == 0 else layer) + k)
+    at = 168 + 8 * (2 * (layer - 2 if side == 0 else layer) + k)
     return (low, high)[side][at : at + 8]
 
 
 def mid_pack_kernel(counts, first, second, low, high, left, right):
     mid_sides(counts[0], lax.axis_index("gz"), first, second, low, high)
     for side, layer, k, n, at in MID_Q:
-        right[at : at + n] = mid_rows(low, high, side, layer, k, 8 - n, 8)
-        left[at : at + n] = mid_rows(low, high, side, layer, k, 4, 4 + n)
+        ref, place, count = mid_rows(low, high, side, layer, k)
+        right[at : at + n] = ref[place + 8 - n : place + 8]
+        left[at : at + n] = ref[place + count - 8 : place + count - 8 + n]
     for side, layer, k, n, at in MID_R:
         at += MID_Q_ROWS
         right[at : at + n] = mid_root_rows(low, high, side, layer, k)
@@ -379,10 +389,12 @@
         i = 32 * side + 2 * layer + k
         natural[i, 0:8] = blank
         natural[i, 24:32] = blank
-        natural[i, 8 - n : 8] = on_left * far_left[at : at + n]
-        natural[i, 8:20] = mid_rows(low, high, side, layer, k, 0, 12)
+        ref, place, count = mid_rows(low, high, side, layer, k)
+        first, last = 14 - count // 2, 14 + count // 2
         natural[i, 20:28] = blank
-        natural[i, 20 : 20 + n] = on_right * far_right[at : at + n]
+        natural[i, first:last] = ref[place : place + count]
+        natural[i, first - n : first] = on_left * far_left[at : at + n]
+        natural[i, last : last + n] = on_right * far_right[at : at + n]
 
     def begin(z):
         for k in range(2):
@@ -607,7 +619,7 @@
     fine_q, fine_y, fine_r, mid_q, mid_r, first, second, to_left, to_right = call(
         with_counts(fine_pre_kernel),
         (low, up, root, high, left, right, far_left, far_right),
-        [fine, (8, 16, 8, LANES), (18, 16, 8, LANES)] + [(16, 16, LANES)] * 2 + [(288, LANES)] * 2 + [(224, LANES)] * 2,
+        [fine, (8, 16, 8, LANES), (18, 16, 8, LANES)] + [(16, 16, LANES)] * 2 + [(264, LANES)] * 2 + [(224, LANES)] * 2,
         [(96, 32, LANES)] + [fine] * 4,
     )
     pairs = mid_pairs(lax.axis_size("gz"))
@@ -615,7 +627,7 @@
     left, right = turn(to_left, to_right)
     first, second, left, right = lax.optimization_barrier((first, second, left, right))
     low, high, to_left, to_right = call(
-        with_counts(mid_pack_kernel), (first, second), [(288, LANES)] * 2 + [(MID_Q_ROWS + MID_R_ROWS, LANES)] * 2
+        with_counts(mid_pack_kernel), (first, second), [(264, LANES)] * 2 + [(MID_Q_ROWS + MID_R_ROWS, LANES)] * 2
     )
     far_left, far_right = turn(to_left, to_right)
     mid = (24, 8, 8, LANES)

time: 80.8 us -> 80.5 us (level)
  no operation moved by 1% of the time
where the time goes in v9:
time: 80.5 us; the launch traced here: 80.3 us
  waiting for transfers between devices  35.1 us (44%)
  starting transfers between devices  34.5 us (43%)
  Pallas kernels  9.94 us (12%)
    ppermute x5, waiting for transfers between devices, turn(): lax.ppermute(to_left, 'xy', [(i, (i - 1) % count) for i in range(count)])  18.3 us
    ppermute x5, starting transfers between devices, turn(): lax.ppermute(to_right, 'xy', [(i, (i + 1) % count) for i in range(count)])  14.3 us
    ppermute x5, waiting for transfers between devices, turn(): lax.ppermute(to_right, 'xy', [(i, (i + 1) % count) for i in range(count)])  12.1 us
    ppermute x4, starting transfers between devices, send(): return lax.ppermute(block, axis, pairs)  11.5 us
    pallas_call x7, Pallas kernels, call(): pl.pallas_call(kernel, out_shape=[jax.ShapeDtypeStruct(s, F32) for s in o...  9.94 us
    ppermute x1, starting transfers between devices, on_device(): lax.ppermute(first, 'gz', pairs[0])  6.64 us
    ppermute x4, waiting for transfers between devices, send(): return lax.ppermute(block, axis, pairs)  3.4 us
    ppermute x1, starting transfers between devices, on_device(): lax.ppermute(second, 'gz', pairs[1])  1.92 us
  transfers between devices with their start and end apart: 16, of which 12 were waited for; matrix products, arithmetic and copies ran while one was open for 0% of the time, Pallas kernels for 0%

profile of v9, /device:TPU:245, one launch (start us, length us, event | category | flops | bytes accessed | tf_op | source)
XLA Modules:
  0.0 80.3 jit_solution(9371759806127674359)
XLA Ops:
  0.6 1.6 %shard_map.50 = (f32[52,16,128]{2,1,0:T(8,128)S(1)}, f32[52,16,128]{2,1,0:T(8,128)S(1)}, f32[32,16,128]{2,1,0:T(8,128)S(1)}, f32[416,128]{1,0:T(8,128)S(1)}, f32[416,128]{1,0:T(8,128)S(1)}) custom-call(f32[8,16,512]{2,1,0:T(8,128)} %load_hbm.1, f32[8,16,512]{2,1,0:T(8,128)} %density_hbm.1, s32[1,2,64]{2,1,0:T(2,128)} %void_hbm.1), custom_call_target="tpu_custom_call" | custom-call | tf_op jit(solution)/shard_map/pallas_call | solution.py:577
  2.2 3.0 %collective-permute-start.1 = (f32[52,16,128]{2,1,0:T(8,128)S(1)}, f32[52,16,128]{2,1,0:T(8,128)S(1)}, u32[]{:S(2)}, u32[]{:S(2)}) collective-permute-start(f32[52,16,128]{2,1,0:T(8,128)S(1)} %get-tuple-element.40), channel_id=1, source_target_pairs={{16,0},{32,16},{48,32},{64,48},{80,64},{96,80},{112,96},{128,112},... | collective-permute-start | bytes 1277960 | tf_op jit(solution)/shard_map/ppermute | solution.py:590
  5.2 2.3 %collective-permute-start = (f32[52,16,128]{2,1,0:T(8,128)S(1)}, f32[52,16,128]{2,1,0:T(8,128)S(1)}, u32[]{:S(2)}, u32[]{:S(2)}) collective-permute-start(f32[52,16,128]{2,1,0:T(8,128)S(1)} %get-tuple-element.39.refs_1_), channel_id=1, source_target_pairs={{0,16},{16,32},{32,48},{48,64},{64,80},{80,96},{96,112},{112,128},... | collective-permute-start | bytes 1277960 | tf_op jit(solution)/shard_map/ppermute | solution.py:590
  7.5 4.4 %collective-permute-start.2 = (f32[416,128]{1,0:T(8,128)S(1)}, f32[416,128]{1,0:T(8,128)S(1)}, u32[]{:S(2)}, u32[]{:S(2)}) collective-permute-start(f32[416,128]{1,0:T(8,128)S(1)} %get-tuple-element.41), channel_id=1, source_target_pairs={{0,1},{1,2},{2,3},{3,4},{4,5},{5,6},{6,7},{7,8},{8,9},{9,10},{10,1... | collective-permute-start | bytes 638984 | tf_op jit(solution)/shard_map/ppermute | solution.py:595
  12.0 0.0 collective-permute-start.3
  12.0 2.8 %collective-permute-done.2.refs_4_ = f32[416,128]{1,0:T(8,128)S(1)} collective-permute-done((f32[416,128]{1,0:T(8,128)S(1)}, f32[416,128]{1,0:T(8,128)S(1)}, u32[]{:S(2)}, u32[]{:S(2)}) %collective-permute-start.2) | collective-permute-done | bytes 213024 | tf_op jit(solution)/shard_map/ppermute | solution.py:595
  14.8 3.7 %collective-permute-done.3.refs_5_ = f32[416,128]{1,0:T(8,128)S(1)} collective-permute-done((f32[416,128]{1,0:T(8,128)S(1)}, f32[416,128]{1,0:T(8,128)S(1)}, u32[]{:S(2)}, u32[]{:S(2)}) %collective-permute-start.3) | collective-permute-done | bytes 213024 | tf_op jit(solution)/shard_map/ppermute | solution.py:596
  18.4 0.0 collective-permute-done.low.refs_0_
  18.4 0.1 shard_map.51
  18.5 4.1 %collective-permute-start.4 = (f32[560,128]{1,0:T(8,128)S(1)}, f32[560,128]{1,0:T(8,128)S(1)}, u32[]{:S(2)}, u32[]{:S(2)}) collective-permute-start(f32[560,128]{1,0:T(8,128)S(1)} %get-tuple-element.48), channel_id=1, source_target_pairs={{0,1},{1,2},{2,3},{3,4},{4,5},{5,6},{6,7},{7,8},{8,9},{9,10},{10,1... | collective-permute-start | bytes 860168 | tf_op jit(solution)/shard_map/ppermute | solution.py:595
  22.6 3.6 %collective-permute-done.4.refs_6_ = f32[560,128]{1,0:T(8,128)S(1)} collective-permute-done((f32[560,128]{1,0:T(8,128)S(1)}, f32[560,128]{1,0:T(8,128)S(1)}, u32[]{:S(2)}, u32[]{:S(2)}) %collective-permute-start.4) | collective-permute-done | bytes 286752 | tf_op jit(solution)/shard_map/ppermute | solution.py:595
  26.2 3.7 %collective-permute-done.5.refs_7_ = f32[560,128]{1,0:T(8,128)S(1)} collective-permute-done((f32[560,128]{1,0:T(8,128)S(1)}, f32[560,128]{1,0:T(8,128)S(1)}, u32[]{:S(2)}, u32[]{:S(2)}) %collective-permute-start.5) | collective-permute-done | bytes 286752 | tf_op jit(solution)/shard_map/ppermute | solution.py:596
  29.9 2.7 %shard_map.52 = (f32[24,16,8,128]{3,2,1,0:T(8,128)S(1)}, f32[8,16,8,128]{3,2,1,0:T(8,128)S(1)}, f32[18,16,8,128]{3,2,1,0:T(8,128)S(1)}, f32[16,16,128]{2,1,0:T(8...) custom-call(f32[52,16,128]{2,1,0:T(8,128)S(1)} %collective-permute-d, ...), custom_call_target="tpu_custom_call" | custom-call | tf_op jit(solution)/shard_map/pallas_call | solution.py:577
  32.6 6.6 %collective-permute-start.6 = (f32[264,128]{1,0:T(8,128)S(1)}, f32[264,128]{1,0:T(8,128)S(1)}, u32[]{:S(2)}, u32[]{:S(2)}) collective-permute-start(f32[264,128]{1,0:T(8,128)S(1)} %get-tuple-element.50), channel_id=1, source_target_pairs={{0,32},{16,48},{32,64},{48,16},{64,96},{80,112},{96,128},{112,80},... | collective-permute-start | bytes 405512 | tf_op jit(solution)/shard_map/ppermute | solution.py:626
  39.2 1.9 %collective-permute-start.7 = (f32[264,128]{1,0:T(8,128)S(1)}, f32[264,128]{1,0:T(8,128)S(1)}, u32[]{:S(2)}, u32[]{:S(2)}) collective-permute-start(f32[264,128]{1,0:T(8,128)S(1)} %get-tuple-element.51), channel_id=1, source_target_pairs={{32,0},{48,80},{64,32},{80,48},{96,64},{112,144},{128,96},{144,112... | collective-permute-start | bytes 405512 | tf_op jit(solution)/shard_map/ppermute | solution.py:626
  41.2 0.3 collective-permute-start.8
  41.5 0.2 collective-permute-start.9
  41.7 1.6 %collective-permute-done.8.refs_4_ = f32[224,128]{1,0:T(8,128)S(1)} collective-permute-done((f32[224,128]{1,0:T(8,128)S(1)}, f32[224,128]{1,0:T(8,128)S(1)}, u32[]{:S(2)}, u32[]{:S(2)}) %collective-permute-start.8) | collective-permute-done | bytes 114720 | tf_op jit(solution)/shard_map/ppermute | solution.py:595
  43.3 3.6 %collective-permute-done.9.refs_5_ = f32[224,128]{1,0:T(8,128)S(1)} collective-permute-done((f32[224,128]{1,0:T(8,128)S(1)}, f32[224,128]{1,0:T(8,128)S(1)}, u32[]{:S(2)}, u32[]{:S(2)}) %collective-permute-start.9) | collective-permute-done | bytes 114720 | tf_op jit(solution)/shard_map/ppermute | solution.py:596
  46.9 1.2 %collective-permute-done.7.refs_1_ = f32[264,128]{1,0:T(8,128)S(1)} collective-permute-done((f32[264,128]{1,0:T(8,128)S(1)}, f32[264,128]{1,0:T(8,128)S(1)}, u32[]{:S(2)}, u32[]{:S(2)}) %collective-permute-start.7) | collective-permute-done | bytes 135200 | tf_op jit(solution)/shard_map/ppermute | solution.py:626
  48.1 0.1 shard_map.53
  48.2 4.3 %collective-permute-start.10 = (f32[432,128]{1,0:T(8,128)S(1)}, f32[432,128]{1,0:T(8,128)S(1)}, u32[]{:S(2)}, u32[]{:S(2)}) collective-permute-start(f32[432,128]{1,0:T(8,128)S(1)} %get-tuple-element.62), channel_id=1, source_target_pairs={{0,1},{1,2},{2,3},{3,4},{4,5},{5,6},{6,7},{7,8},{8,9},{9,10},{10,1... | collective-permute-start | bytes 663560 | tf_op jit(solution)/shard_map/ppermute | solution.py:595
  52.5 2.9 %collective-permute-done.10.refs_6_ = f32[432,128]{1,0:T(8,128)S(1)} collective-permute-done((f32[432,128]{1,0:T(8,128)S(1)}, f32[432,128]{1,0:T(8,128)S(1)}, u32[]{:S(2)}, u32[]{:S(2)}) %collective-permute-start.10) | collective-permute-done | bytes 221216 | tf_op jit(solution)/shard_map/ppermute | solution.py:595
  55.4 3.7 %collective-permute-done.11.refs_7_ = f32[432,128]{1,0:T(8,128)S(1)} collective-permute-done((f32[432,128]{1,0:T(8,128)S(1)}, f32[432,128]{1,0:T(8,128)S(1)}, u32[]{:S(2)}, u32[]{:S(2)}) %collective-permute-start.11) | collective-permute-done | bytes 221216 | tf_op jit(solution)/shard_map/ppermute | solution.py:596
  59.1 1.4 %shard_map.54 = (f32[24,8,8,128]{3,2,1,0:T(8,128)S(1)}, f32[10,8,8,128]{3,2,1,0:T(8,128)S(1)}, f32[20,8,8,128]{3,2,1,0:T(8,128)S(1)}, f32[8,16,128]{2,1,0:T(8,12...) custom-call(f32[264,128]{1,0:T(8,128)S(1)} %get-tuple-element.56.refs_0_, ...), custom_call_target="tpu_custom_call" | custom-call | tf_op jit(solution)/shard_map/pallas_call | solution.py:577
  60.5 1.9 %collective-permute-start.12 = (f32[4,16,128]{2,1,0:T(8,128)S(1)}, f32[4,16,128]{2,1,0:T(8,128)S(1)}, u32[]{:S(2)}, u32[]{:S(2)}) collective-permute-start(f32[4,16,128]{2,1,0:T(8,128)S(1)} %get-tuple-element.64), channel_id=1, source_target_pairs={{0,32},{16,48},{32,64},{48,80},{64,96},{80,112},{96,128},{112,144}... | collective-permute-start | bytes 98312 | tf_op jit(solution)/shard_map/ppermute | solution.py:590
  62.4 4.3 %collective-permute-start.13 = (f32[4,16,128]{2,1,0:T(8,128)S(1)}, f32[4,16,128]{2,1,0:T(8,128)S(1)}, u32[]{:S(2)}, u32[]{:S(2)}) collective-permute-start(f32[4,16,128]{2,1,0:T(8,128)S(1)} %get-tuple-element.66), channel_id=1, source_target_pairs={{32,0},{48,16},{64,32},{80,48},{96,64},{112,80},{128,96},{144,112}... | collective-permute-start | bytes 98312 | tf_op jit(solution)/shard_map/ppermute | solution.py:590
  66.7 3.4 %collective-permute-done.13.refs_2_ = f32[4,16,128]{2,1,0:T(8,128)S(1)} collective-permute-done((f32[4,16,128]{2,1,0:T(8,128)S(1)}, f32[4,16,128]{2,1,0:T(8,128)S(1)}, u32[]{:S(2)}, u32[]{:S(2)}) %collective-permute-start.13) | collective-permute-done | bytes 32800 | tf_op jit(solution)/shard_map/ppermute | solution.py:590
  70.1 1.2 %collective-permute-start.14 = (f32[16,8,128]{2,1,0:T(8,128)S(1)}, f32[16,8,128]{2,1,0:T(8,128)S(1)}, u32[]{:S(2)}, u32[]{:S(2)}) collective-permute-start(f32[16,8,128]{2,1,0:T(8,128)S(1)} %get-tuple-element.67), channel_id=1, source_target_pairs={{0,1},{1,2},{2,3},{3,4},{4,5},{5,6},{6,7},{7,8},{8,9},{9,10},{10,1... | collective-permute-start | bytes 196616 | tf_op jit(solution)/shard_map/ppermute | solution.py:595
  71.3 1.3 %collective-permute-done.14.refs_3_ = f32[16,8,128]{2,1,0:T(8,128)S(1)} collective-permute-done((f32[16,8,128]{2,1,0:T(8,128)S(1)}, f32[16,8,128]{2,1,0:T(8,128)S(1)}, u32[]{:S(2)}, u32[]{:S(2)}) %collective-permute-start.14) | collective-permute-done | bytes 65568 | tf_op jit(solution)/shard_map/ppermute | solution.py:595
  72.6 3.6 %collective-permute-done.15.refs_4_ = f32[16,8,128]{2,1,0:T(8,128)S(1)} collective-permute-done((f32[16,8,128]{2,1,0:T(8,128)S(1)}, f32[16,8,128]{2,1,0:T(8,128)S(1)}, u32[]{:S(2)}, u32[]{:S(2)}) %collective-permute-start.15) | collective-permute-done | bytes 65568 | tf_op jit(solution)/shard_map/ppermute | solution.py:596
  76.2 4.1 %shard_map.56 = (f32[8,16,512]{2,1,0:T(8,128)}, f32[8,16,512]{2,1,0:T(8,128)}) custom-call(f32[4,16,128]{2,1,0:T(8,128)S(1)} %collective-permute-done.12.refs_0_, f32[8,16,128]{2,1,0:T(8,128)S(1)} %get-tuple-element.65.refs_1_, f32[4,16,128]{2,1,0:T(8,128)S(1)} %collective-permute-done.13.refs_2_, f32[16,8,128]{2,1,0:T(8,128)S(1)} %collective-permute-done.14.refs_3_, ...), custom_call_target="tpu_custom_call" | custom-call | tf_op jit(solution)/shard_map/pallas_call | solution.py:577
  (7 shorter events, 0.0 us)
Async XLA Ops:
  2.2 16.2 %collective-permute-start.1 = (f32[52,16,128]{2,1,0:T(8,128)S(1)}, f32[52,16,128]{2,1,0:T(8,128)S(1)}, u32[]{:S(2)}, u32[]{:S(2)}) collective-permute-start(f32[52,16,128]{2,1,0:T(8,128)S(1)} %get-tuple-element.40), channel_id=1, source_target_pairs={{16,0},{32,16},{48,32},{64,48},{80,64},{96,80},{112,96},{128,112},... | collective-permute-start | bytes 1277960 | tf_op jit(solution)/shard_map/ppermute | solution.py:590
  5.2 13.2 %collective-permute-start = (f32[52,16,128]{2,1,0:T(8,128)S(1)}, f32[52,16,128]{2,1,0:T(8,128)S(1)}, u32[]{:S(2)}, u32[]{:S(2)}) collective-permute-start(f32[52,16,128]{2,1,0:T(8,128)S(1)} %get-tuple-element.39.refs_1_), channel_id=1, source_target_pairs={{0,16},{16,32},{32,48},{48,64},{64,80},{80,96},{96,112},{112,128},... | collective-permute-start | bytes 1277960 | tf_op jit(solution)/shard_map/ppermute | solution.py:590
  7.5 7.2 %collective-permute-start.2 = (f32[416,128]{1,0:T(8,128)S(1)}, f32[416,128]{1,0:T(8,128)S(1)}, u32[]{:S(2)}, u32[]{:S(2)}) collective-permute-start(f32[416,128]{1,0:T(8,128)S(1)} %get-tuple-element.41), channel_id=1, source_target_pairs={{0,1},{1,2},{2,3},{3,4},{4,5},{5,6},{6,7},{7,8},{8,9},{9,10},{10,1... | collective-permute-start | bytes 638984 | tf_op jit(solution)/shard_map/ppermute | solution.py:595
  12.0 6.5 %collective-permute-start.3 = (f32[416,128]{1,0:T(8,128)S(1)}, f32[416,128]{1,0:T(8,128)S(1)}, u32[]{:S(2)}, u32[]{:S(2)}) collective-permute-start(f32[416,128]{1,0:T(8,128)S(1)} %get-tuple-element.42), channel_id=1, source_target_pairs={{0,15},{1,0},{2,1},{3,2},{4,3},{5,4},{6,5},{7,6},{8,7},{9,8},{10,9... | collective-permute-start | bytes 638984 | tf_op jit(solution)/shard_map/ppermute | solution.py:596
  18.5 7.7 %collective-permute-start.4 = (f32[560,128]{1,0:T(8,128)S(1)}, f32[560,128]{1,0:T(8,128)S(1)}, u32[]{:S(2)}, u32[]{:S(2)}) collective-permute-start(f32[560,128]{1,0:T(8,128)S(1)} %get-tuple-element.48), channel_id=1, source_target_pairs={{0,1},{1,2},{2,3},{3,4},{4,5},{5,6},{6,7},{7,8},{8,9},{9,10},{10,1... | collective-permute-start | bytes 860168 | tf_op jit(solution)/shard_map/ppermute | solution.py:595
  22.6 7.3 %collective-permute-start.5 = (f32[560,128]{1,0:T(8,128)S(1)}, f32[560,128]{1,0:T(8,128)S(1)}, u32[]{:S(2)}, u32[]{:S(2)}) collective-permute-start(f32[560,128]{1,0:T(8,128)S(1)} %get-tuple-element.49), channel_id=1, source_target_pairs={{0,15},{1,0},{2,1},{3,2},{4,3},{5,4},{6,5},{7,6},{8,7},{9,8},{10,9... | collective-permute-start | bytes 860168 | tf_op jit(solution)/shard_map/ppermute | solution.py:596
  32.6 14.3 %collective-permute-start.6 = (f32[264,128]{1,0:T(8,128)S(1)}, f32[264,128]{1,0:T(8,128)S(1)}, u32[]{:S(2)}, u32[]{:S(2)}) collective-permute-start(f32[264,128]{1,0:T(8,128)S(1)} %get-tuple-element.50), channel_id=1, source_target_pairs={{0,32},{16,48},{32,64},{48,16},{64,96},{80,112},{96,128},{112,80},... | collective-permute-start | bytes 405512 | tf_op jit(solution)/shard_map/ppermute | solution.py:626
  39.2 8.9 %collective-permute-start.7 = (f32[264,128]{1,0:T(8,128)S(1)}, f32[264,128]{1,0:T(8,128)S(1)}, u32[]{:S(2)}, u32[]{:S(2)}) collective-permute-start(f32[264,128]{1,0:T(8,128)S(1)} %get-tuple-element.51), channel_id=1, source_target_pairs={{32,0},{48,80},{64,32},{80,48},{96,64},{112,144},{128,96},{144,112... | collective-permute-start | bytes 405512 | tf_op jit(solution)/shard_map/ppermute | solution.py:626
  41.2 2.1 %collective-permute-start.8 = (f32[224,128]{1,0:T(8,128)S(1)}, f32[224,128]{1,0:T(8,128)S(1)}, u32[]{:S(2)}, u32[]{:S(2)}) collective-permute-start(f32[224,128]{1,0:T(8,128)S(1)} %get-tuple-element.52), channel_id=1, source_target_pairs={{0,1},{1,2},{2,3},{3,4},{4,5},{5,6},{6,7},{7,8},{8,9},{9,10},{10,1... | collective-permute-start | bytes 344072 | tf_op jit(solution)/shard_map/ppermute | solution.py:595
  41.5 5.4 %collective-permute-start.9 = (f32[224,128]{1,0:T(8,128)S(1)}, f32[224,128]{1,0:T(8,128)S(1)}, u32[]{:S(2)}, u32[]{:S(2)}) collective-permute-start(f32[224,128]{1,0:T(8,128)S(1)} %get-tuple-element.53), channel_id=1, source_target_pairs={{0,15},{1,0},{2,1},{3,2},{4,3},{5,4},{6,5},{7,6},{8,7},{9,8},{10,9... | collective-permute-start | bytes 344072 | tf_op jit(solution)/shard_map/ppermute | solution.py:596
  48.2 7.2 %collective-permute-start.10 = (f32[432,128]{1,0:T(8,128)S(1)}, f32[432,128]{1,0:T(8,128)S(1)}, u32[]{:S(2)}, u32[]{:S(2)}) collective-permute-start(f32[432,128]{1,0:T(8,128)S(1)} %get-tuple-element.62), channel_id=1, source_target_pairs={{0,1},{1,2},{2,3},{3,4},{4,5},{5,6},{6,7},{7,8},{8,9},{9,10},{10,1... | collective-permute-start | bytes 663560 | tf_op jit(solution)/shard_map/ppermute | solution.py:595
  52.5 6.6 %collective-permute-start.11 = (f32[432,128]{1,0:T(8,128)S(1)}, f32[432,128]{1,0:T(8,128)S(1)}, u32[]{:S(2)}, u32[]{:S(2)}) collective-permute-start(f32[432,128]{1,0:T(8,128)S(1)} %get-tuple-element.63), channel_id=1, source_target_pairs={{0,15},{1,0},{2,1},{3,2},{4,3},{5,4},{6,5},{7,6},{8,7},{9,8},{10,9... | collective-permute-start | bytes 663560 | tf_op jit(solution)/shard_map/ppermute | solution.py:596
  60.5 6.2 %collective-permute-start.12 = (f32[4,16,128]{2,1,0:T(8,128)S(1)}, f32[4,16,128]{2,1,0:T(8,128)S(1)}, u32[]{:S(2)}, u32[]{:S(2)}) collective-permute-start(f32[4,16,128]{2,1,0:T(8,128)S(1)} %get-tuple-element.64), channel_id=1, source_target_pairs={{0,32},{16,48},{32,64},{48,80},{64,96},{80,112},{96,128},{112,144}... | collective-permute-start | bytes 98312 | tf_op jit(solution)/shard_map/ppermute | solution.py:590
  62.4 7.7 %collective-permute-start.13 = (f32[4,16,128]{2,1,0:T(8,128)S(1)}, f32[4,16,128]{2,1,0:T(8,128)S(1)}, u32[]{:S(2)}, u32[]{:S(2)}) collective-permute-start(f32[4,16,128]{2,1,0:T(8,128)S(1)} %get-tuple-element.66), channel_id=1, source_target_pairs={{32,0},{48,16},{64,32},{80,48},{96,64},{112,80},{128,96},{144,112}... | collective-permute-start | bytes 98312 | tf_op jit(solution)/shard_map/ppermute | solution.py:590
  70.1 2.5 %collective-permute-start.14 = (f32[16,8,128]{2,1,0:T(8,128)S(1)}, f32[16,8,128]{2,1,0:T(8,128)S(1)}, u32[]{:S(2)}, u32[]{:S(2)}) collective-permute-start(f32[16,8,128]{2,1,0:T(8,128)S(1)} %get-tuple-element.67), channel_id=1, source_target_pairs={{0,1},{1,2},{2,3},{3,4},{4,5},{5,6},{6,7},{7,8},{8,9},{9,10},{10,1... | collective-permute-start | bytes 196616 | tf_op jit(solution)/shard_map/ppermute | solution.py:595
  71.3 4.9 %collective-permute-start.15 = (f32[16,8,128]{2,1,0:T(8,128)S(1)}, f32[16,8,128]{2,1,0:T(8,128)S(1)}, u32[]{:S(2)}, u32[]{:S(2)}) collective-permute-start(f32[16,8,128]{2,1,0:T(8,128)S(1)} %get-tuple-element.68), channel_id=1, source_target_pairs={{0,15},{1,0},{2,1},{3,2},{4,3},{5,4},{6,5},{7,6},{8,7},{9,8},{10,9... | collective-permute-start | bytes 196616 | tf_op jit(solution)/shard_map/ppermute | solution.py:596
